TPU v7x, 32 devices: a whole 2x2x4 slice. The times are simulated.
32 devices in a mesh: seq: 8 (over z, x), tp: 4 (over y, core).
Axes of the slice: x: 2, y: 2, z: 4, core: 2. Of those that a mesh axis runs over, the one named last changes fastest.
Arguments:
- values: bfloat16 [2048, 4096], P('seq', 'tp'), may hold values from -6 to 6
- gate: bfloat16 [2048, 4096], P('seq', 'tp'), may hold values from -6 to 6
- residues: float32 [16, 4096], P(None, 'tp'), may hold values from -1.5 to 1.5
- rates: float32 [16, 4096], P(None, 'tp'), may hold values from 0 to 1, as said below
- skip: float32 [4096], P('tp'), may hold values from -4 to 4
- out_weight: bfloat16 [4096, 4096], P('tp'), may hold values from -0.09375 to 0.09375
Outputs:
- output: bfloat16 [2048, 4096], P('seq', 'tp')
Inputs may be any that keep to these rules, and one draw needn't show every extreme that they name: rates are positive and at most 1; the smallest are near 0.25 / 2048.
All inputs are finite; a program needn't handle non-finite values.
Results may differ from a plain program's by a relative error of at most 0.013.
Values may be sent and summed in bfloat16 or wider, within the bound.
No kernel may reach another device: no remote copies, remote signals or barrier semaphores. Data moves between devices by JAX's collectives and lax.ppermute only.
A program may use at most 128 MiB of HBM per device.

v0:
```python
from functools import partial
import math

import jax
import jax.numpy as jnp
from jax import lax
from jax.sharding import PartitionSpec as P

highest = lax.Precision.HIGHEST


def dft_table(rows, cols, count, sign):
    product = (
        jnp.arange(rows, dtype=jnp.int32)[:, None]
        * jnp.arange(cols, dtype=jnp.int32)[None, :]
        % count
    )
    angle = product.astype(jnp.float32) * (2.0 * math.pi / count)
    return (jnp.cos(angle), sign * jnp.sin(angle))


def complex_apply(form, table_re, table_im, data_re, data_im):
    contract = partial(jnp.einsum, form, precision=highest)
    return (
        contract(table_re, data_re) - contract(table_im, data_im),
        contract(table_re, data_im) + contract(table_im, data_re),
    )


def rotate(data_re, data_im, turn_re, turn_im):
    return (data_re * turn_re - data_im * turn_im, data_re * turn_im + data_im * turn_re)


def radix_sizes(count):
    first = 1
    for cand in range(1, count + 1):
        if count % cand == 0 and cand * cand <= count:
            first = cand
    return (first, count // first)


def local_forward(data_re, data_im):
    pairs, length, chan = data_re.shape
    first, second = radix_sizes(length)
    data_re = data_re.reshape(pairs, first, second, chan)
    data_im = data_im.reshape(pairs, first, second, chan)
    table_re, table_im = dft_table(first, first, first, -1.0)
    data_re, data_im = complex_apply("ka,janc->jknc", table_re, table_im, data_re, data_im)
    turn_re, turn_im = dft_table(first, second, length, -1.0)
    data_re, data_im = rotate(
        data_re, data_im, turn_re[None, :, :, None], turn_im[None, :, :, None]
    )
    table_re, table_im = dft_table(second, second, second, -1.0)
    return complex_apply("kb,jabc->jakc", table_re, table_im, data_re, data_im)


def local_inverse(data_re, data_im):
    pairs, first, second, chan = data_re.shape
    length = first * second
    table_re, table_im = dft_table(second, second, second, 1.0)
    data_re, data_im = complex_apply("kb,jabc->jakc", table_re, table_im, data_re, data_im)
    turn_re, turn_im = dft_table(first, second, length, 1.0)
    data_re, data_im = rotate(
        data_re, data_im, turn_re[None, :, :, None], turn_im[None, :, :, None]
    )
    table_re, table_im = dft_table(first, first, first, 1.0)
    data_re, data_im = complex_apply("ka,janc->jknc", table_re, table_im, data_re, data_im)
    return (data_re.reshape(pairs, length, chan), data_im.reshape(pairs, length, chan))


def forward_head(moved, index, total):
    shards, within, chan = moved.shape
    table_re, table_im = dft_table(2 * shards, shards, 2 * shards, -1.0)
    head_re = jnp.einsum("kp,pqc->kqc", table_re, moved, precision=highest)
    head_im = jnp.einsum("kp,pqc->kqc", table_im, moved, precision=highest)
    offsets = index * within + jnp.arange(within, dtype=jnp.int32)
    product = jnp.arange(2 * shards, dtype=jnp.int32)[:, None] * offsets[None, :] % total
    angle = product.astype(jnp.float32) * (2.0 * math.pi / total)
    return rotate(head_re, head_im, jnp.cos(angle)[:, :, None], -jnp.sin(angle)[:, :, None])


def modal_filter(residues, rates, positions):
    result = jnp.zeros(positions.shape[:-1] + (residues.shape[1],), jnp.float32)
    for mode in range(residues.shape[0]):
        result = result + residues[mode] * jnp.sqrt(2.0 * rates[mode]) * jnp.exp(
            -rates[mode] * positions
        )
    return result


def body(values, gate, residues, rates, skip, out_weight):
    shards = lax.axis_size("seq")
    index = lax.axis_index("seq")
    tok, chan = values.shape
    total = 2 * tok * shards
    moved = lax.all_to_all(
        values.reshape(1, tok, chan), "seq", split_axis=1, concat_axis=0, tiled=True
    )
    head_re, head_im = forward_head(moved.astype(jnp.float32), index, total)
    spread_re, spread_im = (
        lax.all_to_all(head_re, "seq", split_axis=0, concat_axis=1, tiled=True),
        lax.all_to_all(head_im, "seq", split_axis=0, concat_axis=1, tiled=True),
    )
    value_re, value_im = local_forward(spread_re, spread_im)
    positions = (index * tok + jnp.arange(tok, dtype=jnp.int32)).astype(jnp.float32)[:, None]
    own_filter = modal_filter(residues, rates, positions)
    moved_filter = lax.all_to_all(
        own_filter.reshape(1, tok, chan), "seq", split_axis=1, concat_axis=0, tiled=True
    )
    fhead_re, fhead_im = forward_head(moved_filter, index, total)
    fspread_re, fspread_im = (
        lax.all_to_all(fhead_re, "seq", split_axis=0, concat_axis=1, tiled=True),
        lax.all_to_all(fhead_im, "seq", split_axis=0, concat_axis=1, tiled=True),
    )
    filt_re, filt_im = local_forward(fspread_re, fspread_im)
    prod_re, prod_im = rotate(value_re, value_im, filt_re, filt_im)
    back_re, back_im = local_inverse(prod_re, prod_im)
    freqs = 2 * index + jnp.arange(2, dtype=jnp.int32)
    product = freqs[:, None] * jnp.arange(tok, dtype=jnp.int32)[None, :] % total
    angle = product.astype(jnp.float32) * (2.0 * math.pi / total)
    back_re, back_im = rotate(
        back_re, back_im, jnp.cos(angle)[:, :, None], jnp.sin(angle)[:, :, None]
    )
    gathered_re, gathered_im = (
        lax.all_to_all(back_re, "seq", split_axis=1, concat_axis=0, tiled=True),
        lax.all_to_all(back_im, "seq", split_axis=1, concat_axis=0, tiled=True),
    )
    table_re, table_im = dft_table(shards, 2 * shards, 2 * shards, 1.0)
    conv_rows = (
        jnp.einsum("pk,kqc->pqc", table_re, gathered_re, precision=highest)
        - jnp.einsum("pk,kqc->pqc", table_im, gathered_im, precision=highest)
    ) * (1.0 / total)
    conv = lax.all_to_all(conv_rows, "seq", split_axis=0, concat_axis=1, tiled=True).reshape(
        tok, chan
    )
    mixed = conv + skip * values.astype(jnp.float32)
    gated = (gate.astype(jnp.float32) * mixed).astype(jnp.bfloat16)
    share = lax.psum_scatter(
        lax.dot_general(
            out_weight, gated, (((0,), (1,)), ((), ())), preferred_element_type=jnp.float32
        ).astype(jnp.bfloat16),
        "tp",
        scatter_dimension=0,
        tiled=True,
    ).astype(jnp.float32)
    return share.T.astype(jnp.bfloat16)


def solution(mesh):
    placed = (P("seq", "tp"), P("seq", "tp"), P(None, "tp"), P(None, "tp"), P("tp"), P("tp", None))
    return jax.shard_map(
        body, mesh=mesh, in_specs=placed, out_specs=P("seq", "tp"), check_vma=False
    )
```

profile of v0, /device:TPU:0, one launch (start us, length us, event | category | flops | bytes accessed | tf_op | source)
XLA Modules:
  0.0 541.1 jit_solution(8977915658152382723)
XLA Ops:
  13.8 7.3 %all-to-all-start = ((bf16[8,2,16384]{2,1,0:T(2,128)(2,1)}), bf16[8,2,16384]{2,1,0:T(2,128)(2,1)S(1)}, u32[]{:S(2)}, u32[]{:S(2)}) async-start(bf16[8,2,16384]{2,1,0:T(2,128)(2,1)} %reshape.1484), calls=%async_computation | async-start | bytes 1048576 | tf_op jit(solution)/shard_map/all_to_all | solution.py:96
  26.2 9.3 %all-to-all-done = bf16[8,2,16384]{2,1,0:T(2,128)(2,1)S(1)} async-done(((bf16[8,2,16384]{2,1,0:T(2,128)(2,1)}), bf16[8,2,16384]{2,1,0:T(2,128)(2,1)S(1)}, u32[]{:S(2)}, u32[]{:S(2)}) %all-to-all-start) | async-done | bytes 524320 | tf_op jit(solution)/shard_map/all_to_all | solution.py:96
  43.8 21.4 %all-to-all-done.3 = f32[1,256,1024]{2,0,1:T(1,128)S(1)} async-done(((f32[1,256,1024]{2,0,1:T(1,128)}), f32[1,256,1024]{2,0,1:T(1,128)S(1)}, u32[]{:S(2)}, u32[]{:S(2)}) %all-to-all-start.3) | async-done | bytes 1048608 | tf_op jit(solution)/shard_map/all_to_all | solution.py:107
  67.7 4.9 multiply_subtract_fusion.1
  75.2 4.5 all-to-all-start.2
  82.3 45.2 %all-to-all-done.2 = f32[16,32,1024]{2,1,0:T(8,128)} async-done(((f32[16,32,1024]{2,1,0:T(8,128)}), f32[16,32,1024]{2,1,0:T(8,128)}, u32[]{:S(2)}, u32[]{:S(2)}) %all-to-all-start.2) | async-done | bytes 2097184 | tf_op jit(solution)/shard_map/all_to_all | solution.py:102
  127.5 4.4 all-to-all-start.1
  134.5 45.2 %all-to-all-done.1 = f32[16,32,1024]{2,1,0:T(8,128)} async-done(((f32[16,32,1024]{2,1,0:T(8,128)}), f32[16,32,1024]{2,1,0:T(8,128)}, u32[]{:S(2)}, u32[]{:S(2)}) %all-to-all-start.1) | async-done | bytes 2097184 | tf_op jit(solution)/shard_map/all_to_all | solution.py:101
  179.7 4.4 all-to-all-start.5
  186.6 45.2 %all-to-all-done.5 = f32[16,32,1024]{2,1,0:T(8,128)} async-done(((f32[16,32,1024]{2,1,0:T(8,128)}), f32[16,32,1024]{2,1,0:T(8,128)}, u32[]{:S(2)}, u32[]{:S(2)}) %all-to-all-start.5) | async-done | bytes 2097184 | tf_op jit(solution)/shard_map/all_to_all | solution.py:113
  231.8 4.8 all-to-all-start.4
  252.0 4.8 fusion.31
  256.9 4.7 fusion.55
  261.6 4.7 fusion.58
  266.3 17.7 %all-to-all-done.4 = f32[16,32,1024]{2,1,0:T(8,128)} async-done(((f32[16,32,1024]{2,1,0:T(8,128)}), f32[16,32,1024]{2,1,0:T(8,128)}, u32[]{:S(2)}, u32[]{:S(2)}) %all-to-all-start.4) | async-done | bytes 2097184 | tf_op jit(solution)/shard_map/all_to_all | solution.py:112
  289.3 5.0 fusion.11
  317.8 4.3 multiply_subtract_fusion
  356.4 4.6 copy.180
  361.0 43.9 %all-to-all-done.6 = f32[2,256,1024]{2,0,1:T(2,128)S(1)} async-done(((f32[2,256,1024]{2,0,1:T(2,128)}), f32[2,256,1024]{2,0,1:T(2,128)S(1)}, u32[]{:S(2)}, u32[]{:S(2)}) %all-to-all-start.6) | async-done | bytes 2097184 | tf_op jit(solution)/shard_map/all_to_all | solution.py:125
  404.9 4.3 all-to-all-start.7
  416.9 40.1 %all-to-all-done.7 = f32[2,256,1024]{2,0,1:T(2,128)} async-done(((f32[2,256,1024]{2,0,1:T(2,128)}), f32[2,256,1024]{2,0,1:T(2,128)}, u32[]{:S(2)}, u32[]{:S(2)}) %all-to-all-start.7) | async-done | bytes 2097184 | tf_op jit(solution)/shard_map/all_to_all | solution.py:126
  466.8 29.3 %all_to_all.129 = f32[8,32,1024]{2,1,0:T(8,128)S(1)} all-to-all(f32[8,32,1024]{2,1,0:T(8,128)S(1)} %copy.183), channel_id=1, replica_groups=mesh['seq'=8,'tp'=4] {'seq'}, dimensions={0} | all-to-all | bytes 2097152 | tf_op jit(solution)/shard_map/all_to_all | solution.py:133
  496.4 7.1 %fusion = bf16[4096,256]{0,1:T(8,128)(2,1)} fusion(bf16[256,1024]{1,0:T(8,128)(2,1)S(1)} %fusion.91, bf16[1024,4096]{1,0:T(8,128)(2,1)} %param.11), kind=kOutput, calls=%fused_computation.1 | convolution fusion | flops 2148532224 | bytes 11010048 | tf_op jit(solution)/shard_map/dot_general | solution.py:139
  503.5 30.7 %reduce-scatter.2.cloned.1.call-done = bf16[1024,256]{0,1:T(8,128)(2,1)} async-done(((bf16[4096,256]{0,1:T(8,128)(2,1)}), bf16[1024,256]{0,1:T(8,128)(2,1)}) %reduce-scatter.2.cloned.1.call-update) | async-done | bytes 524304 | tf_op jit(solution)/shard_map/reduce_scatter | solution.py:138
  (94 shorter events, 129.4 us)
Async XLA Ops:
  8.4 12.7 %copy-start.9 = (f32[16,1024]{1,0:T(8,128)S(1)}, f32[16,1024]{1,0:T(8,128)}, u32[]{:S(2)}) copy-start(f32[16,1024]{1,0:T(8,128)} %param.9) | copy-start | bytes 196612
  8.4 12.7 %copy-start.10 = (f32[16,1024]{1,0:T(8,128)S(1)}, f32[16,1024]{1,0:T(8,128)}, u32[]{:S(2)}) copy-start(f32[16,1024]{1,0:T(8,128)} %param.8) | copy-start | bytes 196612
  13.8 21.7 %all-to-all-start = ((bf16[8,2,16384]{2,1,0:T(2,128)(2,1)}), bf16[8,2,16384]{2,1,0:T(2,128)(2,1)S(1)}, u32[]{:S(2)}, u32[]{:S(2)}) async-start(bf16[8,2,16384]{2,1,0:T(2,128)(2,1)} %reshape.1484), calls=%async_computation | async-start | bytes 1048576 | tf_op jit(solution)/shard_map/all_to_all | solution.py:96
  35.5 29.7 %all-to-all-start.3 = ((f32[1,256,1024]{2,0,1:T(1,128)}), f32[1,256,1024]{2,0,1:T(1,128)S(1)}, u32[]{:S(2)}, u32[]{:S(2)}) async-start(f32[1,256,1024]{2,0,1:T(1,128)} %copy.154), calls=%async_computation.3 | async-start | bytes 2097152 | tf_op jit(solution)/shard_map/all_to_all | solution.py:107
  65.5 2.2 copy-start
  75.2 4.5 copy-start.3
  75.2 52.3 %all-to-all-start.2 = ((f32[16,32,1024]{2,1,0:T(8,128)}), f32[16,32,1024]{2,1,0:T(8,128)}, u32[]{:S(2)}, u32[]{:S(2)}) async-start(f32[16,32,1024]{2,1,0:T(8,128)} %copy.145), calls=%async_computation.2 | async-start | bytes 4194304 | tf_op jit(solution)/shard_map/all_to_all | solution.py:102
  82.2 49.6 %copy-start.2 = (f32[16,32,1024]{2,0,1:T(8,128)S(1)}, f32[16,32,1024]{2,0,1:T(8,128)}, u32[]{:S(2)}) copy-start(f32[16,32,1024]{2,0,1:T(8,128)} %get-tuple-element.8) | copy-start | bytes 6291460
  127.5 52.2 %all-to-all-start.1 = ((f32[16,32,1024]{2,1,0:T(8,128)}), f32[16,32,1024]{2,1,0:T(8,128)}, u32[]{:S(2)}, u32[]{:S(2)}) async-start(f32[16,32,1024]{2,1,0:T(8,128)} %copy.142), calls=%async_computation.1 | async-start | bytes 4194304 | tf_op jit(solution)/shard_map/all_to_all | solution.py:101
  134.5 49.6 %copy-start.1 = (f32[16,32,1024]{2,0,1:T(8,128)S(1)}, f32[16,32,1024]{2,0,1:T(8,128)}, u32[]{:S(2)}) copy-start(f32[16,32,1024]{2,0,1:T(8,128)} %get-tuple-element.7) | copy-start | bytes 6291460
  179.7 52.2 %all-to-all-start.5 = ((f32[16,32,1024]{2,1,0:T(8,128)}), f32[16,32,1024]{2,1,0:T(8,128)}, u32[]{:S(2)}, u32[]{:S(2)}) async-start(f32[16,32,1024]{2,1,0:T(8,128)} %copy.160), calls=%async_computation.5 | async-start | bytes 4194304 | tf_op jit(solution)/shard_map/all_to_all | solution.py:113
  231.8 52.2 %all-to-all-start.4 = ((f32[16,32,1024]{2,1,0:T(8,128)}), f32[16,32,1024]{2,1,0:T(8,128)}, u32[]{:S(2)}, u32[]{:S(2)}) async-start(f32[16,32,1024]{2,1,0:T(8,128)} %copy.157), calls=%async_computation.4 | async-start | bytes 4194304 | tf_op jit(solution)/shard_map/all_to_all | solution.py:112
  285.8 3.4 copy-start.4
  285.8 3.4 copy-start.5
  285.8 3.4 copy-start.6
  352.8 52.1 %all-to-all-start.6 = ((f32[2,256,1024]{2,0,1:T(2,128)}), f32[2,256,1024]{2,0,1:T(2,128)S(1)}, u32[]{:S(2)}, u32[]{:S(2)}) async-start(f32[2,256,1024]{2,0,1:T(2,128)} %copy.177), calls=%async_computation.6 | async-start | bytes 4194304 | tf_op jit(solution)/shard_map/all_to_all | solution.py:125
  404.9 52.2 %all-to-all-start.7 = ((f32[2,256,1024]{2,0,1:T(2,128)}), f32[2,256,1024]{2,0,1:T(2,128)}, u32[]{:S(2)}, u32[]{:S(2)}) async-start(f32[2,256,1024]{2,0,1:T(2,128)} %copy.180), calls=%async_computation.7 | async-start | bytes 4194304 | tf_op jit(solution)/shard_map/all_to_all | solution.py:126
  409.2 124.9 %reduce-scatter.2.cloned.1.call-start = ((), (), s32[]{:S(2)}) async-start(), calls=%async_computation.10 | async-start | bytes 2621440 | tf_op jit(solution)/shard_map/reduce_scatter | solution.py:138
  466.1 30.0 %copy-start.7 = (bf16[256,1024]{1,0:T(8,128)(2,1)S(1)}, bf16[256,1024]{1,0:T(8,128)(2,1)}, u32[]{:S(2)}) copy-start(bf16[256,1024]{1,0:T(8,128)(2,1)} %param.6) | copy-start | bytes 1572868
  466.1 30.0 %copy-start.8 = (bf16[256,1024]{1,0:T(8,128)(2,1)S(1)}, bf16[256,1024]{1,0:T(8,128)(2,1)}, u32[]{:S(2)}) copy-start(bf16[256,1024]{1,0:T(8,128)(2,1)} %param.7) | copy-start | bytes 1572868
  466.1 30.0 %copy-start.11 = (f32[1024]{0:T(1024)S(1)}, f32[1024]{0:T(1024)}, u32[]{:S(2)}) copy-start(f32[1024]{0:T(1024)} %param.10) | copy-start | bytes 12292
Sparse Core Ops, SparseCore 0:
  503.6 30.4 reduce-scatter.1
where the time goes:
time: 549 us; the launch traced here: 541 us
  waiting for transfers between devices  299 us (54%)
  matrix products  105 us (19%)
  local copies, waits for them, and re-layouts  47.3 us (9%)
  starting transfers between devices  37.2 us (7%)
  blocking collectives  29.3 us (5%)
  between operations  14.1 us (3%)
  other arithmetic  9.35 us (2%)
    all_to_all x1, waiting for transfers between devices, body(): lax.all_to_all(head_im, 'seq', split_axis=0, concat_axis=1, tiled=True)  45.2 us
    all_to_all x1, waiting for transfers between devices, body(): lax.all_to_all(fhead_im, 'seq', split_axis=0, concat_axis=1, tiled=True)  45.2 us
    all_to_all x1, waiting for transfers between devices, body(): lax.all_to_all(head_re, 'seq', split_axis=0, concat_axis=1, tiled=True)  45.2 us
    all_to_all x1, waiting for transfers between devices, body(): lax.all_to_all(back_re, 'seq', split_axis=1, concat_axis=0, tiled=True)  43.9 us
    all_to_all x1, waiting for transfers between devices, body(): lax.all_to_all(back_im, 'seq', split_axis=1, concat_axis=0, tiled=True)  40.1 us
    reduce_scatter x1, waiting for transfers between devices, body(): lax.psum_scatter(lax.dot_general(out_weight, gated, (((0,), (1,)), ((), (...  30.7 us
    all_to_all x1, blocking collectives, body(): lax.all_to_all(conv_rows, 'seq', split_axis=0, concat_axis=1, tiled=True)  29.3 us
    dot_general x6, matrix products, complex_apply(): contract(table_im, data_re)  23.4 us
  transfers between devices with their start and end apart: 9, of which 9 were waited for; matrix products, arithmetic and copies ran while one was open for 10% of the time, Pallas kernels for 0%

commit v1 on v0

v1 whole, which is shorter than its diff:
```python
from functools import partial

import jax
import jax.numpy as jnp
from jax import lax
from jax.experimental import pallas as pl
from jax.experimental.pallas import tpu as pltpu
from jax.sharding import PartitionSpec as P

SUB, LANE = 8, 128
F32, BF16 = jnp.float32, jnp.bfloat16

VMEM = pl.BlockSpec(memory_space=pltpu.VMEM)
ANY = pl.BlockSpec(memory_space=pl.ANY)
HBM = "hbm"
PARAMS = pltpu.CompilerParams(vmem_limit_bytes=24 * 2**20)


def in_hbm(array):
    return pltpu.with_memory_space_constraint(array, pltpu.HBM)


def in_vmem(array):
    return pltpu.with_memory_space_constraint(array, pltpu.VMEM)


def row_of(block, mode):
    return jnp.broadcast_to(block[mode : mode + 1, :], (SUB, LANE))


def sublane():
    return lax.broadcasted_iota(jnp.int32, (SUB, LANE), 0)


def lanes_at(step):
    return pl.ds(pl.multiple_of(step * LANE, LANE), LANE)


def gains_of(residues, rates):
    return residues * jnp.sqrt(2.0 * rates)


def spread_table(tok, back):
    run = tok // SUB
    row = lax.broadcasted_iota(jnp.int32, (tok, tok), 1 if back else 0)
    col = lax.broadcasted_iota(jnp.int32, (tok, tok), 0 if back else 1)
    return (col == row % SUB * run + row // SUB).astype(F32).astype(BF16)


ROW_CUTS = 4


def column_copies(other, begin, slots, weight_hbm, out_ref, sems):
    rank = lax.axis_index("tp")
    chips = lax.axis_size("tp") // 2
    block = weight_hbm.shape[1] // (2 * chips)
    wide = out_ref.shape[1] // len(slots)
    tall = out_ref.shape[0] // ROW_CUTS
    core = 1 - rank % 2 if other else rank % 2
    copies = []
    for at, slot in enumerate(slots):
        owner = (rank // 2 + slot) % chips * 2 + core
        columns = pl.ds(pl.multiple_of(owner * block + begin, LANE), wide)
        for cut in range(ROW_CUTS):
            rows = pl.ds(cut * tall, tall)
            copies.append(
                pltpu.make_async_copy(
                    weight_hbm.at[rows, columns],
                    out_ref.at[rows, pl.ds(at * wide, wide)],
                    sems.at[at * ROW_CUTS + cut],
                )
            )
            copies[-1].start()
    return copies


def wait_all(copies):
    for copy in copies:
        copy.wait()


def state_kernel(
    values_hbm, rates_hbm, wire_hbm, values_ref, rates_ref, state_ref, sems, out_sems
):
    tok, chan = values_ref.shape
    modes = rates_ref.shape[0]
    shards = wire_hbm.shape[0]
    parts = sems.shape[0] - 1
    width = chan // parts
    first = pltpu.make_async_copy(rates_hbm, rates_ref, sems.at[parts])
    first.start()
    pieces, outs = [], []
    for part in range(parts):
        lanes = pl.ds(part * width, width)
        pieces.append(
            pltpu.make_async_copy(
                values_hbm.at[:, lanes], values_ref.at[:, lanes], sems.at[part]
            )
        )
        pieces[-1].start()
    left = (SUB - 1 - sublane()).astype(F32)
    first.wait()
    for index in range(chan // LANE):
        if index * LANE % width == 0:
            pieces[index * LANE // width].wait()
        lanes = slice(index * LANE, (index + 1) * LANE)
        rates = rates_ref[:, lanes]
        decay = jnp.exp(-float(SUB) * rates)
        decays = [row_of(decay, mode) for mode in range(modes)]
        held = [jnp.zeros((SUB, LANE), F32)] * modes
        for at in range(0, tok, 2 * SUB):
            pair = values_ref[at : at + 2 * SUB, lanes].astype(F32)
            for half in (pair[:SUB], pair[SUB:]):
                held = [decays[mode] * held[mode] + half for mode in range(modes)]
        rows = [
            jnp.sum(held[mode] * jnp.exp(-row_of(rates, mode) * left), axis=0, keepdims=True)
            for mode in range(modes)
        ]
        state_ref[:, lanes] = jnp.concatenate(rows, axis=0).astype(BF16)
        if (index + 1) * LANE % width == 0:
            part = index * LANE // width
            lanes = pl.ds(part * width, width)
            for shard in range(shards):
                outs.append(
                    pltpu.make_async_copy(
                        state_ref.at[:, lanes], wire_hbm.at[shard, :, lanes],
                        out_sems.at[part, shard],
                    )
                )
                outs[-1].start()
    wait_all(outs)


def local_kernel(
    values_hbm, rates_hbm, residues_hbm, skip_hbm, gate_hbm, weight_hbm,
    near_ref, starts_ref, ahead_ref, rates_ref, spread_ref, first_weight,
    values_ref, residues_ref, skip_ref, gate_ref, wide_ref, taps_ref, sems, weight_sems,
):
    tok, chan = values_ref.shape
    modes = rates_ref.shape[0]
    run = tok // SUB
    copies = [
        pltpu.make_async_copy(source, target, sems.at[at])
        for at, (source, target) in enumerate(
            (
                (values_hbm, values_ref),
                (gate_hbm, gate_ref),
                (rates_hbm, rates_ref),
                (residues_hbm, residues_ref),
                (skip_hbm, skip_ref),
            )
        )
    ]
    for copy in copies:
        copy.start()
    slots = range(lax.axis_size("tp") // 2)
    rest = column_copies(1, 0, slots, weight_hbm, first_weight, weight_sems)
    table = spread_table(tok, False)
    wait_all(copies)
    wide_ref[...] = jnp.dot(table, values_ref[...], preferred_element_type=F32)
    spread_ref[...] = jnp.dot(table, gate_ref[...], preferred_element_type=F32).astype(BF16)

    def step(index, carry):
        lanes = lanes_at(index)
        place = sublane()
        rates = rates_ref[:, lanes]
        gains = gains_of(residues_ref[:, lanes], rates)

        ahead = place.astype(F32)
        decay = jnp.exp(-float(SUB) * rates)
        terms = [
            row_of(gains, mode) * jnp.exp(-row_of(rates, mode) * ahead) for mode in range(modes)
        ]
        for at in range(0, run, SUB):
            total = terms[0]
            for mode in range(1, modes):
                total = total + terms[mode]
            if at == 0:
                total = jnp.where(place == 0, total + skip_ref[:, lanes], total)
            terms = [terms[mode] * row_of(decay, mode) for mode in range(modes)]
            taps_ref[at : at + SUB, :] = total

        for at in range(0, run, SUB):
            sums = [jnp.zeros((SUB, LANE), F32)] * SUB
            for early in range(0, at + SUB, SUB):
                for lag in range(at - early - SUB + 1, at - early + SUB):
                    if lag < 0:
                        continue
                    tap = jnp.broadcast_to(taps_ref[lag : lag + 1, :], (SUB, LANE))
                    for source in range(SUB):
                        target = early + source + lag - at
                        if 0 <= target < SUB:
                            rows = pl.ds((early + source) * SUB, SUB)
                            sums[target] = sums[target] + tap * wide_ref[rows, lanes]
            for target in range(SUB):
                near_ref[pl.ds((at + target) * SUB, SUB), lanes] = sums[target]

        decay = jnp.exp(-rates)
        decay_run = jnp.exp(-float(run) * rates)
        decays = [row_of(decay, mode) for mode in range(modes)]
        held = [jnp.zeros((SUB, LANE), F32)] * modes
        for at in range(run):
            value = wide_ref[at * SUB : (at + 1) * SUB, lanes]
            held = [decays[mode] * held[mode] + value for mode in range(modes)]
        for mode in range(modes):
            whole, power = held[mode], row_of(decay_run, mode)
            for shift in (1, 2, 4):
                moved = jnp.where(place >= shift, pltpu.roll(whole, shift, 0), 0.0)
                whole = whole + power * moved
                power = power * power
            before = jnp.where(place >= 1, pltpu.roll(whole, 1, 0), 0.0)
            first = row_of(gains, mode) * decays[mode]
            rows = slice(mode * SUB, (mode + 1) * SUB)
            starts_ref[rows, lanes] = first * before
        ahead_ref[:, lanes] = gains * decay
        return carry

    lax.fori_loop(0, chan // LANE, step, 0)
    wait_all(rest)


def gate_kernel(
    states_ref, near_ref, starts_ref, ahead_ref, rates_ref, spread_ref, weight_ref, weight_hbm,
    gated_ref, sent_ref, kept_weight, later_weight, held_ref, state_ref, decay_ref, sems,
):
    slots = range(lax.axis_size("tp") // 2)
    begin = weight_ref.shape[1] // len(slots)
    rest = column_copies(0, 0, slots, weight_hbm, kept_weight, sems.at[0])
    rest += column_copies(1, begin, slots, weight_hbm, later_weight, sems.at[1])
    tok, chan = spread_ref.shape
    shards, modes = states_ref.shape[:2]
    run = tok // SUB
    place = lax.axis_index("seq")
    rates = rates_ref[...]
    decay_ref[...] = jnp.exp(-rates)
    far = jnp.exp(-float(tok) * rates)
    before = jnp.zeros((modes, chan), F32)
    for shard in range(shards - 1):
        passed = far * before + states_ref[shard].astype(F32)
        before = jnp.where(shard < place, passed, before)
    state_ref[...] = before * ahead_ref[...]
    passed = (sublane() * run).astype(F32)

    def step(index, carry):
        lanes = lanes_at(index)
        decays, terms = [], []
        for mode in range(modes):
            rows, row = slice(mode * SUB, (mode + 1) * SUB), slice(mode, mode + 1)
            decays.append(jnp.broadcast_to(decay_ref[row, lanes], (SUB, LANE)))
            state = jnp.broadcast_to(state_ref[row, lanes], (SUB, LANE))
            rate = jnp.broadcast_to(rates_ref[row, lanes], (SUB, LANE))
            terms.append(starts_ref[rows, lanes] + state * jnp.exp(-rate * passed))
        for at in range(0, run, 2):
            totals = []
            for spot in (at, at + 1):
                total = near_ref[spot * SUB : (spot + 1) * SUB, lanes]
                for mode in range(modes):
                    total = total + terms[mode]
                terms = [terms[mode] * decays[mode] for mode in range(modes)]
                totals.append(total)
            rows = slice(at * SUB, (at + 2) * SUB)
            gate = spread_ref[rows, lanes].astype(F32)
            held_ref[rows, lanes] = (gate * jnp.concatenate(totals, axis=0)).astype(BF16)
        return carry

    lax.fori_loop(0, chan // LANE, step, 0)
    project(spread_table(tok, True), held_ref, gated_ref)
    project(gated_ref, weight_ref, sent_ref)
    wait_all(rest)


def project(left_ref, right_ref, out_ref):
    total = out_ref.shape[1]
    tile = 2 * LANE if total % (2 * LANE) == 0 else LANE
    for first in range(0, total, tile):
        lanes = slice(first, first + tile)
        out_ref[:, lanes] = jnp.dot(
            left_ref[...], right_ref[:, lanes], preferred_element_type=F32
        ).astype(out_ref.dtype)


def product(gated_ref, weight):
    return jnp.dot(gated_ref[...], weight, preferred_element_type=F32)


def middle_kernel(
    gated_ref, kept_weight, sent_weight, weight_hbm, kept_ref, sent_ref, later_ref, sems
):
    chips = lax.axis_size("tp") // 2
    begin = kept_ref.shape[1] // chips
    copies = column_copies(0, begin, range(1, chips), weight_hbm, later_ref, sems)
    project(gated_ref, kept_weight, kept_ref)
    project(gated_ref, sent_weight, sent_ref)
    wait_all(copies)


def join_kernel(kept_ref, moved_ref, *going_refs):
    wide = going_refs[0].shape[1]
    for hop, going_ref in enumerate(going_refs, 1):
        lanes = slice(hop * wide, (hop + 1) * wide)
        going_ref[...] = (kept_ref[:, lanes] + moved_ref[:, lanes].astype(F32)).astype(BF16)


def going_kernel(gated_ref, weight_ref, moved_ref, *going_refs):
    wide = going_refs[0].shape[1]
    for hop, going_ref in enumerate(going_refs, 1):
        lanes = slice((hop - 1) * wide, hop * wide)
        total = product(gated_ref, weight_ref[:, lanes])
        total = total + moved_ref[:, hop * wide : (hop + 1) * wide].astype(F32)
        going_ref[...] = total.astype(BF16)


def own_kernel(gated_ref, weight_hbm, moved_ref, kept_ref, moved_first_ref, *refs):
    others, (first_ref, own_ref, weight_ref, sems) = refs[:-4], refs[-4:]
    narrow, wide = first_ref.shape[1], own_ref.shape[1]
    copies = column_copies(0, narrow, range(1), weight_hbm, weight_ref, sems)
    total = kept_ref[:, :narrow] + moved_first_ref[:, :narrow].astype(F32)
    for other in others:
        total = total + other[...].astype(F32)
    first_ref[...] = total.astype(BF16)
    wait_all(copies)
    own_ref[...] = moved_ref[:, :wide].astype(F32) + product(gated_ref, weight_ref[...])


def final_kernel(first_ref, own_ref, *refs):
    others, (out_hbm, wide_ref, sems) = refs[:-3], refs[-3:]
    tok, narrow = first_ref.shape
    count = sems.shape[0] - 1
    copies = [
        pltpu.make_async_copy(first_ref, out_hbm.at[:, pl.ds(0, narrow)], sems.at[count])
    ]
    copies[0].start()
    for part in range(count):
        rows = pl.ds(part * tok // count, tok // count)
        total = own_ref[rows, :]
        for other in others:
            total = total + other[rows, :].astype(F32)
        wide_ref[rows, :] = total.astype(BF16)
        columns = pl.ds(narrow, wide_ref.shape[1])
        copies.append(
            pltpu.make_async_copy(wide_ref.at[rows], out_hbm.at[rows, columns], sems.at[part])
        )
        copies[-1].start()
    wait_all(copies)


def call(kernel, outs, *operands, scratch=(), macs=0, out_spec=VMEM):
    specs, arrays = [], []
    for operand in operands:
        spec, array = operand if isinstance(operand, tuple) else (VMEM, operand)
        specs.append(ANY if spec is HBM else spec)
        arrays.append(in_hbm(array) if spec is HBM else array)
    return pl.pallas_call(
        kernel,
        out_shape=outs,
        in_specs=specs,
        out_specs=[out_spec] * len(outs),
        scratch_shapes=scratch,
        compiler_params=PARAMS,
        cost_estimate=pl.CostEstimate(flops=2 * macs, bytes_accessed=0, transcendentals=0),
    )(*arrays)


def body(values, gate, residues, rates, skip, out_weight):
    shards, tp = lax.axis_size("seq"), lax.axis_size("tp")
    tok, chan = values.shape
    modes = rates.shape[0]
    chips = tp // 2
    block = out_weight.shape[1] // tp
    here = pltpu.VMEM
    parts = 4 if chan % (4 * LANE) == 0 else 1
    cores = [(rank, rank ^ 1) for rank in range(tp)]
    sources = [(HBM, each) for each in (values, rates, residues, skip.reshape(1, chan), gate)]
    (wire,) = call(
        state_kernel,
        [jax.ShapeDtypeStruct((shards, modes, chan), BF16)],
        *sources[:2],
        scratch=[
            here((tok, chan), BF16),
            here((modes, chan), F32),
            here((modes, chan), BF16),
            pltpu.SemaphoreType.DMA((parts + 1,)),
            pltpu.SemaphoreType.DMA((parts, shards)),
        ],
        out_spec=ANY,
    )
    states = lax.all_to_all(wire, "seq", split_axis=0, concat_axis=0, tiled=True)
    narrow = max(LANE, block // 4)
    wide = block - narrow
    weight = (HBM, out_weight)
    tables = call(
        local_kernel,
        [
            here((tok, chan), F32),
            here((modes * SUB, chan), F32),
            here((modes, chan), F32),
            here((modes, chan), F32),
            here((tok, chan), BF16),
            here((chan, chips * narrow), BF16),
        ],
        *sources, weight,
        scratch=[
            here((tok, chan), BF16),
            here((modes, chan), F32),
            here((1, chan), F32),
            here((tok, chan), BF16),
            here((tok, chan), F32),
            here((tok // SUB, LANE), F32),
            pltpu.SemaphoreType.DMA((len(sources),)),
            pltpu.SemaphoreType.DMA((chips * ROW_CUTS,)),
        ],
    )

    gated, sent, kept_weight, sent_weight = call(
        gate_kernel,
        [
            here((tok, chan), BF16),
            here((tok, chips * narrow), BF16),
            here((chan, chips * narrow), BF16),
            here((chan, chips * wide), BF16),
        ],
        states, *tables, weight,
        scratch=[
            here((tok, chan), BF16),
            here((modes, chan), F32),
            here((modes, chan), F32),
            pltpu.SemaphoreType.DMA((2, chips * ROW_CUTS)),
        ],
    )
    moved_first = lax.ppermute(sent, "tp", cores)
    kept, sent, later = call(
        middle_kernel,
        [
            here((tok, chips * narrow), F32),
            here((tok, chips * wide), BF16),
            here((chan, (chips - 1) * wide), BF16),
        ],
        gated, kept_weight, sent_weight, weight,
        scratch=[pltpu.SemaphoreType.DMA(((chips - 1) * ROW_CUTS,))],
    )
    moved = lax.ppermute(sent, "tp", cores)

    def to_chips(going):
        return [
            lax.ppermute(each, "tp", [(rank, (rank + 2 * hop) % tp) for rank in range(tp)])
            for hop, each in enumerate(going, 1)
        ]

    first = to_chips(
        call(
            join_kernel, [here((tok, narrow), BF16)] * (chips - 1), kept, moved_first,
            macs=16 * tok * chan * block,
        )
    )
    second = to_chips(
        call(going_kernel, [here((tok, wide), BF16)] * (chips - 1), gated, later, moved)
    )
    done, own = call(
        own_kernel, [here((tok, narrow), BF16), here((tok, wide), F32)],
        gated, weight, moved, kept, moved_first, *first,
        macs=16 * tok * chan * block,
        scratch=[here((chan, wide), BF16), pltpu.SemaphoreType.DMA((ROW_CUTS,))],
    )
    (out,) = call(
        final_kernel, [jax.ShapeDtypeStruct((tok, block), BF16)], done, own, *second,
        scratch=[here((tok, wide), BF16), pltpu.SemaphoreType.DMA((5,))],
        out_spec=ANY,
    )
    return out


def solution(mesh):
    placed = (P("seq", "tp"), P("seq", "tp"), P(None, "tp"), P(None, "tp"), P("tp"), P("tp", None))
    return jax.shard_map(
        body, mesh=mesh, in_specs=placed, out_specs=P("seq", "tp"), check_vma=False
    )
```

time: 549 us -> 40.1 us (0.07); the launches traced: 541 us -> 39.8 us
  waiting for transfers between devices: 299 us -> 12.2 us
  matrix products: 105 us -> 0 us
  local copies, waits for them, and re-layouts: 47.3 us -> 0 us
  blocking collectives: 29.3 us -> 0 us
  starting transfers between devices: 37.2 us -> 11.1 us
  Pallas kernels: 0 us -> 16.5 us
  between operations: 14.1 us -> 0.07 us
  other arithmetic: 9.35 us -> 0 us
    all_to_all x8 -> x1, waiting for transfers between devices: 268 us -> 4.03 us  [body(): lax.all_to_all(wire, 'seq', split_axis=0, concat_axis=0, tiled=True)]
    dot_general x31 -> x0, matrix products: 105 us -> none  [the longest x6 23.4 us: complex_apply(): contract(table_im, data_re)]
    reduce_scatter x1 -> x0, waiting for transfers between devices: 30.7 us -> none  [body(): lax.psum_scatter(lax.dot_general(out_weight, gated, (((0,), (1,)), ((), (...]
    all_to_all x8 -> x1, starting transfers between devices: 37 us -> 7.26 us  [body(): lax.all_to_all(wire, 'seq', split_axis=0, concat_axis=0, tiled=True)]
    all_to_all x1 -> x0, blocking collectives: 29.3 us -> none  [body(): lax.all_to_all(conv_rows, 'seq', split_axis=0, concat_axis=1, tiled=True)]
    all_to_all x10 -> x0, local copies, waits for them, and re-layouts: 19.7 us -> none  [the longest x3 7.92 us: body(): lax.all_to_all(back_im, 'seq', split_axis=1, concat_axis=0, tiled=True)]
    pallas_call x0 -> x8, Pallas kernels: none -> 16.5 us  [call(): pl.pallas_call(kernel, out_shape=outs, in_specs=specs, out_specs=[out_spe...]
    add x5 -> x0, local copies, waits for them, and re-layouts: 13 us -> none  [the longest x3 9.75 us: rotate(): data_re * turn_im + data_im * turn_re]
  transfers between devices with their start and end apart: 9 -> 5, of which waited for: 9 -> 4; matrix products, arithmetic and copies ran while one was open for 10% -> 0% of each run, Pallas kernels for 0% -> 25%
where the time goes in v1:
time: 40.1 us; the launch traced here: 39.8 us
  Pallas kernels  16.5 us (41%)
  waiting for transfers between devices  12.2 us (30%)
  starting transfers between devices  11.1 us (28%)
    pallas_call x8, Pallas kernels, call(): pl.pallas_call(kernel, out_shape=outs, in_specs=specs, out_specs=[out_spe...  16.5 us
    ppermute x2, waiting for transfers between devices, to_chips(): lax.ppermute(each, 'tp', [(rank, (rank + 2 * hop) % tp) for rank in range...  7.87 us
    all_to_all x1, starting transfers between devices, body(): lax.all_to_all(wire, 'seq', split_axis=0, concat_axis=0, tiled=True)  7.26 us
    all_to_all x1, waiting for transfers between devices, body(): lax.all_to_all(wire, 'seq', split_axis=0, concat_axis=0, tiled=True)  4.03 us
    ppermute x2, starting transfers between devices, to_chips(): lax.ppermute(each, 'tp', [(rank, (rank + 2 * hop) % tp) for rank in range...  3.18 us
  transfers between devices with their start and end apart: 5, of which 4 were waited for; matrix products, arithmetic and copies ran while one was open for 0% of the time, Pallas kernels for 25%

profile of v1, /device:TPU:0, one launch (start us, length us, event | category | flops | bytes accessed | tf_op | source)
XLA Modules:
  0.0 39.8 jit_solution(1941224344937351026)
XLA Ops:
  0.0 3.3 %shard_map.64 = bf16[8,16,1024]{2,1,0:T(8,128)(2,1)} custom-call(bf16[256,1024]{1,0:T(8,128)(2,1)} %values_hbm.3, f32[16,1024]{1,0:T(8,128)} %rates_hbm.3), custom_call_target="tpu_custom_call" | custom-call | tf_op jit(solution)/shard_map/pallas_call | solution.py:353
  3.3 7.3 %all-to-all-start = ((bf16[8,16,1024]{2,1,0:T(8,128)(2,1)}), bf16[8,16,1024]{2,1,0:T(8,128)(2,1)S(1)}, u32[]{:S(2)}, u32[]{:S(2)}) async-start(bf16[8,16,1024]{2,1,0:T(8,128)(2,1)} %shard_map.64), calls=%async_computation | async-start | bytes 524288 | tf_op jit(solution)/shard_map/all_to_all | solution.py:387
  10.6 4.9 %shard_map.65 = (f32[256,1024]{1,0:T(8,128)S(1)}, f32[128,1024]{1,0:T(8,128)S(1)}, f32[16,1024]{1,0:T(8,128)S(1)}, f32[16,1024]{1,0:T(8,128)S(1)}, bf16[256,1024...) custom-call(bf16[256,1024]{1,0:T(8,128)(2,1)} %values_hbm.3, f32[16,1024]{1,0:T(8,128)} %rates_hbm.3, ...), custom_call_target="tpu_custom_call" | custom-call | tf_op jit(solution)/shard_map/pallas_call | solution.py:353
  15.5 4.0 %all-to-all-done.states_ref = bf16[8,16,1024]{2,1,0:T(8,128)(2,1)S(1)} async-done(((bf16[8,16,1024]{2,1,0:T(8,128)(2,1)}), bf16[8,16,1024]{2,1,0:T(8,128)(2,1)S(1)}, u32[]{:S(2)}, u32[]{:S(2)}) %all-to-all-start) | async-done | bytes 262176 | tf_op jit(solution)/shard_map/all_to_all | solution.py:387
  19.5 2.4 %shard_map.66 = (bf16[256,1024]{1,0:T(8,128)(2,1)S(1)}, bf16[256,512]{1,0:T(8,128)(2,1)S(1)}, bf16[1024,512]{1,0:T(8,128)(2,1)S(1)}, bf16[1024,1536]{1,0:T(8,128)(2,1)S(1)}) custom-call(bf16[8,16,1024]{2,1,0:T(8,128)(2,1)S(1)} %all-to-all-done.states_ref, f32[256,1024]{1,0:T(8,128)S(1)} %get-tuple-element.20.near_ref, ...), custom_call_target="tpu_custom_call" | custom-call | tf_op jit(solution)/shard_map/pallas_call | solution.py:353
  21.9 0.1 collective-permute-start.1
  22.0 2.4 %shard_map.67 = (f32[256,512]{1,0:T(8,128)S(1)}, bf16[256,1536]{1,0:T(8,128)(2,1)S(1)}, bf16[1024,768]{1,0:T(8,128)(2,1)S(1)}) custom-call(bf16[256,1024]{1,0:T(8,128)(2,1)S(1)} %get-tuple-element.26.gated_ref, bf16[1024,512]{1,0:T(8,128)(2,1)S(1)} %get-tuple-element.27.kept_weight, bf16[1024,1536]{1,0:T(8,128)(2,1)S(1)} %get-tuple-element.28.sent_weight, ...), custom_call_target="tpu_custom_call" | custom-call | tf_op jit(solution)/shard_map/pallas_call | solution.py:353
  24.5 0.6 %collective-permute-start = (bf16[256,1536]{1,0:T(8,128)(2,1)S(1)}, bf16[256,1536]{1,0:T(8,128)(2,1)S(1)}, u32[]{:S(2)}, u32[]{:S(2)}) collective-permute-start(bf16[256,1536]{1,0:T(8,128)(2,1)S(1)} %get-tuple-element.29), channel_id=1, source_target_pairs={{0,1},{1,0},{2,3},{3,2},{4,5},{5,4},{6,7},{7,6},{8,9},{9,8},{10,11... | collective-permute-start | bytes 2359304 | tf_op jit(solution)/shard_map/ppermute | solution.py:441
  25.0 0.0 collective-permute-done.1.moved_ref.moved_first_ref
  25.1 1.6 %collective-permute-start.2 = (bf16[256,256]{1,0:T(8,128)(2,1)S(1)}, bf16[256,256]{1,0:T(8,128)(2,1)S(1)}, u32[]{:S(2)}, u32[]{:S(2)}) collective-permute-start(bf16[256,256]{1,0:T(8,128)(2,1)S(1)} %shard_map.68), channel_id=1, source_target_pairs={{0,2},{1,3},{2,0},{3,1},{4,6},{5,7},{6,4},{7,5},{8,10},{9,11},{10,... | collective-permute-start | bytes 393224 | tf_op jit(solution)/shard_map/ppermute | solution.py:445
  26.7 0.3 collective-permute-done.moved_ref
  26.9 0.6 %shard_map.70 = bf16[256,768]{1,0:T(8,128)(2,1)S(1)} custom-call(bf16[256,1024]{1,0:T(8,128)(2,1)S(1)} %get-tuple-element.26.gated_ref, bf16[1024,768]{1,0:T(8,128)(2,1)S(1)} %get-tuple-element.34.weight_ref, bf16[256,1536]{1,0:T(8,128)(2,1)S(1)} %collective-permute-done.moved_ref), custom_call_target="tpu_custom_call" | custom-call | tf_op jit(solution)/shard_map/pallas_call | solution.py:353
  27.5 1.6 %collective-permute-start.3 = (bf16[256,768]{1,0:T(8,128)(2,1)S(1)}, bf16[256,768]{1,0:T(8,128)(2,1)S(1)}, u32[]{:S(2)}, u32[]{:S(2)}) collective-permute-start(bf16[256,768]{1,0:T(8,128)(2,1)S(1)} %shard_map.70), channel_id=1, source_target_pairs={{0,2},{1,3},{2,0},{3,1},{4,6},{5,7},{6,4},{7,5},{8,10},{9,11},{10,... | collective-permute-start | bytes 1179656 | tf_op jit(solution)/shard_map/ppermute | solution.py:445
  29.1 1.4 %collective-permute-done.2.refs_0_ = bf16[256,256]{1,0:T(8,128)(2,1)S(1)} collective-permute-done((bf16[256,256]{1,0:T(8,128)(2,1)S(1)}, bf16[256,256]{1,0:T(8,128)(2,1)S(1)}, u32[]{:S(2)}, u32[]{:S(2)}) %collective-permute-start.2) | collective-permute-done | bytes 131104 | tf_op jit(solution)/shard_map/ppermute | solution.py:445
  30.6 2.0 %shard_map.69 = (bf16[256,256]{1,0:T(8,128)(2,1)S(1)}, f32[256,768]{1,0:T(8,128)S(1)}) custom-call(bf16[256,1024]{1,0:T(8,128)(2,1)S(1)} %get-tuple-element.26.gated_ref, bf16[1024,4096]{1,0:T(8,128)(2,1)} %weight_hbm.7, bf16[256,1536]{1,0:T(8,128)(2,1)S(1)} %collective-permute-done.moved_ref, f32[256,512]{1,0:T(8,128)S(1)} %get-tuple-element.30.kept_ref, ...), custom_call_target="tpu_custom_call" | custom-call | flops 8589934592 | tf_op jit(solution)/shard_map/pallas_call | solution.py:353
  32.6 6.4 %collective-permute-done.3.refs_0_ = bf16[256,768]{1,0:T(8,128)(2,1)S(1)} collective-permute-done((bf16[256,768]{1,0:T(8,128)(2,1)S(1)}, bf16[256,768]{1,0:T(8,128)(2,1)S(1)}, u32[]{:S(2)}, u32[]{:S(2)}) %collective-permute-start.3) | collective-permute-done | bytes 393248 | tf_op jit(solution)/shard_map/ppermute | solution.py:445
  39.0 0.8 %shard_map.71 = bf16[256,1024]{1,0:T(8,128)(2,1)} custom-call(bf16[256,256]{1,0:T(8,128)(2,1)S(1)} %get-tuple-element.32.first_ref, f32[256,768]{1,0:T(8,128)S(1)} %get-tuple-element.33.own_ref, bf16[256,768]{1,0:T(8,128)(2,1)S(1)} %collective-permute-done.3.refs_0_), custom_call_target="tpu_custom_call" | custom-call | tf_op jit(solution)/shard_map/pallas_call | solution.py:353
  (1 shorter events, 0.0 us)
Async XLA Ops:
  3.3 16.2 %all-to-all-start = ((bf16[8,16,1024]{2,1,0:T(8,128)(2,1)}), bf16[8,16,1024]{2,1,0:T(8,128)(2,1)S(1)}, u32[]{:S(2)}, u32[]{:S(2)}) async-start(bf16[8,16,1024]{2,1,0:T(8,128)(2,1)} %shard_map.64), calls=%async_computation | async-start | bytes 524288 | tf_op jit(solution)/shard_map/all_to_all | solution.py:387
  21.9 3.1 %collective-permute-start.1 = (bf16[256,512]{1,0:T(8,128)(2,1)S(1)}, bf16[256,512]{1,0:T(8,128)(2,1)S(1)}, u32[]{:S(2)}, u32[]{:S(2)}) collective-permute-start(bf16[256,512]{1,0:T(8,128)(2,1)S(1)} %get-tuple-element.31), channel_id=1, source_target_pairs={{0,1},{1,0},{2,3},{3,2},{4,5},{5,4},{6,7},{7,6},{8,9},{9,8},{10,11... | collective-permute-start | bytes 786440 | tf_op jit(solution)/shard_map/ppermute | solution.py:430
  24.5 2.5 %collective-permute-start = (bf16[256,1536]{1,0:T(8,128)(2,1)S(1)}, bf16[256,1536]{1,0:T(8,128)(2,1)S(1)}, u32[]{:S(2)}, u32[]{:S(2)}) collective-permute-start(bf16[256,1536]{1,0:T(8,128)(2,1)S(1)} %get-tuple-element.29), channel_id=1, source_target_pairs={{0,1},{1,0},{2,3},{3,2},{4,5},{5,4},{6,7},{7,6},{8,9},{9,8},{10,11... | collective-permute-start | bytes 2359304 | tf_op jit(solution)/shard_map/ppermute | solution.py:441
  25.1 5.5 %collective-permute-start.2 = (bf16[256,256]{1,0:T(8,128)(2,1)S(1)}, bf16[256,256]{1,0:T(8,128)(2,1)S(1)}, u32[]{:S(2)}, u32[]{:S(2)}) collective-permute-start(bf16[256,256]{1,0:T(8,128)(2,1)S(1)} %shard_map.68), channel_id=1, source_target_pairs={{0,2},{1,3},{2,0},{3,1},{4,6},{5,7},{6,4},{7,5},{8,10},{9,11},{10,... | collective-permute-start | bytes 393224 | tf_op jit(solution)/shard_map/ppermute | solution.py:445
  27.5 11.5 %collective-permute-start.3 = (bf16[256,768]{1,0:T(8,128)(2,1)S(1)}, bf16[256,768]{1,0:T(8,128)(2,1)S(1)}, u32[]{:S(2)}, u32[]{:S(2)}) collective-permute-start(bf16[256,768]{1,0:T(8,128)(2,1)S(1)} %shard_map.70), channel_id=1, source_target_pairs={{0,2},{1,3},{2,0},{3,1},{4,6},{5,7},{6,4},{7,5},{8,10},{9,11},{10,... | collective-permute-start | bytes 1179656 | tf_op jit(solution)/shard_map/ppermute | solution.py:445

commit v2 on v1

--- a/solution.py
+++ b/solution.py
@@ -74,22 +74,23 @@
     return copies
 
 
+def group_order(count):
+    return sorted(range(count), key=lambda rank: (abs(2 * rank + 1 - count), -rank))
+
+
 def wait_all(copies):
     for copy in copies:
         copy.wait()
 
 
-def state_kernel(
-    values_hbm, rates_hbm, wire_hbm, values_ref, rates_ref, state_ref, sems, out_sems
-):
+def state_kernel(values_hbm, rates_hbm, wire_ref, values_ref, rates_ref, sems):
     tok, chan = values_ref.shape
     modes = rates_ref.shape[0]
-    shards = wire_hbm.shape[0]
     parts = sems.shape[0] - 1
     width = chan // parts
     first = pltpu.make_async_copy(rates_hbm, rates_ref, sems.at[parts])
     first.start()
-    pieces, outs = [], []
+    pieces = []
     for part in range(parts):
         lanes = pl.ds(part * width, width)
         pieces.append(
@@ -116,24 +117,14 @@
             jnp.sum(held[mode] * jnp.exp(-row_of(rates, mode) * left), axis=0, keepdims=True)
             for mode in range(modes)
         ]
-        state_ref[:, lanes] = jnp.concatenate(rows, axis=0).astype(BF16)
-        if (index + 1) * LANE % width == 0:
-            part = index * LANE // width
-            lanes = pl.ds(part * width, width)
-            for shard in range(shards):
-                outs.append(
-                    pltpu.make_async_copy(
-                        state_ref.at[:, lanes], wire_hbm.at[shard, :, lanes],
-                        out_sems.at[part, shard],
-                    )
-                )
-                outs[-1].start()
-    wait_all(outs)
+        state = jnp.concatenate(rows, axis=0).astype(BF16)
+        for shard in range(wire_ref.shape[0]):
+            wire_ref[shard, :, lanes] = state
 
 
 def local_kernel(
     values_hbm, rates_hbm, residues_hbm, skip_hbm, gate_hbm, weight_hbm,
-    near_ref, starts_ref, ahead_ref, rates_ref, spread_ref, first_weight,
+    near_ref, starts_ref, ahead_ref, rates_ref, spread_ref, first_weight, kept_weight,
     values_ref, residues_ref, skip_ref, gate_ref, wide_ref, taps_ref, sems, weight_sems,
 ):
     tok, chan = values_ref.shape
@@ -153,8 +144,9 @@
     ]
     for copy in copies:
         copy.start()
-    slots = range(lax.axis_size("tp") // 2)
-    rest = column_copies(1, 0, slots, weight_hbm, first_weight, weight_sems)
+    slots = range(1, lax.axis_size("tp") // 2)
+    rest = column_copies(1, 0, slots, weight_hbm, first_weight, weight_sems.at[0])
+    rest += column_copies(0, 0, slots, weight_hbm, kept_weight, weight_sems.at[1])
     table = spread_table(tok, False)
     wait_all(copies)
     wide_ref[...] = jnp.dot(table, values_ref[...], preferred_element_type=F32)
@@ -221,12 +213,12 @@
 
 def gate_kernel(
     states_ref, near_ref, starts_ref, ahead_ref, rates_ref, spread_ref, weight_ref, weight_hbm,
-    gated_ref, sent_ref, kept_weight, later_weight, held_ref, state_ref, decay_ref, sems,
+    gated_ref, sent_ref, later_weight, last_weight, held_ref, state_ref, decay_ref, sems,
 ):
-    slots = range(lax.axis_size("tp") // 2)
+    slots = range(1, lax.axis_size("tp") // 2)
     begin = weight_ref.shape[1] // len(slots)
-    rest = column_copies(0, 0, slots, weight_hbm, kept_weight, sems.at[0])
-    rest += column_copies(1, begin, slots, weight_hbm, later_weight, sems.at[1])
+    rest = column_copies(1, begin, slots, weight_hbm, later_weight, sems.at[0])
+    rest += column_copies(0, begin, slots, weight_hbm, last_weight, sems.at[1])
     tok, chan = spread_ref.shape
     shards, modes = states_ref.shape[:2]
     run = tok // SUB
@@ -235,8 +227,9 @@
     decay_ref[...] = jnp.exp(-rates)
     far = jnp.exp(-float(tok) * rates)
     before = jnp.zeros((modes, chan), F32)
+    order = group_order(shards)
     for shard in range(shards - 1):
-        passed = far * before + states_ref[shard].astype(F32)
+        passed = far * before + states_ref[order.index(shard)].astype(F32)
         before = jnp.where(shard < place, passed, before)
     state_ref[...] = before * ahead_ref[...]
     passed = (sublane() * run).astype(F32)
@@ -283,43 +276,48 @@
     return jnp.dot(gated_ref[...], weight, preferred_element_type=F32)
 
 
-def middle_kernel(
-    gated_ref, kept_weight, sent_weight, weight_hbm, kept_ref, sent_ref, later_ref, sems
-):
-    chips = lax.axis_size("tp") // 2
-    begin = kept_ref.shape[1] // chips
-    copies = column_copies(0, begin, range(1, chips), weight_hbm, later_ref, sems)
+def middle_kernel(gated_ref, kept_weight, sent_weight, kept_ref, sent_ref):
     project(gated_ref, kept_weight, kept_ref)
     project(gated_ref, sent_weight, sent_ref)
-    wait_all(copies)
 
 
 def join_kernel(kept_ref, moved_ref, *going_refs):
     wide = going_refs[0].shape[1]
-    for hop, going_ref in enumerate(going_refs, 1):
-        lanes = slice(hop * wide, (hop + 1) * wide)
+    for at, going_ref in enumerate(going_refs):
+        lanes = slice(at * wide, (at + 1) * wide)
         going_ref[...] = (kept_ref[:, lanes] + moved_ref[:, lanes].astype(F32)).astype(BF16)
 
 
-def going_kernel(gated_ref, weight_ref, moved_ref, *going_refs):
+def going_kernel(gated_ref, weight_ref, moved_ref, after_ref, *going_refs):
     wide = going_refs[0].shape[1]
-    for hop, going_ref in enumerate(going_refs, 1):
-        lanes = slice((hop - 1) * wide, hop * wide)
+    for at, going_ref in enumerate(going_refs):
+        lanes = slice(at * wide, (at + 1) * wide)
         total = product(gated_ref, weight_ref[:, lanes])
-        total = total + moved_ref[:, hop * wide : (hop + 1) * wide].astype(F32)
-        going_ref[...] = total.astype(BF16)
-
-
-def own_kernel(gated_ref, weight_hbm, moved_ref, kept_ref, moved_first_ref, *refs):
+        going_ref[...] = (total + moved_ref[:, lanes].astype(F32)).astype(BF16)
+
+
+def late_kernel(gated_ref, weight_hbm, *refs):
+    (low_ref, high_ref, weight_ref, sems) = refs[-4:]
+    half = low_ref.shape[1]
+    wait_all(column_copies(1, 0, range(1), weight_hbm, weight_ref, sems))
+    low_ref[...] = product(gated_ref, weight_ref[:, :half]).astype(BF16)
+    high_ref[...] = product(gated_ref, weight_ref[:, half:]).astype(BF16)
+
+
+def own_kernel(gated_ref, weight_hbm, low_ref, high_ref, *refs):
     others, (first_ref, own_ref, weight_ref, sems) = refs[:-4], refs[-4:]
-    narrow, wide = first_ref.shape[1], own_ref.shape[1]
-    copies = column_copies(0, narrow, range(1), weight_hbm, weight_ref, sems)
-    total = kept_ref[:, :narrow] + moved_first_ref[:, :narrow].astype(F32)
+    narrow, half = first_ref.shape[1], low_ref.shape[1]
+    wait_all(column_copies(0, 0, range(1), weight_hbm, weight_ref, sems))
+    total = low_ref[:, :narrow].astype(F32) + product(gated_ref, weight_ref[:, :narrow])
     for other in others:
         total = total + other[...].astype(F32)
     first_ref[...] = total.astype(BF16)
-    wait_all(copies)
-    own_ref[...] = moved_ref[:, :wide].astype(F32) + product(gated_ref, weight_ref[...])
+    own_ref[:, : half - narrow] = low_ref[:, narrow:].astype(F32) + product(
+        gated_ref, weight_ref[:, narrow:half]
+    )
+    own_ref[:, half - narrow :] = high_ref[...].astype(F32) + product(
+        gated_ref, weight_ref[:, half:]
+    )
 
 
 def final_kernel(first_ref, own_ref, *refs):
@@ -366,6 +364,7 @@
     tok, chan = values.shape
     modes = rates.shape[0]
     chips = tp // 2
+    away = chips - 1
     block = out_weight.shape[1] // tp
     here = pltpu.VMEM
     parts = 4 if chan % (4 * LANE) == 0 else 1
@@ -378,17 +377,17 @@
         scratch=[
             here((tok, chan), BF16),
             here((modes, chan), F32),
-            here((modes, chan), BF16),
             pltpu.SemaphoreType.DMA((parts + 1,)),
-            pltpu.SemaphoreType.DMA((parts, shards)),
         ],
-        out_spec=ANY,
-    )
-    states = lax.all_to_all(wire, "seq", split_axis=0, concat_axis=0, tiled=True)
+    )
+    states = lax.all_to_all(
+        wire, "seq", split_axis=0, concat_axis=0, tiled=True,
+        axis_index_groups=[group_order(shards)],
+    )
     narrow = max(LANE, block // 4)
     wide = block - narrow
     weight = (HBM, out_weight)
-    tables = call(
+    *tables, first_weight, kept_weight = call(
         local_kernel,
         [
             here((tok, chan), F32),
@@ -396,7 +395,8 @@
             here((modes, chan), F32),
             here((modes, chan), F32),
             here((tok, chan), BF16),
-            here((chan, chips * narrow), BF16),
+            here((chan, away * narrow), BF16),
+            here((chan, away * narrow), BF16),
         ],
         *sources, weight,
         scratch=[
@@ -407,36 +407,31 @@
             here((tok, chan), F32),
             here((tok // SUB, LANE), F32),
             pltpu.SemaphoreType.DMA((len(sources),)),
-            pltpu.SemaphoreType.DMA((chips * ROW_CUTS,)),
+            pltpu.SemaphoreType.DMA((2, away * ROW_CUTS)),
         ],
     )
 
-    gated, sent, kept_weight, sent_weight = call(
+    gated, sent, sent_weight, last_weight = call(
         gate_kernel,
         [
             here((tok, chan), BF16),
-            here((tok, chips * narrow), BF16),
-            here((chan, chips * narrow), BF16),
-            here((chan, chips * wide), BF16),
+            here((tok, away * narrow), BF16),
+            here((chan, away * wide), BF16),
+            here((chan, away * wide), BF16),
         ],
-        states, *tables, weight,
+        states, *tables, first_weight, weight,
         scratch=[
             here((tok, chan), BF16),
             here((modes, chan), F32),
             here((modes, chan), F32),
-            pltpu.SemaphoreType.DMA((2, chips * ROW_CUTS)),
+            pltpu.SemaphoreType.DMA((2, away * ROW_CUTS)),
         ],
     )
     moved_first = lax.ppermute(sent, "tp", cores)
-    kept, sent, later = call(
+    kept, sent = call(
         middle_kernel,
-        [
-            here((tok, chips * narrow), F32),
-            here((tok, chips * wide), BF16),
-            here((chan, (chips - 1) * wide), BF16),
-        ],
-        gated, kept_weight, sent_weight, weight,
-        scratch=[pltpu.SemaphoreType.DMA(((chips - 1) * ROW_CUTS,))],
+        [here((tok, away * narrow), F32), here((tok, away * wide), BF16)],
+        gated, kept_weight, sent_weight,
     )
     moved = lax.ppermute(sent, "tp", cores)
 
@@ -446,24 +441,27 @@
             for hop, each in enumerate(going, 1)
         ]
 
-    first = to_chips(
-        call(
-            join_kernel, [here((tok, narrow), BF16)] * (chips - 1), kept, moved_first,
-            macs=16 * tok * chan * block,
-        )
-    )
-    second = to_chips(
-        call(going_kernel, [here((tok, wide), BF16)] * (chips - 1), gated, later, moved)
-    )
+    hint = 16 * tok * chan * block
+    going = call(join_kernel, [here((tok, narrow), BF16)] * away, kept, moved_first, macs=hint)
+    first = to_chips(going)
+    going = call(
+        going_kernel, [here((tok, wide), BF16)] * away,
+        gated, last_weight, moved, (ANY, going[-1]),
+    )
+    second = to_chips(going)
+    late = [here((chan, block), BF16), pltpu.SemaphoreType.DMA((ROW_CUTS,))]
+    halves = call(
+        late_kernel, [here((tok, block // 2), BF16)] * 2,
+        gated, weight, (ANY, going[-1]), (ANY, first[-1]), scratch=late, macs=hint,
+    )
+    halves = [lax.ppermute(each, "tp", cores) for each in halves]
     done, own = call(
         own_kernel, [here((tok, narrow), BF16), here((tok, wide), F32)],
-        gated, weight, moved, kept, moved_first, *first,
-        macs=16 * tok * chan * block,
-        scratch=[here((chan, wide), BF16), pltpu.SemaphoreType.DMA((ROW_CUTS,))],
+        gated, weight, *halves, *first, scratch=late,
     )
     (out,) = call(
         final_kernel, [jax.ShapeDtypeStruct((tok, block), BF16)], done, own, *second,
-        scratch=[here((tok, wide), BF16), pltpu.SemaphoreType.DMA((5,))],
+        scratch=[here((tok, wide), BF16), pltpu.SemaphoreType.DMA((3,))],
         out_spec=ANY,
     )
     return out

time: 40.1 us -> 36.7 us (0.915)
  waiting for transfers between devices: 12.2 us -> 7.74 us
  starting transfers between devices: 11.1 us -> 11.9 us
    ppermute x2, waiting for transfers between devices: 7.87 us -> 4.07 us  [to_chips(): lax.ppermute(each, 'tp', [(rank, (rank + 2 * hop) % tp) for rank in range...]
    all_to_all x1, waiting for transfers between devices: 4.03 us -> 2.21 us  [body(): lax.all_to_all(wire, 'seq', split_axis=0, concat_axis=0, tiled=True, axis...]
    ppermute x0 -> x2, waiting for transfers between devices: none -> 1.4 us  [body(): halves = [lax.ppermute(each, 'tp', cores) for each in halves]]
    ppermute x0 -> x2, starting transfers between devices: none -> 0.57 us  [body(): halves = [lax.ppermute(each, 'tp', cores) for each in halves]]
    all_to_all x1, starting transfers between devices: 7.26 us -> 7.83 us  [body(): lax.all_to_all(wire, 'seq', split_axis=0, concat_axis=0, tiled=True, axis...]
    pallas_call x8 -> x9, Pallas kernels: 16.5 us -> 16.7 us  [call(): pl.pallas_call(kernel, out_shape=outs, in_specs=specs, out_specs=[out_spe...]
  transfers between devices with their start and end apart: 5 -> 7, of which waited for: 4 -> 6; matrix products, arithmetic and copies ran while one was open for 0% -> 0% of each run, Pallas kernels for 25% -> 29%
where the time goes in v2:
time: 36.7 us; the launch traced here: 36.4 us
  Pallas kernels  16.7 us (46%)
  starting transfers between devices  11.9 us (32%)
  waiting for transfers between devices  7.74 us (21%)
    pallas_call x9, Pallas kernels, call(): pl.pallas_call(kernel, out_shape=outs, in_specs=specs, out_specs=[out_spe...  16.7 us
    all_to_all x1, starting transfers between devices, body(): lax.all_to_all(wire, 'seq', split_axis=0, concat_axis=0, tiled=True, axis...  7.83 us
    ppermute x2, waiting for transfers between devices, to_chips(): lax.ppermute(each, 'tp', [(rank, (rank + 2 * hop) % tp) for rank in range...  4.07 us
    ppermute x2, starting transfers between devices, to_chips(): lax.ppermute(each, 'tp', [(rank, (rank + 2 * hop) % tp) for rank in range...  2.86 us
    all_to_all x1, waiting for transfers between devices, body(): lax.all_to_all(wire, 'seq', split_axis=0, concat_axis=0, tiled=True, axis...  2.21 us
    ppermute x2, waiting for transfers between devices, body(): halves = [lax.ppermute(each, 'tp', cores) for each in halves]  1.4 us
  transfers between devices with their start and end apart: 7, of which 6 were waited for; matrix products, arithmetic and copies ran while one was open for 0% of the time, Pallas kernels for 29%

profile of v2, /device:TPU:0, one launch (start us, length us, event | category | flops | bytes accessed | tf_op | source)
XLA Modules:
  0.0 36.4 jit_solution(576100641921748582)
XLA Ops:
  0.0 3.1 %shard_map.64 = bf16[8,16,1024]{2,1,0:T(8,128)(2,1)} custom-call(bf16[256,1024]{1,0:T(8,128)(2,1)} %values_hbm.3, f32[16,1024]{1,0:T(8,128)} %rates_hbm.3), custom_call_target="tpu_custom_call" | custom-call | tf_op jit(solution)/shard_map/pallas_call | solution.py:351
  3.1 7.8 %all-to-all-start = ((bf16[8,16,1024]{2,1,0:T(8,128)(2,1)}), bf16[8,16,1024]{2,1,0:T(8,128)(2,1)S(1)}, u32[]{:S(2)}, u32[]{:S(2)}) async-start(bf16[8,16,1024]{2,1,0:T(8,128)(2,1)} %shard_map.64), calls=%async_computation | async-start | bytes 524288 | tf_op jit(solution)/shard_map/all_to_all | solution.py:383
  10.9 4.9 %shard_map.65 = (f32[256,1024]{1,0:T(8,128)S(1)}, f32[128,1024]{1,0:T(8,128)S(1)}, f32[16,1024]{1,0:T(8,128)S(1)}, f32[16,1024]{1,0:T(8,128)S(1)}, bf16[256,1024...) custom-call(bf16[256,1024]{1,0:T(8,128)(2,1)} %values_hbm.3, f32[16,1024]{1,0:T(8,128)} %rates_hbm.3, ...), custom_call_target="tpu_custom_call" | custom-call | tf_op jit(solution)/shard_map/pallas_call | solution.py:351
  15.8 2.2 %all-to-all-done.states_ref = bf16[8,16,1024]{2,1,0:T(8,128)(2,1)S(1)} async-done(((bf16[8,16,1024]{2,1,0:T(8,128)(2,1)}), bf16[8,16,1024]{2,1,0:T(8,128)(2,1)S(1)}, u32[]{:S(2)}, u32[]{:S(2)}) %all-to-all-start) | async-done | bytes 262176 | tf_op jit(solution)/shard_map/all_to_all | solution.py:383
  18.0 2.1 %shard_map.66 = (bf16[256,1024]{1,0:T(8,128)(2,1)S(1)}, bf16[256,256]{1,0:T(8,128)(2,1)S(1)}, bf16[1024,768]{1,0:T(8,128)(2,1)S(1)}, bf16[1024,768]{1,0:T(8,128)(2,1)S(1)}) custom-call(bf16[8,16,1024]{2,1,0:T(8,128)(2,1)S(1)} %all-to-all-done.states_ref, f32[256,1024]{1,0:T(8,128)S(1)} %get-tuple-element.22.near_ref, ...), custom_call_target="tpu_custom_call" | custom-call | tf_op jit(solution)/shard_map/pallas_call | solution.py:351
  20.1 0.1 collective-permute-start.1
  20.2 0.7 %shard_map.67 = (f32[256,256]{1,0:T(8,128)S(1)}, bf16[256,768]{1,0:T(8,128)(2,1)S(1)}) custom-call(bf16[256,1024]{1,0:T(8,128)(2,1)S(1)} %get-tuple-element.28.gated_ref, bf16[1024,256]{1,0:T(8,128)(2,1)S(1)} %get-tuple-element.30.kept_weight, bf16[1024,768]{1,0:T(8,128)(2,1)S(1)} %get-tuple-element.31.sent_weight), custom_call_target="tpu_custom_call" | custom-call | tf_op jit(solution)/shard_map/pallas_call | solution.py:351
  20.9 0.6 %collective-permute-start = (bf16[256,768]{1,0:T(8,128)(2,1)S(1)}, bf16[256,768]{1,0:T(8,128)(2,1)S(1)}, u32[]{:S(2)}, u32[]{:S(2)}) collective-permute-start(bf16[256,768]{1,0:T(8,128)(2,1)S(1)} %get-tuple-element.32), channel_id=1, source_target_pairs={{0,1},{1,0},{2,3},{3,2},{4,5},{5,4},{6,7},{7,6},{8,9},{9,8},{10,11... | collective-permute-start | bytes 1179656 | tf_op jit(solution)/shard_map/ppermute | solution.py:436
  21.5 0.1 collective-permute-done.1.moved_ref
  21.6 1.6 %collective-permute-start.2 = (bf16[256,256]{1,0:T(8,128)(2,1)S(1)}, bf16[256,256]{1,0:T(8,128)(2,1)S(1)}, u32[]{:S(2)}, u32[]{:S(2)}) collective-permute-start(bf16[256,256]{1,0:T(8,128)(2,1)S(1)} %shard_map.68.after_ref), channel_id=1, source_target_pairs={{0,2},{1,3},{2,0},{3,1},{4,6},{5,7},{6,4},{7,5},{8,10},{9,11},{10,... | collective-permute-start | bytes 393224 | tf_op jit(solution)/shard_map/ppermute | solution.py:440
  23.2 0.0 collective-permute-done.moved_ref
  23.2 0.6 %shard_map.69.refs_0_ = bf16[256,768]{1,0:T(8,128)(2,1)S(1)} custom-call(bf16[256,1024]{1,0:T(8,128)(2,1)S(1)} %get-tuple-element.28.gated_ref, bf16[1024,768]{1,0:T(8,128)(2,1)S(1)} %get-tuple-element.29.weight_ref, bf16[256,768]{1,0:T(8,128)(2,1)S(1)} %collective-permute-done.moved_ref, bf16[256,256]{1,0:T(8,128)(2,1)S(1)} %shard_map.68.after_ref), custom_call_target="tpu_custom_call" | custom-call | tf_op jit(solution)/shard_map/pallas_call | solution.py:351
  23.7 1.3 %collective-permute-start.5 = (bf16[256,768]{1,0:T(8,128)(2,1)S(1)}, bf16[256,768]{1,0:T(8,128)(2,1)S(1)}, u32[]{:S(2)}, u32[]{:S(2)}) collective-permute-start(bf16[256,768]{1,0:T(8,128)(2,1)S(1)} %shard_map.69.refs_0_), channel_id=1, source_target_pairs={{0,2},{1,3},{2,0},{3,1},{4,6},{5,7},{6,4},{7,5},{8,10},{9,11},{10,... | collective-permute-start | bytes 1179656 | tf_op jit(solution)/shard_map/ppermute | solution.py:440
  25.0 2.9 %collective-permute-done.2.refs_1_.refs_0_ = bf16[256,256]{1,0:T(8,128)(2,1)S(1)} collective-permute-done((bf16[256,256]{1,0:T(8,128)(2,1)S(1)}, bf16[256,256]{1,0:T(8,128)(2,1)S(1)}, u32[]{:S(2)}, u32[]{:S(2)}) %collective-permute-start.2) | collective-permute-done | bytes 131104 | tf_op jit(solution)/shard_map/ppermute | solution.py:440
  27.9 2.3 %shard_map.70 = (bf16[256,512]{1,0:T(8,128)(2,1)S(1)}, bf16[256,512]{1,0:T(8,128)(2,1)S(1)}) custom-call(bf16[256,1024]{1,0:T(8,128)(2,1)S(1)} %get-tuple-element.28.gated_ref, bf16[1024,4096]{1,0:T(8,128)(2,1)} %weight_hbm.7, bf16[256,768]{1,0:T(8,128)(2,1)S(1)} %shard_map.69.refs_0_, bf16[256,256]{1,0:T(8,128)(2,1)S(1)} %collective-permute-done.2.refs_1_.refs_0_), custom_call_target="tpu_custom_call" | custom-call | flops 8589934592 | tf_op jit(solution)/shard_map/pallas_call | solution.py:351
  30.2 0.1 collective-permute-start.3
  30.2 0.5 %collective-permute-start.4 = (bf16[256,512]{1,0:T(8,128)(2,1)S(1)}, bf16[256,512]{1,0:T(8,128)(2,1)S(1)}, u32[]{:S(2)}, u32[]{:S(2)}) collective-permute-start(bf16[256,512]{1,0:T(8,128)(2,1)S(1)} %get-tuple-element.36), channel_id=1, source_target_pairs={{0,1},{1,0},{2,3},{3,2},{4,5},{5,4},{6,7},{7,6},{8,9},{9,8},{10,11... | collective-permute-start | bytes 786440 | tf_op jit(solution)/shard_map/ppermute | solution.py:457
  30.7 1.0 %collective-permute-done.3.low_ref = bf16[256,512]{1,0:T(8,128)(2,1)S(1)} collective-permute-done((bf16[256,512]{1,0:T(8,128)(2,1)S(1)}, bf16[256,512]{1,0:T(8,128)(2,1)S(1)}, u32[]{:S(2)}, u32[]{:S(2)}) %collective-permute-start.3) | collective-permute-done | bytes 262176 | tf_op jit(solution)/shard_map/ppermute | solution.py:457
  31.8 0.4 %collective-permute-done.4.high_ref = bf16[256,512]{1,0:T(8,128)(2,1)S(1)} collective-permute-done((bf16[256,512]{1,0:T(8,128)(2,1)S(1)}, bf16[256,512]{1,0:T(8,128)(2,1)S(1)}, u32[]{:S(2)}, u32[]{:S(2)}) %collective-permute-start.4) | collective-permute-done | bytes 262176 | tf_op jit(solution)/shard_map/ppermute | solution.py:457
  32.1 2.3 %shard_map.71 = (bf16[256,256]{1,0:T(8,128)(2,1)S(1)}, f32[256,768]{1,0:T(8,128)S(1)}) custom-call(bf16[256,1024]{1,0:T(8,128)(2,1)S(1)} %get-tuple-element.28.gated_ref, bf16[1024,4096]{1,0:T(8,128)(2,1)} %weight_hbm.7, bf16[256,512]{1,0:T(8,128)(2,1)S(1)} %collective-permute-done.3.low_ref, bf16[256,512]{1,0:T(8,128)(2,1)S(1)} %collective-permute-done.4.high_ref, ...), custom_call_target="tpu_custom_call" | custom-call | tf_op jit(solution)/shard_map/pallas_call | solution.py:351
  34.4 1.2 %collective-permute-done.5.refs_0_ = bf16[256,768]{1,0:T(8,128)(2,1)S(1)} collective-permute-done((bf16[256,768]{1,0:T(8,128)(2,1)S(1)}, bf16[256,768]{1,0:T(8,128)(2,1)S(1)}, u32[]{:S(2)}, u32[]{:S(2)}) %collective-permute-start.5) | collective-permute-done | bytes 393248 | tf_op jit(solution)/shard_map/ppermute | solution.py:440
  35.6 0.8 %shard_map.72 = bf16[256,1024]{1,0:T(8,128)(2,1)} custom-call(bf16[256,256]{1,0:T(8,128)(2,1)S(1)} %get-tuple-element.37.first_ref, f32[256,768]{1,0:T(8,128)S(1)} %get-tuple-element.38.own_ref, bf16[256,768]{1,0:T(8,128)(2,1)S(1)} %collective-permute-done.5.refs_0_), custom_call_target="tpu_custom_call" | custom-call | tf_op jit(solution)/shard_map/pallas_call | solution.py:351
  (1 shorter events, 0.0 us)
Async XLA Ops:
  3.1 14.9 %all-to-all-start = ((bf16[8,16,1024]{2,1,0:T(8,128)(2,1)}), bf16[8,16,1024]{2,1,0:T(8,128)(2,1)S(1)}, u32[]{:S(2)}, u32[]{:S(2)}) async-start(bf16[8,16,1024]{2,1,0:T(8,128)(2,1)} %shard_map.64), calls=%async_computation | async-start | bytes 524288 | tf_op jit(solution)/shard_map/all_to_all | solution.py:383
  20.1 1.4 %collective-permute-start.1 = (bf16[256,256]{1,0:T(8,128)(2,1)S(1)}, bf16[256,256]{1,0:T(8,128)(2,1)S(1)}, u32[]{:S(2)}, u32[]{:S(2)}) collective-permute-start(bf16[256,256]{1,0:T(8,128)(2,1)S(1)} %get-tuple-element.34), channel_id=1, source_target_pairs={{0,1},{1,0},{2,3},{3,2},{4,5},{5,4},{6,7},{7,6},{8,9},{9,8},{10,11... | collective-permute-start | bytes 393224 | tf_op jit(solution)/shard_map/ppermute | solution.py:430
  20.9 2.2 %collective-permute-start = (bf16[256,768]{1,0:T(8,128)(2,1)S(1)}, bf16[256,768]{1,0:T(8,128)(2,1)S(1)}, u32[]{:S(2)}, u32[]{:S(2)}) collective-permute-start(bf16[256,768]{1,0:T(8,128)(2,1)S(1)} %get-tuple-element.32), channel_id=1, source_target_pairs={{0,1},{1,0},{2,3},{3,2},{4,5},{5,4},{6,7},{7,6},{8,9},{9,8},{10,11... | collective-permute-start | bytes 1179656 | tf_op jit(solution)/shard_map/ppermute | solution.py:436
  21.6 6.3 %collective-permute-start.2 = (bf16[256,256]{1,0:T(8,128)(2,1)S(1)}, bf16[256,256]{1,0:T(8,128)(2,1)S(1)}, u32[]{:S(2)}, u32[]{:S(2)}) collective-permute-start(bf16[256,256]{1,0:T(8,128)(2,1)S(1)} %shard_map.68.after_ref), channel_id=1, source_target_pairs={{0,2},{1,3},{2,0},{3,1},{4,6},{5,7},{6,4},{7,5},{8,10},{9,11},{10,... | collective-permute-start | bytes 393224 | tf_op jit(solution)/shard_map/ppermute | solution.py:440
  23.7 11.9 %collective-permute-start.5 = (bf16[256,768]{1,0:T(8,128)(2,1)S(1)}, bf16[256,768]{1,0:T(8,128)(2,1)S(1)}, u32[]{:S(2)}, u32[]{:S(2)}) collective-permute-start(bf16[256,768]{1,0:T(8,128)(2,1)S(1)} %shard_map.69.refs_0_), channel_id=1, source_target_pairs={{0,2},{1,3},{2,0},{3,1},{4,6},{5,7},{6,4},{7,5},{8,10},{9,11},{10,... | collective-permute-start | bytes 1179656 | tf_op jit(solution)/shard_map/ppermute | solution.py:440
  30.2 1.6 %collective-permute-start.3 = (bf16[256,512]{1,0:T(8,128)(2,1)S(1)}, bf16[256,512]{1,0:T(8,128)(2,1)S(1)}, u32[]{:S(2)}, u32[]{:S(2)}) collective-permute-start(bf16[256,512]{1,0:T(8,128)(2,1)S(1)} %get-tuple-element.35), channel_id=1, source_target_pairs={{0,1},{1,0},{2,3},{3,2},{4,5},{5,4},{6,7},{7,6},{8,9},{9,8},{10,11... | collective-permute-start | bytes 786440 | tf_op jit(solution)/shard_map/ppermute | solution.py:457
  30.2 1.9 %collective-permute-start.4 = (bf16[256,512]{1,0:T(8,128)(2,1)S(1)}, bf16[256,512]{1,0:T(8,128)(2,1)S(1)}, u32[]{:S(2)}, u32[]{:S(2)}) collective-permute-start(bf16[256,512]{1,0:T(8,128)(2,1)S(1)} %get-tuple-element.36), channel_id=1, source_target_pairs={{0,1},{1,0},{2,3},{3,2},{4,5},{5,4},{6,7},{7,6},{8,9},{9,8},{10,11... | collective-permute-start | bytes 786440 | tf_op jit(solution)/shard_map/ppermute | solution.py:457

commit v3 on v2

--- a/solution.py
+++ b/solution.py
@@ -40,10 +40,10 @@
     return residues * jnp.sqrt(2.0 * rates)
 
 
-def spread_table(tok, back):
+def spread_table(tok):
     run = tok // SUB
-    row = lax.broadcasted_iota(jnp.int32, (tok, tok), 1 if back else 0)
-    col = lax.broadcasted_iota(jnp.int32, (tok, tok), 0 if back else 1)
+    row = lax.broadcasted_iota(jnp.int32, (tok, tok), 0)
+    col = lax.broadcasted_iota(jnp.int32, (tok, tok), 1)
     return (col == row % SUB * run + row // SUB).astype(F32).astype(BF16)
 
 
@@ -75,7 +75,8 @@
 
 
 def group_order(count):
-    return sorted(range(count), key=lambda rank: (abs(2 * rank + 1 - count), -rank))
+    others = [rank for rank in range(count) if rank != count // 2]
+    return [count // 2] + sorted(others, key=lambda rank: (-abs(2 * rank + 1 - count), rank))
 
 
 def wait_all(copies):
@@ -124,8 +125,8 @@
 
 def local_kernel(
     values_hbm, rates_hbm, residues_hbm, skip_hbm, gate_hbm, weight_hbm,
-    near_ref, starts_ref, ahead_ref, rates_ref, spread_ref, first_weight, kept_weight,
-    values_ref, residues_ref, skip_ref, gate_ref, wide_ref, taps_ref, sems, weight_sems,
+    near_ref, reach_ref, decay_ref, far_ref, gate_ref, first_weight, kept_weight,
+    values_ref, rates_ref, residues_ref, skip_ref, wide_ref, taps_ref, sum_ref, order_ref, sems, weight_sems,
 ):
     tok, chan = values_ref.shape
     modes = rates_ref.shape[0]
@@ -147,10 +148,9 @@
     slots = range(1, lax.axis_size("tp") // 2)
     rest = column_copies(1, 0, slots, weight_hbm, first_weight, weight_sems.at[0])
     rest += column_copies(0, 0, slots, weight_hbm, kept_weight, weight_sems.at[1])
-    table = spread_table(tok, False)
+    table = spread_table(tok)
     wait_all(copies)
     wide_ref[...] = jnp.dot(table, values_ref[...], preferred_element_type=F32)
-    spread_ref[...] = jnp.dot(table, gate_ref[...], preferred_element_type=F32).astype(BF16)
 
     def step(index, carry):
         lanes = lanes_at(index)
@@ -185,7 +185,7 @@
                             rows = pl.ds((early + source) * SUB, SUB)
                             sums[target] = sums[target] + tap * wide_ref[rows, lanes]
             for target in range(SUB):
-                near_ref[pl.ds((at + target) * SUB, SUB), lanes] = sums[target]
+                sum_ref[pl.ds((at + target) * SUB, SUB), :] = sums[target]
 
         decay = jnp.exp(-rates)
         decay_run = jnp.exp(-float(run) * rates)
@@ -194,6 +194,7 @@
         for at in range(run):
             value = wide_ref[at * SUB : (at + 1) * SUB, lanes]
             held = [decays[mode] * held[mode] + value for mode in range(modes)]
+        terms = []
         for mode in range(modes):
             whole, power = held[mode], row_of(decay_run, mode)
             for shift in (1, 2, 4):
@@ -202,9 +203,18 @@
                 power = power * power
             before = jnp.where(place >= 1, pltpu.roll(whole, 1, 0), 0.0)
             first = row_of(gains, mode) * decays[mode]
+            terms.append(first * before)
             rows = slice(mode * SUB, (mode + 1) * SUB)
-            starts_ref[rows, lanes] = first * before
-        ahead_ref[:, lanes] = gains * decay
+            reach_ref[rows, lanes] = first * jnp.exp(-row_of(rates, mode) * ahead)
+        for at in range(run):
+            total = sum_ref[at * SUB : (at + 1) * SUB, :]
+            for mode in range(modes):
+                total = total + terms[mode]
+            terms = [terms[mode] * decays[mode] for mode in range(modes)]
+            order_ref[pl.ds(at, SUB, stride=run), :] = total
+        near_ref[:, lanes] = order_ref[...]
+        decay_ref[:, lanes] = jnp.exp(-float(SUB) * rates)
+        far_ref[:, lanes] = jnp.exp(-float(tok) * rates)
         return carry
 
     lax.fori_loop(0, chan // LANE, step, 0)
@@ -212,27 +222,23 @@
 
 
 def gate_kernel(
-    states_ref, near_ref, starts_ref, ahead_ref, rates_ref, spread_ref, weight_ref, weight_hbm,
-    gated_ref, sent_ref, later_weight, last_weight, held_ref, state_ref, decay_ref, sems,
+    states_ref, near_ref, reach_ref, decay_ref, far_ref, gate_ref, weight_ref, weight_hbm,
+    gated_ref, sent_ref, later_weight, last_weight, state_ref, sems,
 ):
     slots = range(1, lax.axis_size("tp") // 2)
     begin = weight_ref.shape[1] // len(slots)
     rest = column_copies(1, begin, slots, weight_hbm, later_weight, sems.at[0])
     rest += column_copies(0, begin, slots, weight_hbm, last_weight, sems.at[1])
-    tok, chan = spread_ref.shape
+    tok, chan = gate_ref.shape
     shards, modes = states_ref.shape[:2]
-    run = tok // SUB
     place = lax.axis_index("seq")
-    rates = rates_ref[...]
-    decay_ref[...] = jnp.exp(-rates)
-    far = jnp.exp(-float(tok) * rates)
+    far = far_ref[...]
     before = jnp.zeros((modes, chan), F32)
     order = group_order(shards)
     for shard in range(shards - 1):
         passed = far * before + states_ref[order.index(shard)].astype(F32)
         before = jnp.where(shard < place, passed, before)
-    state_ref[...] = before * ahead_ref[...]
-    passed = (sublane() * run).astype(F32)
+    state_ref[...] = before
 
     def step(index, carry):
         lanes = lanes_at(index)
@@ -241,23 +247,21 @@
             rows, row = slice(mode * SUB, (mode + 1) * SUB), slice(mode, mode + 1)
             decays.append(jnp.broadcast_to(decay_ref[row, lanes], (SUB, LANE)))
             state = jnp.broadcast_to(state_ref[row, lanes], (SUB, LANE))
-            rate = jnp.broadcast_to(rates_ref[row, lanes], (SUB, LANE))
-            terms.append(starts_ref[rows, lanes] + state * jnp.exp(-rate * passed))
-        for at in range(0, run, 2):
+            terms.append(state * reach_ref[rows, lanes])
+        for at in range(0, tok, 2 * SUB):
             totals = []
-            for spot in (at, at + 1):
-                total = near_ref[spot * SUB : (spot + 1) * SUB, lanes]
+            for first in (at, at + SUB):
+                total = near_ref[first : first + SUB, lanes]
                 for mode in range(modes):
                     total = total + terms[mode]
                 terms = [terms[mode] * decays[mode] for mode in range(modes)]
                 totals.append(total)
-            rows = slice(at * SUB, (at + 2) * SUB)
-            gate = spread_ref[rows, lanes].astype(F32)
-            held_ref[rows, lanes] = (gate * jnp.concatenate(totals, axis=0)).astype(BF16)
+            rows = slice(at, at + 2 * SUB)
+            gate = gate_ref[rows, lanes].astype(F32)
+            gated_ref[rows, lanes] = (gate * jnp.concatenate(totals, axis=0)).astype(BF16)
         return carry
 
     lax.fori_loop(0, chan // LANE, step, 0)
-    project(spread_table(tok, True), held_ref, gated_ref)
     project(gated_ref, weight_ref, sent_ref)
     wait_all(rest)
 
@@ -402,10 +406,12 @@
         scratch=[
             here((tok, chan), BF16),
             here((modes, chan), F32),
+            here((modes, chan), F32),
             here((1, chan), F32),
-            here((tok, chan), BF16),
             here((tok, chan), F32),
             here((tok // SUB, LANE), F32),
+            here((tok, LANE), F32),
+            here((tok, LANE), F32),
             pltpu.SemaphoreType.DMA((len(sources),)),
             pltpu.SemaphoreType.DMA((2, away * ROW_CUTS)),
         ],
@@ -421,8 +427,6 @@
         ],
         states, *tables, first_weight, weight,
         scratch=[
-            here((tok, chan), BF16),
-            here((modes, chan), F32),
             here((modes, chan), F32),
             pltpu.SemaphoreType.DMA((2, away * ROW_CUTS)),
         ],
@@ -437,7 +441,7 @@
 
     def to_chips(going):
         return [
-            lax.ppermute(each, "tp", [(rank, (rank + 2 * hop) % tp) for rank in range(tp)])
+            lax.ppermute(each, "tp", [(rank, (rank + 2 * hop) % tp) for rank in reversed(range(tp))])
             for hop, each in enumerate(going, 1)
         ]
 

time: 36.7 us -> 36.3 us (0.989)
  waiting for transfers between devices: 7.74 us -> 6.05 us
  Pallas kernels: 16.7 us -> 17.9 us
    all_to_all x1, waiting for transfers between devices: 2.21 us -> 0.52 us  [body(): lax.all_to_all(wire, 'seq', split_axis=0, concat_axis=0, tiled=True, axis...]
    pallas_call x9, Pallas kernels: 16.7 us -> 17.9 us  [call(): pl.pallas_call(kernel, out_shape=outs, in_specs=specs, out_specs=[out_spe...]
  transfers between devices with their start and end apart: 7 -> 7, of which waited for: 6 -> 6; matrix products, arithmetic and copies ran while one was open for 0% -> 0% of each run, Pallas kernels for 29% -> 34%
where the time goes in v3:
time: 36.3 us; the launch traced here: 35.9 us
  Pallas kernels  17.9 us (49%)
  starting transfers between devices  11.9 us (33%)
  waiting for transfers between devices  6.05 us (17%)
    pallas_call x9, Pallas kernels, call(): pl.pallas_call(kernel, out_shape=outs, in_specs=specs, out_specs=[out_spe...  17.9 us
    all_to_all x1, starting transfers between devices, body(): lax.all_to_all(wire, 'seq', split_axis=0, concat_axis=0, tiled=True, axis...  7.82 us
    ppermute x2, waiting for transfers between devices, to_chips(): lax.ppermute(each, 'tp', [(rank, (rank + 2 * hop) % tp) for rank in rever...  4.07 us
    ppermute x2, starting transfers between devices, to_chips(): lax.ppermute(each, 'tp', [(rank, (rank + 2 * hop) % tp) for rank in rever...  2.86 us
    ppermute x2, waiting for transfers between devices, body(): halves = [lax.ppermute(each, 'tp', cores) for each in halves]  1.4 us
  transfers between devices with their start and end apart: 7, of which 6 were waited for; matrix products, arithmetic and copies ran while one was open for 0% of the time, Pallas kernels for 34%

profile of v3, /device:TPU:0, one launch (start us, length us, event | category | flops | bytes accessed | tf_op | source)
XLA Modules:
  0.0 35.9 jit_solution(1714762593907566572)
XLA Ops:
  0.0 3.1 %shard_map.64 = bf16[8,16,1024]{2,1,0:T(8,128)(2,1)} custom-call(bf16[256,1024]{1,0:T(8,128)(2,1)} %values_hbm.3, f32[16,1024]{1,0:T(8,128)} %rates_hbm.3), custom_call_target="tpu_custom_call" | custom-call | tf_op jit(solution)/shard_map/pallas_call | solution.py:355
  3.1 7.8 %all-to-all-start = ((bf16[8,16,1024]{2,1,0:T(8,128)(2,1)}), bf16[8,16,1024]{2,1,0:T(8,128)(2,1)S(1)}, u32[]{:S(2)}, u32[]{:S(2)}) async-start(bf16[8,16,1024]{2,1,0:T(8,128)(2,1)} %shard_map.64), calls=%async_computation | async-start | bytes 524288 | tf_op jit(solution)/shard_map/all_to_all | solution.py:387
  10.9 6.2 %shard_map.65 = (f32[256,1024]{1,0:T(8,128)S(1)}, f32[128,1024]{1,0:T(8,128)S(1)}, f32[16,1024]{1,0:T(8,128)S(1)}, f32[16,1024]{1,0:T(8,128)S(1)}, bf16[256,1024...) custom-call(bf16[256,1024]{1,0:T(8,128)(2,1)} %values_hbm.3, f32[16,1024]{1,0:T(8,128)} %rates_hbm.3, ...), custom_call_target="tpu_custom_call" | custom-call | tf_op jit(solution)/shard_map/pallas_call | solution.py:355
  17.2 0.5 %all-to-all-done.states_ref = bf16[8,16,1024]{2,1,0:T(8,128)(2,1)S(1)} async-done(((bf16[8,16,1024]{2,1,0:T(8,128)(2,1)}), bf16[8,16,1024]{2,1,0:T(8,128)(2,1)S(1)}, u32[]{:S(2)}, u32[]{:S(2)}) %all-to-all-start) | async-done | bytes 262176 | tf_op jit(solution)/shard_map/all_to_all | solution.py:387
  17.7 1.9 %shard_map.66 = (bf16[256,1024]{1,0:T(8,128)(2,1)S(1)}, bf16[256,256]{1,0:T(8,128)(2,1)S(1)}, bf16[1024,768]{1,0:T(8,128)(2,1)S(1)}, bf16[1024,768]{1,0:T(8,128)(2,1)S(1)}) custom-call(bf16[8,16,1024]{2,1,0:T(8,128)(2,1)S(1)} %all-to-all-done.states_ref, f32[256,1024]{1,0:T(8,128)S(1)} %get-tuple-element.22.near_ref, ...), custom_call_target="tpu_custom_call" | custom-call | tf_op jit(solution)/shard_map/pallas_call | solution.py:355
  19.6 0.1 collective-permute-start.1
  19.7 0.7 %shard_map.67 = (f32[256,256]{1,0:T(8,128)S(1)}, bf16[256,768]{1,0:T(8,128)(2,1)S(1)}) custom-call(bf16[256,1024]{1,0:T(8,128)(2,1)S(1)} %get-tuple-element.28.gated_ref, bf16[1024,256]{1,0:T(8,128)(2,1)S(1)} %get-tuple-element.30.kept_weight, bf16[1024,768]{1,0:T(8,128)(2,1)S(1)} %get-tuple-element.31.sent_weight), custom_call_target="tpu_custom_call" | custom-call | tf_op jit(solution)/shard_map/pallas_call | solution.py:355
  20.4 0.6 %collective-permute-start = (bf16[256,768]{1,0:T(8,128)(2,1)S(1)}, bf16[256,768]{1,0:T(8,128)(2,1)S(1)}, u32[]{:S(2)}, u32[]{:S(2)}) collective-permute-start(bf16[256,768]{1,0:T(8,128)(2,1)S(1)} %get-tuple-element.32), channel_id=1, source_target_pairs={{0,1},{1,0},{2,3},{3,2},{4,5},{5,4},{6,7},{7,6},{8,9},{9,8},{10,11... | collective-permute-start | bytes 1179656 | tf_op jit(solution)/shard_map/ppermute | solution.py:440
  21.0 0.1 collective-permute-done.1.moved_ref
  21.1 1.6 %collective-permute-start.2 = (bf16[256,256]{1,0:T(8,128)(2,1)S(1)}, bf16[256,256]{1,0:T(8,128)(2,1)S(1)}, u32[]{:S(2)}, u32[]{:S(2)}) collective-permute-start(bf16[256,256]{1,0:T(8,128)(2,1)S(1)} %shard_map.68.after_ref), channel_id=1, source_target_pairs={{3,1},{2,0},{1,3},{0,2},{7,5},{6,4},{5,7},{4,6},{11,9},{10,8},{9,1... | collective-permute-start | bytes 393224 | tf_op jit(solution)/shard_map/ppermute | solution.py:444
  22.7 0.0 collective-permute-done.moved_ref
  22.7 0.6 %shard_map.69.refs_0_ = bf16[256,768]{1,0:T(8,128)(2,1)S(1)} custom-call(bf16[256,1024]{1,0:T(8,128)(2,1)S(1)} %get-tuple-element.28.gated_ref, bf16[1024,768]{1,0:T(8,128)(2,1)S(1)} %get-tuple-element.29.weight_ref, bf16[256,768]{1,0:T(8,128)(2,1)S(1)} %collective-permute-done.moved_ref, bf16[256,256]{1,0:T(8,128)(2,1)S(1)} %shard_map.68.after_ref), custom_call_target="tpu_custom_call" | custom-call | tf_op jit(solution)/shard_map/pallas_call | solution.py:355
  23.2 1.3 %collective-permute-start.5 = (bf16[256,768]{1,0:T(8,128)(2,1)S(1)}, bf16[256,768]{1,0:T(8,128)(2,1)S(1)}, u32[]{:S(2)}, u32[]{:S(2)}) collective-permute-start(bf16[256,768]{1,0:T(8,128)(2,1)S(1)} %shard_map.69.refs_0_), channel_id=1, source_target_pairs={{3,1},{2,0},{1,3},{0,2},{7,5},{6,4},{5,7},{4,6},{11,9},{10,8},{9,1... | collective-permute-start | bytes 1179656 | tf_op jit(solution)/shard_map/ppermute | solution.py:444
  24.5 2.9 %collective-permute-done.2.refs_1_.refs_0_ = bf16[256,256]{1,0:T(8,128)(2,1)S(1)} collective-permute-done((bf16[256,256]{1,0:T(8,128)(2,1)S(1)}, bf16[256,256]{1,0:T(8,128)(2,1)S(1)}, u32[]{:S(2)}, u32[]{:S(2)}) %collective-permute-start.2) | collective-permute-done | bytes 131104 | tf_op jit(solution)/shard_map/ppermute | solution.py:444
  27.4 2.3 %shard_map.70 = (bf16[256,512]{1,0:T(8,128)(2,1)S(1)}, bf16[256,512]{1,0:T(8,128)(2,1)S(1)}) custom-call(bf16[256,1024]{1,0:T(8,128)(2,1)S(1)} %get-tuple-element.28.gated_ref, bf16[1024,4096]{1,0:T(8,128)(2,1)} %weight_hbm.7, bf16[256,768]{1,0:T(8,128)(2,1)S(1)} %shard_map.69.refs_0_, bf16[256,256]{1,0:T(8,128)(2,1)S(1)} %collective-permute-done.2.refs_1_.refs_0_), custom_call_target="tpu_custom_call" | custom-call | flops 8589934592 | tf_op jit(solution)/shard_map/pallas_call | solution.py:355
  29.7 0.1 collective-permute-start.3
  29.7 0.5 %collective-permute-start.4 = (bf16[256,512]{1,0:T(8,128)(2,1)S(1)}, bf16[256,512]{1,0:T(8,128)(2,1)S(1)}, u32[]{:S(2)}, u32[]{:S(2)}) collective-permute-start(bf16[256,512]{1,0:T(8,128)(2,1)S(1)} %get-tuple-element.36), channel_id=1, source_target_pairs={{0,1},{1,0},{2,3},{3,2},{4,5},{5,4},{6,7},{7,6},{8,9},{9,8},{10,11... | collective-permute-start | bytes 786440 | tf_op jit(solution)/shard_map/ppermute | solution.py:461
  30.2 1.0 %collective-permute-done.3.low_ref = bf16[256,512]{1,0:T(8,128)(2,1)S(1)} collective-permute-done((bf16[256,512]{1,0:T(8,128)(2,1)S(1)}, bf16[256,512]{1,0:T(8,128)(2,1)S(1)}, u32[]{:S(2)}, u32[]{:S(2)}) %collective-permute-start.3) | collective-permute-done | bytes 262176 | tf_op jit(solution)/shard_map/ppermute | solution.py:461
  31.3 0.4 %collective-permute-done.4.high_ref = bf16[256,512]{1,0:T(8,128)(2,1)S(1)} collective-permute-done((bf16[256,512]{1,0:T(8,128)(2,1)S(1)}, bf16[256,512]{1,0:T(8,128)(2,1)S(1)}, u32[]{:S(2)}, u32[]{:S(2)}) %collective-permute-start.4) | collective-permute-done | bytes 262176 | tf_op jit(solution)/shard_map/ppermute | solution.py:461
  31.6 2.3 %shard_map.71 = (bf16[256,256]{1,0:T(8,128)(2,1)S(1)}, f32[256,768]{1,0:T(8,128)S(1)}) custom-call(bf16[256,1024]{1,0:T(8,128)(2,1)S(1)} %get-tuple-element.28.gated_ref, bf16[1024,4096]{1,0:T(8,128)(2,1)} %weight_hbm.7, bf16[256,512]{1,0:T(8,128)(2,1)S(1)} %collective-permute-done.3.low_ref, bf16[256,512]{1,0:T(8,128)(2,1)S(1)} %collective-permute-done.4.high_ref, ...), custom_call_target="tpu_custom_call" | custom-call | tf_op jit(solution)/shard_map/pallas_call | solution.py:355
  33.9 1.2 %collective-permute-done.5.refs_0_ = bf16[256,768]{1,0:T(8,128)(2,1)S(1)} collective-permute-done((bf16[256,768]{1,0:T(8,128)(2,1)S(1)}, bf16[256,768]{1,0:T(8,128)(2,1)S(1)}, u32[]{:S(2)}, u32[]{:S(2)}) %collective-permute-start.5) | collective-permute-done | bytes 393248 | tf_op jit(solution)/shard_map/ppermute | solution.py:444
  35.1 0.8 %shard_map.72 = bf16[256,1024]{1,0:T(8,128)(2,1)} custom-call(bf16[256,256]{1,0:T(8,128)(2,1)S(1)} %get-tuple-element.37.first_ref, f32[256,768]{1,0:T(8,128)S(1)} %get-tuple-element.38.own_ref, bf16[256,768]{1,0:T(8,128)(2,1)S(1)} %collective-permute-done.5.refs_0_), custom_call_target="tpu_custom_call" | custom-call | tf_op jit(solution)/shard_map/pallas_call | solution.py:355
  (1 shorter events, 0.0 us)
Async XLA Ops:
  3.1 14.6 %all-to-all-start = ((bf16[8,16,1024]{2,1,0:T(8,128)(2,1)}), bf16[8,16,1024]{2,1,0:T(8,128)(2,1)S(1)}, u32[]{:S(2)}, u32[]{:S(2)}) async-start(bf16[8,16,1024]{2,1,0:T(8,128)(2,1)} %shard_map.64), calls=%async_computation | async-start | bytes 524288 | tf_op jit(solution)/shard_map/all_to_all | solution.py:387
  19.6 1.4 %collective-permute-start.1 = (bf16[256,256]{1,0:T(8,128)(2,1)S(1)}, bf16[256,256]{1,0:T(8,128)(2,1)S(1)}, u32[]{:S(2)}, u32[]{:S(2)}) collective-permute-start(bf16[256,256]{1,0:T(8,128)(2,1)S(1)} %get-tuple-element.34), channel_id=1, source_target_pairs={{0,1},{1,0},{2,3},{3,2},{4,5},{5,4},{6,7},{7,6},{8,9},{9,8},{10,11... | collective-permute-start | bytes 393224 | tf_op jit(solution)/shard_map/ppermute | solution.py:434
  20.4 2.2 %collective-permute-start = (bf16[256,768]{1,0:T(8,128)(2,1)S(1)}, bf16[256,768]{1,0:T(8,128)(2,1)S(1)}, u32[]{:S(2)}, u32[]{:S(2)}) collective-permute-start(bf16[256,768]{1,0:T(8,128)(2,1)S(1)} %get-tuple-element.32), channel_id=1, source_target_pairs={{0,1},{1,0},{2,3},{3,2},{4,5},{5,4},{6,7},{7,6},{8,9},{9,8},{10,11... | collective-permute-start | bytes 1179656 | tf_op jit(solution)/shard_map/ppermute | solution.py:440
  21.1 6.3 %collective-permute-start.2 = (bf16[256,256]{1,0:T(8,128)(2,1)S(1)}, bf16[256,256]{1,0:T(8,128)(2,1)S(1)}, u32[]{:S(2)}, u32[]{:S(2)}) collective-permute-start(bf16[256,256]{1,0:T(8,128)(2,1)S(1)} %shard_map.68.after_ref), channel_id=1, source_target_pairs={{3,1},{2,0},{1,3},{0,2},{7,5},{6,4},{5,7},{4,6},{11,9},{10,8},{9,1... | collective-permute-start | bytes 393224 | tf_op jit(solution)/shard_map/ppermute | solution.py:444
  23.2 11.9 %collective-permute-start.5 = (bf16[256,768]{1,0:T(8,128)(2,1)S(1)}, bf16[256,768]{1,0:T(8,128)(2,1)S(1)}, u32[]{:S(2)}, u32[]{:S(2)}) collective-permute-start(bf16[256,768]{1,0:T(8,128)(2,1)S(1)} %shard_map.69.refs_0_), channel_id=1, source_target_pairs={{3,1},{2,0},{1,3},{0,2},{7,5},{6,4},{5,7},{4,6},{11,9},{10,8},{9,1... | collective-permute-start | bytes 1179656 | tf_op jit(solution)/shard_map/ppermute | solution.py:444
  29.7 1.6 %collective-permute-start.3 = (bf16[256,512]{1,0:T(8,128)(2,1)S(1)}, bf16[256,512]{1,0:T(8,128)(2,1)S(1)}, u32[]{:S(2)}, u32[]{:S(2)}) collective-permute-start(bf16[256,512]{1,0:T(8,128)(2,1)S(1)} %get-tuple-element.35), channel_id=1, source_target_pairs={{0,1},{1,0},{2,3},{3,2},{4,5},{5,4},{6,7},{7,6},{8,9},{9,8},{10,11... | collective-permute-start | bytes 786440 | tf_op jit(solution)/shard_map/ppermute | solution.py:461
  29.7 1.9 %collective-permute-start.4 = (bf16[256,512]{1,0:T(8,128)(2,1)S(1)}, bf16[256,512]{1,0:T(8,128)(2,1)S(1)}, u32[]{:S(2)}, u32[]{:S(2)}) collective-permute-start(bf16[256,512]{1,0:T(8,128)(2,1)S(1)} %get-tuple-element.36), channel_id=1, source_target_pairs={{0,1},{1,0},{2,3},{3,2},{4,5},{5,4},{6,7},{7,6},{8,9},{9,8},{10,11... | collective-permute-start | bytes 786440 | tf_op jit(solution)/shard_map/ppermute | solution.py:461

commit v4 on v3

--- a/solution.py
+++ b/solution.py
@@ -126,7 +126,8 @@
 def local_kernel(
     values_hbm, rates_hbm, residues_hbm, skip_hbm, gate_hbm, weight_hbm,
     near_ref, reach_ref, decay_ref, far_ref, gate_ref, first_weight, kept_weight,
-    values_ref, rates_ref, residues_ref, skip_ref, wide_ref, taps_ref, sum_ref, order_ref, sems, weight_sems,
+    values_ref, rates_ref, residues_ref, skip_ref, wide_ref, taps_ref, first_ref, snap_ref,
+    order_ref, sems, weight_sems,
 ):
     tok, chan = values_ref.shape
     modes = rates_ref.shape[0]
@@ -136,10 +137,10 @@
         for at, (source, target) in enumerate(
             (
                 (values_hbm, values_ref),
-                (gate_hbm, gate_ref),
                 (rates_hbm, rates_ref),
                 (residues_hbm, residues_ref),
                 (skip_hbm, skip_ref),
+                (gate_hbm, gate_ref),
             )
         )
     ]
@@ -148,6 +149,7 @@
     slots = range(1, lax.axis_size("tp") // 2)
     rest = column_copies(1, 0, slots, weight_hbm, first_weight, weight_sems.at[0])
     rest += column_copies(0, 0, slots, weight_hbm, kept_weight, weight_sems.at[1])
+    rest.append(copies.pop())
     table = spread_table(tok)
     wait_all(copies)
     wide_ref[...] = jnp.dot(table, values_ref[...], preferred_element_type=F32)
@@ -159,42 +161,25 @@
         gains = gains_of(residues_ref[:, lanes], rates)
 
         ahead = place.astype(F32)
-        decay = jnp.exp(-float(SUB) * rates)
-        terms = [
-            row_of(gains, mode) * jnp.exp(-row_of(rates, mode) * ahead) for mode in range(modes)
-        ]
-        for at in range(0, run, SUB):
-            total = terms[0]
-            for mode in range(1, modes):
-                total = total + terms[mode]
-            if at == 0:
-                total = jnp.where(place == 0, total + skip_ref[:, lanes], total)
-            terms = [terms[mode] * row_of(decay, mode) for mode in range(modes)]
-            taps_ref[at : at + SUB, :] = total
-
-        for at in range(0, run, SUB):
-            sums = [jnp.zeros((SUB, LANE), F32)] * SUB
-            for early in range(0, at + SUB, SUB):
-                for lag in range(at - early - SUB + 1, at - early + SUB):
-                    if lag < 0:
-                        continue
-                    tap = jnp.broadcast_to(taps_ref[lag : lag + 1, :], (SUB, LANE))
-                    for source in range(SUB):
-                        target = early + source + lag - at
-                        if 0 <= target < SUB:
-                            rows = pl.ds((early + source) * SUB, SUB)
-                            sums[target] = sums[target] + tap * wide_ref[rows, lanes]
-            for target in range(SUB):
-                sum_ref[pl.ds((at + target) * SUB, SUB), :] = sums[target]
-
-        decay = jnp.exp(-rates)
+        decay, decay_block = jnp.exp(-rates), jnp.exp(-float(SUB) * rates)
         decay_run = jnp.exp(-float(run) * rates)
         decays = [row_of(decay, mode) for mode in range(modes)]
+        taps = jnp.where(place == 0, skip_ref[:, lanes], 0.0)
+        for mode in range(modes):
+            gain = row_of(gains, mode)
+            term = gain * jnp.exp(-row_of(rates, mode) * ahead)
+            taps = taps + term
+            first_ref[mode * SUB : (mode + 1) * SUB, :] = gain * decays[mode]
+            reach_ref[mode * SUB : (mode + 1) * SUB, lanes] = term * decays[mode]
+        taps_ref[...] = taps
+
         held = [jnp.zeros((SUB, LANE), F32)] * modes
         for at in range(run):
+            if at % SUB == 0:
+                for mode in range(modes):
+                    snap_ref[at // SUB, mode * SUB : (mode + 1) * SUB, :] = held[mode]
             value = wide_ref[at * SUB : (at + 1) * SUB, lanes]
             held = [decays[mode] * held[mode] + value for mode in range(modes)]
-        terms = []
         for mode in range(modes):
             whole, power = held[mode], row_of(decay_run, mode)
             for shift in (1, 2, 4):
@@ -202,16 +187,31 @@
                 whole = whole + power * moved
                 power = power * power
             before = jnp.where(place >= 1, pltpu.roll(whole, 1, 0), 0.0)
-            first = row_of(gains, mode) * decays[mode]
-            terms.append(first * before)
             rows = slice(mode * SUB, (mode + 1) * SUB)
-            reach_ref[rows, lanes] = first * jnp.exp(-row_of(rates, mode) * ahead)
-        for at in range(run):
-            total = sum_ref[at * SUB : (at + 1) * SUB, :]
-            for mode in range(modes):
-                total = total + terms[mode]
-            terms = [terms[mode] * decays[mode] for mode in range(modes)]
-            order_ref[pl.ds(at, SUB, stride=run), :] = total
+            fade = row_of(decay_block, mode)
+            for block in range(run // SUB):
+                snap_ref[block, rows, :] = first_ref[rows, :] * (snap_ref[block, rows, :] + before)
+                before = fade * before
+
+        for block in range(run // SUB):
+            values = [
+                wide_ref[(block * SUB + at) * SUB : (block * SUB + at + 1) * SUB, lanes]
+                for at in range(SUB)
+            ]
+            sums = [jnp.zeros((SUB, LANE), F32)] * SUB
+            for lag in range(SUB):
+                tap = jnp.broadcast_to(taps_ref[lag : lag + 1, :], (SUB, LANE))
+                for at in range(lag, SUB):
+                    sums[at] = sums[at] + tap * values[at - lag]
+            terms = [
+                snap_ref[block, mode * SUB : (mode + 1) * SUB, :] for mode in range(modes)
+            ]
+            for at in range(SUB):
+                total = sums[at]
+                for mode in range(modes):
+                    total = total + terms[mode]
+                terms = [terms[mode] * decays[mode] for mode in range(modes)]
+                order_ref[pl.ds(block * SUB + at, SUB, stride=run), :] = total
         near_ref[:, lanes] = order_ref[...]
         decay_ref[:, lanes] = jnp.exp(-float(SUB) * rates)
         far_ref[:, lanes] = jnp.exp(-float(tok) * rates)
@@ -409,8 +409,9 @@
             here((modes, chan), F32),
             here((1, chan), F32),
             here((tok, chan), F32),
-            here((tok // SUB, LANE), F32),
-            here((tok, LANE), F32),
+            here((SUB, LANE), F32),
+            here((modes * SUB, LANE), F32),
+            here((tok // SUB // SUB, modes * SUB, LANE), F32),
             here((tok, LANE), F32),
             pltpu.SemaphoreType.DMA((len(sources),)),
             pltpu.SemaphoreType.DMA((2, away * ROW_CUTS)),

time: 36.3 us -> 36.2 us (level)
  waiting for transfers between devices: 6.05 us -> 7.28 us
  Pallas kernels: 17.9 us -> 16.7 us
    all_to_all x1, waiting for transfers between devices: 0.52 us -> 1.75 us  [body(): lax.all_to_all(wire, 'seq', split_axis=0, concat_axis=0, tiled=True, axis...]
    pallas_call x9, Pallas kernels: 17.9 us -> 16.7 us  [call(): pl.pallas_call(kernel, out_shape=outs, in_specs=specs, out_specs=[out_spe...]
  transfers between devices with their start and end apart: 7 -> 7, of which waited for: 6 -> 6; matrix products, arithmetic and copies ran while one was open for 0% -> 0% of each run, Pallas kernels for 34% -> 30%
where the time goes in v4:
time: 36.2 us; the launch traced here: 35.9 us
  Pallas kernels  16.7 us (46%)
  starting transfers between devices  11.9 us (33%)
  waiting for transfers between devices  7.28 us (20%)
    pallas_call x9, Pallas kernels, call(): pl.pallas_call(kernel, out_shape=outs, in_specs=specs, out_specs=[out_spe...  16.7 us
    all_to_all x1, starting transfers between devices, body(): lax.all_to_all(wire, 'seq', split_axis=0, concat_axis=0, tiled=True, axis...  7.82 us
    ppermute x2, waiting for transfers between devices, to_chips(): lax.ppermute(each, 'tp', [(rank, (rank + 2 * hop) % tp) for rank in rever...  4.07 us
    ppermute x2, starting transfers between devices, to_chips(): lax.ppermute(each, 'tp', [(rank, (rank + 2 * hop) % tp) for rank in rever...  2.86 us
    all_to_all x1, waiting for transfers between devices, body(): lax.all_to_all(wire, 'seq', split_axis=0, concat_axis=0, tiled=True, axis...  1.75 us
    ppermute x2, waiting for transfers between devices, body(): halves = [lax.ppermute(each, 'tp', cores) for each in halves]  1.4 us
  transfers between devices with their start and end apart: 7, of which 6 were waited for; matrix products, arithmetic and copies ran while one was open for 0% of the time, Pallas kernels for 30%

profile of v4, /device:TPU:0, one launch (start us, length us, event | category | flops | bytes accessed | tf_op | source)
XLA Modules:
  0.0 35.9 jit_solution(8836496153080899161)
XLA Ops:
  0.0 3.1 %shard_map.64 = bf16[8,16,1024]{2,1,0:T(8,128)(2,1)} custom-call(bf16[256,1024]{1,0:T(8,128)(2,1)} %values_hbm.3, f32[16,1024]{1,0:T(8,128)} %rates_hbm.3), custom_call_target="tpu_custom_call" | custom-call | tf_op jit(solution)/shard_map/pallas_call | solution.py:355
  3.1 7.8 %all-to-all-start = ((bf16[8,16,1024]{2,1,0:T(8,128)(2,1)}), bf16[8,16,1024]{2,1,0:T(8,128)(2,1)S(1)}, u32[]{:S(2)}, u32[]{:S(2)}) async-start(bf16[8,16,1024]{2,1,0:T(8,128)(2,1)} %shard_map.64), calls=%async_computation | async-start | bytes 524288 | tf_op jit(solution)/shard_map/all_to_all | solution.py:387
  10.9 5.0 %shard_map.65 = (f32[256,1024]{1,0:T(8,128)S(1)}, f32[128,1024]{1,0:T(8,128)S(1)}, f32[16,1024]{1,0:T(8,128)S(1)}, f32[16,1024]{1,0:T(8,128)S(1)}, bf16[256,1024...) custom-call(bf16[256,1024]{1,0:T(8,128)(2,1)} %values_hbm.3, f32[16,1024]{1,0:T(8,128)} %rates_hbm.3, ...), custom_call_target="tpu_custom_call" | custom-call | tf_op jit(solution)/shard_map/pallas_call | solution.py:355
  15.9 1.8 %all-to-all-done.states_ref = bf16[8,16,1024]{2,1,0:T(8,128)(2,1)S(1)} async-done(((bf16[8,16,1024]{2,1,0:T(8,128)(2,1)}), bf16[8,16,1024]{2,1,0:T(8,128)(2,1)S(1)}, u32[]{:S(2)}, u32[]{:S(2)}) %all-to-all-start) | async-done | bytes 262176 | tf_op jit(solution)/shard_map/all_to_all | solution.py:387
  17.7 1.9 %shard_map.66 = (bf16[256,1024]{1,0:T(8,128)(2,1)S(1)}, bf16[256,256]{1,0:T(8,128)(2,1)S(1)}, bf16[1024,768]{1,0:T(8,128)(2,1)S(1)}, bf16[1024,768]{1,0:T(8,128)(2,1)S(1)}) custom-call(bf16[8,16,1024]{2,1,0:T(8,128)(2,1)S(1)} %all-to-all-done.states_ref, f32[256,1024]{1,0:T(8,128)S(1)} %get-tuple-element.22.near_ref, ...), custom_call_target="tpu_custom_call" | custom-call | tf_op jit(solution)/shard_map/pallas_call | solution.py:355
  19.6 0.1 collective-permute-start.1
  19.7 0.7 %shard_map.67 = (f32[256,256]{1,0:T(8,128)S(1)}, bf16[256,768]{1,0:T(8,128)(2,1)S(1)}) custom-call(bf16[256,1024]{1,0:T(8,128)(2,1)S(1)} %get-tuple-element.28.gated_ref, bf16[1024,256]{1,0:T(8,128)(2,1)S(1)} %get-tuple-element.30.kept_weight, bf16[1024,768]{1,0:T(8,128)(2,1)S(1)} %get-tuple-element.31.sent_weight), custom_call_target="tpu_custom_call" | custom-call | tf_op jit(solution)/shard_map/pallas_call | solution.py:355
  20.4 0.6 %collective-permute-start = (bf16[256,768]{1,0:T(8,128)(2,1)S(1)}, bf16[256,768]{1,0:T(8,128)(2,1)S(1)}, u32[]{:S(2)}, u32[]{:S(2)}) collective-permute-start(bf16[256,768]{1,0:T(8,128)(2,1)S(1)} %get-tuple-element.32), channel_id=1, source_target_pairs={{0,1},{1,0},{2,3},{3,2},{4,5},{5,4},{6,7},{7,6},{8,9},{9,8},{10,11... | collective-permute-start | bytes 1179656 | tf_op jit(solution)/shard_map/ppermute | solution.py:441
  21.0 0.1 collective-permute-done.1.moved_ref
  21.1 1.6 %collective-permute-start.2 = (bf16[256,256]{1,0:T(8,128)(2,1)S(1)}, bf16[256,256]{1,0:T(8,128)(2,1)S(1)}, u32[]{:S(2)}, u32[]{:S(2)}) collective-permute-start(bf16[256,256]{1,0:T(8,128)(2,1)S(1)} %shard_map.68.after_ref), channel_id=1, source_target_pairs={{3,1},{2,0},{1,3},{0,2},{7,5},{6,4},{5,7},{4,6},{11,9},{10,8},{9,1... | collective-permute-start | bytes 393224 | tf_op jit(solution)/shard_map/ppermute | solution.py:445
  22.7 0.0 collective-permute-done.moved_ref
  22.7 0.6 %shard_map.69.refs_0_ = bf16[256,768]{1,0:T(8,128)(2,1)S(1)} custom-call(bf16[256,1024]{1,0:T(8,128)(2,1)S(1)} %get-tuple-element.28.gated_ref, bf16[1024,768]{1,0:T(8,128)(2,1)S(1)} %get-tuple-element.29.weight_ref, bf16[256,768]{1,0:T(8,128)(2,1)S(1)} %collective-permute-done.moved_ref, bf16[256,256]{1,0:T(8,128)(2,1)S(1)} %shard_map.68.after_ref), custom_call_target="tpu_custom_call" | custom-call | tf_op jit(solution)/shard_map/pallas_call | solution.py:355
  23.2 1.3 %collective-permute-start.5 = (bf16[256,768]{1,0:T(8,128)(2,1)S(1)}, bf16[256,768]{1,0:T(8,128)(2,1)S(1)}, u32[]{:S(2)}, u32[]{:S(2)}) collective-permute-start(bf16[256,768]{1,0:T(8,128)(2,1)S(1)} %shard_map.69.refs_0_), channel_id=1, source_target_pairs={{3,1},{2,0},{1,3},{0,2},{7,5},{6,4},{5,7},{4,6},{11,9},{10,8},{9,1... | collective-permute-start | bytes 1179656 | tf_op jit(solution)/shard_map/ppermute | solution.py:445
  24.5 2.9 %collective-permute-done.2.refs_1_.refs_0_ = bf16[256,256]{1,0:T(8,128)(2,1)S(1)} collective-permute-done((bf16[256,256]{1,0:T(8,128)(2,1)S(1)}, bf16[256,256]{1,0:T(8,128)(2,1)S(1)}, u32[]{:S(2)}, u32[]{:S(2)}) %collective-permute-start.2) | collective-permute-done | bytes 131104 | tf_op jit(solution)/shard_map/ppermute | solution.py:445
  27.4 2.3 %shard_map.70 = (bf16[256,512]{1,0:T(8,128)(2,1)S(1)}, bf16[256,512]{1,0:T(8,128)(2,1)S(1)}) custom-call(bf16[256,1024]{1,0:T(8,128)(2,1)S(1)} %get-tuple-element.28.gated_ref, bf16[1024,4096]{1,0:T(8,128)(2,1)} %weight_hbm.7, bf16[256,768]{1,0:T(8,128)(2,1)S(1)} %shard_map.69.refs_0_, bf16[256,256]{1,0:T(8,128)(2,1)S(1)} %collective-permute-done.2.refs_1_.refs_0_), custom_call_target="tpu_custom_call" | custom-call | flops 8589934592 | tf_op jit(solution)/shard_map/pallas_call | solution.py:355
  29.7 0.1 collective-permute-start.3
  29.7 0.5 %collective-permute-start.4 = (bf16[256,512]{1,0:T(8,128)(2,1)S(1)}, bf16[256,512]{1,0:T(8,128)(2,1)S(1)}, u32[]{:S(2)}, u32[]{:S(2)}) collective-permute-start(bf16[256,512]{1,0:T(8,128)(2,1)S(1)} %get-tuple-element.36), channel_id=1, source_target_pairs={{0,1},{1,0},{2,3},{3,2},{4,5},{5,4},{6,7},{7,6},{8,9},{9,8},{10,11... | collective-permute-start | bytes 786440 | tf_op jit(solution)/shard_map/ppermute | solution.py:462
  30.2 1.0 %collective-permute-done.3.low_ref = bf16[256,512]{1,0:T(8,128)(2,1)S(1)} collective-permute-done((bf16[256,512]{1,0:T(8,128)(2,1)S(1)}, bf16[256,512]{1,0:T(8,128)(2,1)S(1)}, u32[]{:S(2)}, u32[]{:S(2)}) %collective-permute-start.3) | collective-permute-done | bytes 262176 | tf_op jit(solution)/shard_map/ppermute | solution.py:462
  31.3 0.4 %collective-permute-done.4.high_ref = bf16[256,512]{1,0:T(8,128)(2,1)S(1)} collective-permute-done((bf16[256,512]{1,0:T(8,128)(2,1)S(1)}, bf16[256,512]{1,0:T(8,128)(2,1)S(1)}, u32[]{:S(2)}, u32[]{:S(2)}) %collective-permute-start.4) | collective-permute-done | bytes 262176 | tf_op jit(solution)/shard_map/ppermute | solution.py:462
  31.6 2.3 %shard_map.71 = (bf16[256,256]{1,0:T(8,128)(2,1)S(1)}, f32[256,768]{1,0:T(8,128)S(1)}) custom-call(bf16[256,1024]{1,0:T(8,128)(2,1)S(1)} %get-tuple-element.28.gated_ref, bf16[1024,4096]{1,0:T(8,128)(2,1)} %weight_hbm.7, bf16[256,512]{1,0:T(8,128)(2,1)S(1)} %collective-permute-done.3.low_ref, bf16[256,512]{1,0:T(8,128)(2,1)S(1)} %collective-permute-done.4.high_ref, ...), custom_call_target="tpu_custom_call" | custom-call | tf_op jit(solution)/shard_map/pallas_call | solution.py:355
  33.9 1.2 %collective-permute-done.5.refs_0_ = bf16[256,768]{1,0:T(8,128)(2,1)S(1)} collective-permute-done((bf16[256,768]{1,0:T(8,128)(2,1)S(1)}, bf16[256,768]{1,0:T(8,128)(2,1)S(1)}, u32[]{:S(2)}, u32[]{:S(2)}) %collective-permute-start.5) | collective-permute-done | bytes 393248 | tf_op jit(solution)/shard_map/ppermute | solution.py:445
  35.1 0.8 %shard_map.72 = bf16[256,1024]{1,0:T(8,128)(2,1)} custom-call(bf16[256,256]{1,0:T(8,128)(2,1)S(1)} %get-tuple-element.37.first_ref, f32[256,768]{1,0:T(8,128)S(1)} %get-tuple-element.38.own_ref, bf16[256,768]{1,0:T(8,128)(2,1)S(1)} %collective-permute-done.5.refs_0_), custom_call_target="tpu_custom_call" | custom-call | tf_op jit(solution)/shard_map/pallas_call | solution.py:355
  (1 shorter events, 0.0 us)
Async XLA Ops:
  3.1 14.6 %all-to-all-start = ((bf16[8,16,1024]{2,1,0:T(8,128)(2,1)}), bf16[8,16,1024]{2,1,0:T(8,128)(2,1)S(1)}, u32[]{:S(2)}, u32[]{:S(2)}) async-start(bf16[8,16,1024]{2,1,0:T(8,128)(2,1)} %shard_map.64), calls=%async_computation | async-start | bytes 524288 | tf_op jit(solution)/shard_map/all_to_all | solution.py:387
  19.6 1.4 %collective-permute-start.1 = (bf16[256,256]{1,0:T(8,128)(2,1)S(1)}, bf16[256,256]{1,0:T(8,128)(2,1)S(1)}, u32[]{:S(2)}, u32[]{:S(2)}) collective-permute-start(bf16[256,256]{1,0:T(8,128)(2,1)S(1)} %get-tuple-element.34), channel_id=1, source_target_pairs={{0,1},{1,0},{2,3},{3,2},{4,5},{5,4},{6,7},{7,6},{8,9},{9,8},{10,11... | collective-permute-start | bytes 393224 | tf_op jit(solution)/shard_map/ppermute | solution.py:435
  20.4 2.2 %collective-permute-start = (bf16[256,768]{1,0:T(8,128)(2,1)S(1)}, bf16[256,768]{1,0:T(8,128)(2,1)S(1)}, u32[]{:S(2)}, u32[]{:S(2)}) collective-permute-start(bf16[256,768]{1,0:T(8,128)(2,1)S(1)} %get-tuple-element.32), channel_id=1, source_target_pairs={{0,1},{1,0},{2,3},{3,2},{4,5},{5,4},{6,7},{7,6},{8,9},{9,8},{10,11... | collective-permute-start | bytes 1179656 | tf_op jit(solution)/shard_map/ppermute | solution.py:441
  21.1 6.3 %collective-permute-start.2 = (bf16[256,256]{1,0:T(8,128)(2,1)S(1)}, bf16[256,256]{1,0:T(8,128)(2,1)S(1)}, u32[]{:S(2)}, u32[]{:S(2)}) collective-permute-start(bf16[256,256]{1,0:T(8,128)(2,1)S(1)} %shard_map.68.after_ref), channel_id=1, source_target_pairs={{3,1},{2,0},{1,3},{0,2},{7,5},{6,4},{5,7},{4,6},{11,9},{10,8},{9,1... | collective-permute-start | bytes 393224 | tf_op jit(solution)/shard_map/ppermute | solution.py:445
  23.2 11.9 %collective-permute-start.5 = (bf16[256,768]{1,0:T(8,128)(2,1)S(1)}, bf16[256,768]{1,0:T(8,128)(2,1)S(1)}, u32[]{:S(2)}, u32[]{:S(2)}) collective-permute-start(bf16[256,768]{1,0:T(8,128)(2,1)S(1)} %shard_map.69.refs_0_), channel_id=1, source_target_pairs={{3,1},{2,0},{1,3},{0,2},{7,5},{6,4},{5,7},{4,6},{11,9},{10,8},{9,1... | collective-permute-start | bytes 1179656 | tf_op jit(solution)/shard_map/ppermute | solution.py:445
  29.7 1.6 %collective-permute-start.3 = (bf16[256,512]{1,0:T(8,128)(2,1)S(1)}, bf16[256,512]{1,0:T(8,128)(2,1)S(1)}, u32[]{:S(2)}, u32[]{:S(2)}) collective-permute-start(bf16[256,512]{1,0:T(8,128)(2,1)S(1)} %get-tuple-element.35), channel_id=1, source_target_pairs={{0,1},{1,0},{2,3},{3,2},{4,5},{5,4},{6,7},{7,6},{8,9},{9,8},{10,11... | collective-permute-start | bytes 786440 | tf_op jit(solution)/shard_map/ppermute | solution.py:462
  29.7 1.9 %collective-permute-start.4 = (bf16[256,512]{1,0:T(8,128)(2,1)S(1)}, bf16[256,512]{1,0:T(8,128)(2,1)S(1)}, u32[]{:S(2)}, u32[]{:S(2)}) collective-permute-start(bf16[256,512]{1,0:T(8,128)(2,1)S(1)} %get-tuple-element.36), channel_id=1, source_target_pairs={{0,1},{1,0},{2,3},{3,2},{4,5},{5,4},{6,7},{7,6},{8,9},{9,8},{10,11... | collective-permute-start | bytes 786440 | tf_op jit(solution)/shard_map/ppermute | solution.py:462

commit v5 on v4

--- a/solution.py
+++ b/solution.py
@@ -75,8 +75,7 @@
 
 
 def group_order(count):
-    others = [rank for rank in range(count) if rank != count // 2]
-    return [count // 2] + sorted(others, key=lambda rank: (-abs(2 * rank + 1 - count), rank))
+    return [(count // 2 + at) % count for at in range(count)]
 
 
 def wait_all(copies):

time: 36.2 us -> 36.1 us (level)
  no operation moved by 1% of the time
where the time goes in v5:
time: 36.1 us; the launch traced here: 35.7 us
  Pallas kernels  16.7 us (46%)
  starting transfers between devices  11.9 us (33%)
  waiting for transfers between devices  7.09 us (20%)
    pallas_call x9, Pallas kernels, call(): pl.pallas_call(kernel, out_shape=outs, in_specs=specs, out_specs=[out_spe...  16.7 us
    all_to_all x1, starting transfers between devices, body(): lax.all_to_all(wire, 'seq', split_axis=0, concat_axis=0, tiled=True, axis...  7.83 us
    ppermute x2, waiting for transfers between devices, to_chips(): lax.ppermute(each, 'tp', [(rank, (rank + 2 * hop) % tp) for rank in rever...  4.07 us
    ppermute x2, starting transfers between devices, to_chips(): lax.ppermute(each, 'tp', [(rank, (rank + 2 * hop) % tp) for rank in rever...  2.86 us
    all_to_all x1, waiting for transfers between devices, body(): lax.all_to_all(wire, 'seq', split_axis=0, concat_axis=0, tiled=True, axis...  1.55 us
    ppermute x2, waiting for transfers between devices, body(): halves = [lax.ppermute(each, 'tp', cores) for each in halves]  1.4 us
  transfers between devices with their start and end apart: 7, of which 6 were waited for; matrix products, arithmetic and copies ran while one was open for 0% of the time, Pallas kernels for 30%

profile of v5, /device:TPU:0, one launch (start us, length us, event | category | flops | bytes accessed | tf_op | source)
XLA Modules:
  0.0 35.7 jit_solution(2371254904224045621)
XLA Ops:
  0.0 3.1 %shard_map.64 = bf16[8,16,1024]{2,1,0:T(8,128)(2,1)} custom-call(bf16[256,1024]{1,0:T(8,128)(2,1)} %values_hbm.3, f32[16,1024]{1,0:T(8,128)} %rates_hbm.3), custom_call_target="tpu_custom_call" | custom-call | tf_op jit(solution)/shard_map/pallas_call | solution.py:354
  3.1 7.8 %all-to-all-start = ((bf16[8,16,1024]{2,1,0:T(8,128)(2,1)}), bf16[8,16,1024]{2,1,0:T(8,128)(2,1)S(1)}, u32[]{:S(2)}, u32[]{:S(2)}) async-start(bf16[8,16,1024]{2,1,0:T(8,128)(2,1)} %shard_map.64), calls=%async_computation | async-start | bytes 524288 | tf_op jit(solution)/shard_map/all_to_all | solution.py:386
  10.9 5.0 %shard_map.65 = (f32[256,1024]{1,0:T(8,128)S(1)}, f32[128,1024]{1,0:T(8,128)S(1)}, f32[16,1024]{1,0:T(8,128)S(1)}, f32[16,1024]{1,0:T(8,128)S(1)}, bf16[256,1024...) custom-call(bf16[256,1024]{1,0:T(8,128)(2,1)} %values_hbm.3, f32[16,1024]{1,0:T(8,128)} %rates_hbm.3, ...), custom_call_target="tpu_custom_call" | custom-call | tf_op jit(solution)/shard_map/pallas_call | solution.py:354
  15.9 1.6 %all-to-all-done.states_ref = bf16[8,16,1024]{2,1,0:T(8,128)(2,1)S(1)} async-done(((bf16[8,16,1024]{2,1,0:T(8,128)(2,1)}), bf16[8,16,1024]{2,1,0:T(8,128)(2,1)S(1)}, u32[]{:S(2)}, u32[]{:S(2)}) %all-to-all-start) | async-done | bytes 262176 | tf_op jit(solution)/shard_map/all_to_all | solution.py:386
  17.5 1.9 %shard_map.66 = (bf16[256,1024]{1,0:T(8,128)(2,1)S(1)}, bf16[256,256]{1,0:T(8,128)(2,1)S(1)}, bf16[1024,768]{1,0:T(8,128)(2,1)S(1)}, bf16[1024,768]{1,0:T(8,128)(2,1)S(1)}) custom-call(bf16[8,16,1024]{2,1,0:T(8,128)(2,1)S(1)} %all-to-all-done.states_ref, f32[256,1024]{1,0:T(8,128)S(1)} %get-tuple-element.22.near_ref, ...), custom_call_target="tpu_custom_call" | custom-call | tf_op jit(solution)/shard_map/pallas_call | solution.py:354
  19.4 0.1 collective-permute-start.1
  19.5 0.7 %shard_map.67 = (f32[256,256]{1,0:T(8,128)S(1)}, bf16[256,768]{1,0:T(8,128)(2,1)S(1)}) custom-call(bf16[256,1024]{1,0:T(8,128)(2,1)S(1)} %get-tuple-element.28.gated_ref, bf16[1024,256]{1,0:T(8,128)(2,1)S(1)} %get-tuple-element.30.kept_weight, bf16[1024,768]{1,0:T(8,128)(2,1)S(1)} %get-tuple-element.31.sent_weight), custom_call_target="tpu_custom_call" | custom-call | tf_op jit(solution)/shard_map/pallas_call | solution.py:354
  20.2 0.6 %collective-permute-start = (bf16[256,768]{1,0:T(8,128)(2,1)S(1)}, bf16[256,768]{1,0:T(8,128)(2,1)S(1)}, u32[]{:S(2)}, u32[]{:S(2)}) collective-permute-start(bf16[256,768]{1,0:T(8,128)(2,1)S(1)} %get-tuple-element.32), channel_id=1, source_target_pairs={{0,1},{1,0},{2,3},{3,2},{4,5},{5,4},{6,7},{7,6},{8,9},{9,8},{10,11... | collective-permute-start | bytes 1179656 | tf_op jit(solution)/shard_map/ppermute | solution.py:440
  20.8 0.1 collective-permute-done.1.moved_ref
  20.9 1.6 %collective-permute-start.2 = (bf16[256,256]{1,0:T(8,128)(2,1)S(1)}, bf16[256,256]{1,0:T(8,128)(2,1)S(1)}, u32[]{:S(2)}, u32[]{:S(2)}) collective-permute-start(bf16[256,256]{1,0:T(8,128)(2,1)S(1)} %shard_map.68.after_ref), channel_id=1, source_target_pairs={{3,1},{2,0},{1,3},{0,2},{7,5},{6,4},{5,7},{4,6},{11,9},{10,8},{9,1... | collective-permute-start | bytes 393224 | tf_op jit(solution)/shard_map/ppermute | solution.py:444
  22.5 0.0 collective-permute-done.moved_ref
  22.5 0.6 %shard_map.69.refs_0_ = bf16[256,768]{1,0:T(8,128)(2,1)S(1)} custom-call(bf16[256,1024]{1,0:T(8,128)(2,1)S(1)} %get-tuple-element.28.gated_ref, bf16[1024,768]{1,0:T(8,128)(2,1)S(1)} %get-tuple-element.29.weight_ref, bf16[256,768]{1,0:T(8,128)(2,1)S(1)} %collective-permute-done.moved_ref, bf16[256,256]{1,0:T(8,128)(2,1)S(1)} %shard_map.68.after_ref), custom_call_target="tpu_custom_call" | custom-call | tf_op jit(solution)/shard_map/pallas_call | solution.py:354
  23.0 1.3 %collective-permute-start.5 = (bf16[256,768]{1,0:T(8,128)(2,1)S(1)}, bf16[256,768]{1,0:T(8,128)(2,1)S(1)}, u32[]{:S(2)}, u32[]{:S(2)}) collective-permute-start(bf16[256,768]{1,0:T(8,128)(2,1)S(1)} %shard_map.69.refs_0_), channel_id=1, source_target_pairs={{3,1},{2,0},{1,3},{0,2},{7,5},{6,4},{5,7},{4,6},{11,9},{10,8},{9,1... | collective-permute-start | bytes 1179656 | tf_op jit(solution)/shard_map/ppermute | solution.py:444
  24.3 2.9 %collective-permute-done.2.refs_1_.refs_0_ = bf16[256,256]{1,0:T(8,128)(2,1)S(1)} collective-permute-done((bf16[256,256]{1,0:T(8,128)(2,1)S(1)}, bf16[256,256]{1,0:T(8,128)(2,1)S(1)}, u32[]{:S(2)}, u32[]{:S(2)}) %collective-permute-start.2) | collective-permute-done | bytes 131104 | tf_op jit(solution)/shard_map/ppermute | solution.py:444
  27.2 2.3 %shard_map.70 = (bf16[256,512]{1,0:T(8,128)(2,1)S(1)}, bf16[256,512]{1,0:T(8,128)(2,1)S(1)}) custom-call(bf16[256,1024]{1,0:T(8,128)(2,1)S(1)} %get-tuple-element.28.gated_ref, bf16[1024,4096]{1,0:T(8,128)(2,1)} %weight_hbm.7, bf16[256,768]{1,0:T(8,128)(2,1)S(1)} %shard_map.69.refs_0_, bf16[256,256]{1,0:T(8,128)(2,1)S(1)} %collective-permute-done.2.refs_1_.refs_0_), custom_call_target="tpu_custom_call" | custom-call | flops 8589934592 | tf_op jit(solution)/shard_map/pallas_call | solution.py:354
  29.5 0.1 collective-permute-start.3
  29.5 0.5 %collective-permute-start.4 = (bf16[256,512]{1,0:T(8,128)(2,1)S(1)}, bf16[256,512]{1,0:T(8,128)(2,1)S(1)}, u32[]{:S(2)}, u32[]{:S(2)}) collective-permute-start(bf16[256,512]{1,0:T(8,128)(2,1)S(1)} %get-tuple-element.36), channel_id=1, source_target_pairs={{0,1},{1,0},{2,3},{3,2},{4,5},{5,4},{6,7},{7,6},{8,9},{9,8},{10,11... | collective-permute-start | bytes 786440 | tf_op jit(solution)/shard_map/ppermute | solution.py:461
  30.0 1.0 %collective-permute-done.3.low_ref = bf16[256,512]{1,0:T(8,128)(2,1)S(1)} collective-permute-done((bf16[256,512]{1,0:T(8,128)(2,1)S(1)}, bf16[256,512]{1,0:T(8,128)(2,1)S(1)}, u32[]{:S(2)}, u32[]{:S(2)}) %collective-permute-start.3) | collective-permute-done | bytes 262176 | tf_op jit(solution)/shard_map/ppermute | solution.py:461
  31.1 0.4 %collective-permute-done.4.high_ref = bf16[256,512]{1,0:T(8,128)(2,1)S(1)} collective-permute-done((bf16[256,512]{1,0:T(8,128)(2,1)S(1)}, bf16[256,512]{1,0:T(8,128)(2,1)S(1)}, u32[]{:S(2)}, u32[]{:S(2)}) %collective-permute-start.4) | collective-permute-done | bytes 262176 | tf_op jit(solution)/shard_map/ppermute | solution.py:461
  31.4 2.3 %shard_map.71 = (bf16[256,256]{1,0:T(8,128)(2,1)S(1)}, f32[256,768]{1,0:T(8,128)S(1)}) custom-call(bf16[256,1024]{1,0:T(8,128)(2,1)S(1)} %get-tuple-element.28.gated_ref, bf16[1024,4096]{1,0:T(8,128)(2,1)} %weight_hbm.7, bf16[256,512]{1,0:T(8,128)(2,1)S(1)} %collective-permute-done.3.low_ref, bf16[256,512]{1,0:T(8,128)(2,1)S(1)} %collective-permute-done.4.high_ref, ...), custom_call_target="tpu_custom_call" | custom-call | tf_op jit(solution)/shard_map/pallas_call | solution.py:354
  33.7 1.2 %collective-permute-done.5.refs_0_ = bf16[256,768]{1,0:T(8,128)(2,1)S(1)} collective-permute-done((bf16[256,768]{1,0:T(8,128)(2,1)S(1)}, bf16[256,768]{1,0:T(8,128)(2,1)S(1)}, u32[]{:S(2)}, u32[]{:S(2)}) %collective-permute-start.5) | collective-permute-done | bytes 393248 | tf_op jit(solution)/shard_map/ppermute | solution.py:444
  34.9 0.8 %shard_map.72 = bf16[256,1024]{1,0:T(8,128)(2,1)} custom-call(bf16[256,256]{1,0:T(8,128)(2,1)S(1)} %get-tuple-element.37.first_ref, f32[256,768]{1,0:T(8,128)S(1)} %get-tuple-element.38.own_ref, bf16[256,768]{1,0:T(8,128)(2,1)S(1)} %collective-permute-done.5.refs_0_), custom_call_target="tpu_custom_call" | custom-call | tf_op jit(solution)/shard_map/pallas_call | solution.py:354
  (1 shorter events, 0.0 us)
Async XLA Ops:
  3.1 14.4 %all-to-all-start = ((bf16[8,16,1024]{2,1,0:T(8,128)(2,1)}), bf16[8,16,1024]{2,1,0:T(8,128)(2,1)S(1)}, u32[]{:S(2)}, u32[]{:S(2)}) async-start(bf16[8,16,1024]{2,1,0:T(8,128)(2,1)} %shard_map.64), calls=%async_computation | async-start | bytes 524288 | tf_op jit(solution)/shard_map/all_to_all | solution.py:386
  19.4 1.4 %collective-permute-start.1 = (bf16[256,256]{1,0:T(8,128)(2,1)S(1)}, bf16[256,256]{1,0:T(8,128)(2,1)S(1)}, u32[]{:S(2)}, u32[]{:S(2)}) collective-permute-start(bf16[256,256]{1,0:T(8,128)(2,1)S(1)} %get-tuple-element.34), channel_id=1, source_target_pairs={{0,1},{1,0},{2,3},{3,2},{4,5},{5,4},{6,7},{7,6},{8,9},{9,8},{10,11... | collective-permute-start | bytes 393224 | tf_op jit(solution)/shard_map/ppermute | solution.py:434
  20.2 2.2 %collective-permute-start = (bf16[256,768]{1,0:T(8,128)(2,1)S(1)}, bf16[256,768]{1,0:T(8,128)(2,1)S(1)}, u32[]{:S(2)}, u32[]{:S(2)}) collective-permute-start(bf16[256,768]{1,0:T(8,128)(2,1)S(1)} %get-tuple-element.32), channel_id=1, source_target_pairs={{0,1},{1,0},{2,3},{3,2},{4,5},{5,4},{6,7},{7,6},{8,9},{9,8},{10,11... | collective-permute-start | bytes 1179656 | tf_op jit(solution)/shard_map/ppermute | solution.py:440
  20.9 6.3 %collective-permute-start.2 = (bf16[256,256]{1,0:T(8,128)(2,1)S(1)}, bf16[256,256]{1,0:T(8,128)(2,1)S(1)}, u32[]{:S(2)}, u32[]{:S(2)}) collective-permute-start(bf16[256,256]{1,0:T(8,128)(2,1)S(1)} %shard_map.68.after_ref), channel_id=1, source_target_pairs={{3,1},{2,0},{1,3},{0,2},{7,5},{6,4},{5,7},{4,6},{11,9},{10,8},{9,1... | collective-permute-start | bytes 393224 | tf_op jit(solution)/shard_map/ppermute | solution.py:444
  23.0 11.9 %collective-permute-start.5 = (bf16[256,768]{1,0:T(8,128)(2,1)S(1)}, bf16[256,768]{1,0:T(8,128)(2,1)S(1)}, u32[]{:S(2)}, u32[]{:S(2)}) collective-permute-start(bf16[256,768]{1,0:T(8,128)(2,1)S(1)} %shard_map.69.refs_0_), channel_id=1, source_target_pairs={{3,1},{2,0},{1,3},{0,2},{7,5},{6,4},{5,7},{4,6},{11,9},{10,8},{9,1... | collective-permute-start | bytes 1179656 | tf_op jit(solution)/shard_map/ppermute | solution.py:444
  29.5 1.6 %collective-permute-start.3 = (bf16[256,512]{1,0:T(8,128)(2,1)S(1)}, bf16[256,512]{1,0:T(8,128)(2,1)S(1)}, u32[]{:S(2)}, u32[]{:S(2)}) collective-permute-start(bf16[256,512]{1,0:T(8,128)(2,1)S(1)} %get-tuple-element.35), channel_id=1, source_target_pairs={{0,1},{1,0},{2,3},{3,2},{4,5},{5,4},{6,7},{7,6},{8,9},{9,8},{10,11... | collective-permute-start | bytes 786440 | tf_op jit(solution)/shard_map/ppermute | solution.py:461
  29.5 1.9 %collective-permute-start.4 = (bf16[256,512]{1,0:T(8,128)(2,1)S(1)}, bf16[256,512]{1,0:T(8,128)(2,1)S(1)}, u32[]{:S(2)}, u32[]{:S(2)}) collective-permute-start(bf16[256,512]{1,0:T(8,128)(2,1)S(1)} %get-tuple-element.36), channel_id=1, source_target_pairs={{0,1},{1,0},{2,3},{3,2},{4,5},{5,4},{6,7},{7,6},{8,9},{9,8},{10,11... | collective-permute-start | bytes 786440 | tf_op jit(solution)/shard_map/ppermute | solution.py:461

commit v6 on v5

--- a/solution.py
+++ b/solution.py
@@ -125,8 +125,9 @@
 def local_kernel(
     values_hbm, rates_hbm, residues_hbm, skip_hbm, gate_hbm, weight_hbm,
     near_ref, reach_ref, decay_ref, far_ref, gate_ref, first_weight, kept_weight,
+    sent_weight, last_weight,
     values_ref, rates_ref, residues_ref, skip_ref, wide_ref, taps_ref, first_ref, snap_ref,
-    order_ref, sems, weight_sems,
+    order_ref, sent_held, last_held, sems, weight_sems, out_sems,
 ):
     tok, chan = values_ref.shape
     modes = rates_ref.shape[0]
@@ -148,6 +149,9 @@
     slots = range(1, lax.axis_size("tp") // 2)
     rest = column_copies(1, 0, slots, weight_hbm, first_weight, weight_sems.at[0])
     rest += column_copies(0, 0, slots, weight_hbm, kept_weight, weight_sems.at[1])
+    begin = kept_weight.shape[1] // len(slots)
+    passing = column_copies(1, begin, slots, weight_hbm, sent_held, weight_sems.at[2])
+    passing += column_copies(0, begin, slots, weight_hbm, last_held, weight_sems.at[3])
     rest.append(copies.pop())
     table = spread_table(tok)
     wait_all(copies)
@@ -216,18 +220,20 @@
         far_ref[:, lanes] = jnp.exp(-float(tok) * rates)
         return carry
 
-    lax.fori_loop(0, chan // LANE, step, 0)
+    steps = chan // LANE
+    lax.fori_loop(0, steps // 2, step, 0)
+    wait_all(passing)
+    for at, (held, target) in enumerate(((sent_held, sent_weight), (last_held, last_weight))):
+        rest.append(pltpu.make_async_copy(held, target, out_sems.at[at]))
+        rest[-1].start()
+    lax.fori_loop(steps // 2, steps, step, 0)
     wait_all(rest)
 
 
 def gate_kernel(
-    states_ref, near_ref, reach_ref, decay_ref, far_ref, gate_ref, weight_ref, weight_hbm,
-    gated_ref, sent_ref, later_weight, last_weight, state_ref, sems,
+    states_ref, near_ref, reach_ref, decay_ref, far_ref, gate_ref, weight_ref,
+    gated_ref, sent_ref, state_ref,
 ):
-    slots = range(1, lax.axis_size("tp") // 2)
-    begin = weight_ref.shape[1] // len(slots)
-    rest = column_copies(1, begin, slots, weight_hbm, later_weight, sems.at[0])
-    rest += column_copies(0, begin, slots, weight_hbm, last_weight, sems.at[1])
     tok, chan = gate_ref.shape
     shards, modes = states_ref.shape[:2]
     place = lax.axis_index("seq")
@@ -262,7 +268,6 @@
 
     lax.fori_loop(0, chan // LANE, step, 0)
     project(gated_ref, weight_ref, sent_ref)
-    wait_all(rest)
 
 
 def project(left_ref, right_ref, out_ref):
@@ -345,7 +350,7 @@
     wait_all(copies)
 
 
-def call(kernel, outs, *operands, scratch=(), macs=0, out_spec=VMEM):
+def call(kernel, outs, *operands, scratch=(), macs=0, out_spec=VMEM, in_place=0):
     specs, arrays = [], []
     for operand in operands:
         spec, array = operand if isinstance(operand, tuple) else (VMEM, operand)
@@ -355,7 +360,7 @@
         kernel,
         out_shape=outs,
         in_specs=specs,
-        out_specs=[out_spec] * len(outs),
+        out_specs=[out_spec] * (len(outs) - in_place) + [ANY] * in_place,
         scratch_shapes=scratch,
         compiler_params=PARAMS,
         cost_estimate=pl.CostEstimate(flops=2 * macs, bytes_accessed=0, transcendentals=0),
@@ -390,7 +395,7 @@
     narrow = max(LANE, block // 4)
     wide = block - narrow
     weight = (HBM, out_weight)
-    *tables, first_weight, kept_weight = call(
+    *tables, first_weight, kept_weight, sent_weight, last_weight = call(
         local_kernel,
         [
             here((tok, chan), F32),
@@ -400,8 +405,11 @@
             here((tok, chan), BF16),
             here((chan, away * narrow), BF16),
             here((chan, away * narrow), BF16),
+            pltpu.HBM((chan, away * wide), BF16),
+            pltpu.HBM((chan, away * wide), BF16),
         ],
         *sources, weight,
+        in_place=2,
         scratch=[
             here((tok, chan), BF16),
             here((modes, chan), F32),
@@ -412,24 +420,20 @@
             here((modes * SUB, LANE), F32),
             here((tok // SUB // SUB, modes * SUB, LANE), F32),
             here((tok, LANE), F32),
-            pltpu.SemaphoreType.DMA((len(sources),)),
-            pltpu.SemaphoreType.DMA((2, away * ROW_CUTS)),
-        ],
-    )
-
-    gated, sent, sent_weight, last_weight = call(
-        gate_kernel,
-        [
-            here((tok, chan), BF16),
-            here((tok, away * narrow), BF16),
             here((chan, away * wide), BF16),
             here((chan, away * wide), BF16),
+            pltpu.SemaphoreType.DMA((len(sources),)),
+            pltpu.SemaphoreType.DMA((4, away * ROW_CUTS)),
+            pltpu.SemaphoreType.DMA((2,)),
         ],
-        states, *tables, first_weight, weight,
-        scratch=[
-            here((modes, chan), F32),
-            pltpu.SemaphoreType.DMA((2, away * ROW_CUTS)),
-        ],
+    )
+
+    hint = 16 * tok * chan * block
+    gated, sent = call(
+        gate_kernel,
+        [here((tok, chan), BF16), here((tok, away * narrow), BF16)],
+        states, *tables, first_weight,
+        scratch=[here((modes, chan), F32)], macs=hint,
     )
     moved_first = lax.ppermute(sent, "tp", cores)
     kept, sent = call(
@@ -445,7 +449,6 @@
             for hop, each in enumerate(going, 1)
         ]
 
-    hint = 16 * tok * chan * block
     going = call(join_kernel, [here((tok, narrow), BF16)] * away, kept, moved_first, macs=hint)
     first = to_chips(going)
     going = call(

time: 36.1 us -> 35.8 us (level)
  waiting for transfers between devices: 7.09 us -> 5.94 us
  Pallas kernels: 16.7 us -> 17.5 us
    all_to_all x1, waiting for transfers between devices: 1.55 us -> 0.51 us  [body(): lax.all_to_all(wire, 'seq', split_axis=0, concat_axis=0, tiled=True, axis...]
    pallas_call x9, Pallas kernels: 16.7 us -> 17.5 us  [call(): pl.pallas_call(kernel, out_shape=outs, in_specs=specs, out_specs=[out_spe...]
  transfers between devices with their start and end apart: 7 -> 7, of which waited for: 6 -> 6; matrix products, arithmetic and copies ran while one was open for 0% -> 0% of each run, Pallas kernels for 30% -> 33%
where the time goes in v6:
time: 35.8 us; the launch traced here: 35.5 us
  Pallas kernels  17.5 us (49%)
  starting transfers between devices  12 us (34%)
  waiting for transfers between devices  5.94 us (17%)
    pallas_call x9, Pallas kernels, call(): pl.pallas_call(kernel, out_shape=outs, in_specs=specs, out_specs=[out_spe...  17.5 us
    all_to_all x1, starting transfers between devices, body(): lax.all_to_all(wire, 'seq', split_axis=0, concat_axis=0, tiled=True, axis...  7.83 us
    ppermute x2, waiting for transfers between devices, to_chips(): lax.ppermute(each, 'tp', [(rank, (rank + 2 * hop) % tp) for rank in rever...  3.97 us
    ppermute x2, starting transfers between devices, to_chips(): lax.ppermute(each, 'tp', [(rank, (rank + 2 * hop) % tp) for rank in rever...  2.96 us
    ppermute x2, waiting for transfers between devices, body(): halves = [lax.ppermute(each, 'tp', cores) for each in halves]  1.4 us
  transfers between devices with their start and end apart: 7, of which 6 were waited for; matrix products, arithmetic and copies ran while one was open for 0% of the time, Pallas kernels for 33%

profile of v6, /device:TPU:0, one launch (start us, length us, event | category | flops | bytes accessed | tf_op | source)
XLA Modules:
  0.0 35.5 jit_solution(14927560313343795622)
XLA Ops:
  0.0 3.1 %shard_map.64 = bf16[8,16,1024]{2,1,0:T(8,128)(2,1)} custom-call(bf16[256,1024]{1,0:T(8,128)(2,1)} %values_hbm.3, f32[16,1024]{1,0:T(8,128)} %rates_hbm.3), custom_call_target="tpu_custom_call" | custom-call | tf_op jit(solution)/shard_map/pallas_call | solution.py:359
  3.1 7.8 %all-to-all-start = ((bf16[8,16,1024]{2,1,0:T(8,128)(2,1)}), bf16[8,16,1024]{2,1,0:T(8,128)(2,1)S(1)}, u32[]{:S(2)}, u32[]{:S(2)}) async-start(bf16[8,16,1024]{2,1,0:T(8,128)(2,1)} %shard_map.64), calls=%async_computation | async-start | bytes 524288 | tf_op jit(solution)/shard_map/all_to_all | solution.py:391
  10.9 6.0 %shard_map.65 = (f32[256,1024]{1,0:T(8,128)S(1)}, f32[128,1024]{1,0:T(8,128)S(1)}, f32[16,1024]{1,0:T(8,128)S(1)}, f32[16,1024]{1,0:T(8,128)S(1)}, bf16[256,1024...) custom-call(bf16[256,1024]{1,0:T(8,128)(2,1)} %values_hbm.3, ...), custom_call_target="tpu_custom_call" | custom-call | tf_op jit(solution)/shard_map/pallas_call | solution.py:359
  17.0 0.5 %all-to-all-done.states_ref = bf16[8,16,1024]{2,1,0:T(8,128)(2,1)S(1)} async-done(((bf16[8,16,1024]{2,1,0:T(8,128)(2,1)}), bf16[8,16,1024]{2,1,0:T(8,128)(2,1)S(1)}, u32[]{:S(2)}, u32[]{:S(2)}) %all-to-all-start) | async-done | bytes 262176 | tf_op jit(solution)/shard_map/all_to_all | solution.py:391
  17.5 1.7 %shard_map.66 = (bf16[256,1024]{1,0:T(8,128)(2,1)S(1)}, bf16[256,256]{1,0:T(8,128)(2,1)S(1)}) custom-call(bf16[8,16,1024]{2,1,0:T(8,128)(2,1)S(1)} %all-to-all-done.states_ref, f32[256,1024]{1,0:T(8,128)S(1)} %get-tuple-element.22.near_ref, f32[128,1024]{1,0:T(8,128)S(1)} %get-tuple-element.23.reach_ref, f32[16,1024]{1,0:T(8,128)S(1)} %get-tuple-element.24.decay_ref, ...), custom_call_target="tpu_custom_call" | custom-call | flops 8589934592 | tf_op jit(solution)/shard_map/pallas_call | solution.py:359
  19.2 0.1 collective-permute-start.1
  19.3 0.0 copy-done.1
  19.3 0.7 %shard_map.67 = (f32[256,256]{1,0:T(8,128)S(1)}, bf16[256,768]{1,0:T(8,128)(2,1)S(1)}) custom-call(bf16[256,1024]{1,0:T(8,128)(2,1)S(1)} %get-tuple-element.28.gated_ref, bf16[1024,256]{1,0:T(8,128)(2,1)S(1)} %get-tuple-element.30.kept_weight, bf16[1024,768]{1,0:T(8,128)(2,1)S(1)} %copy-done.1), custom_call_target="tpu_custom_call" | custom-call | tf_op jit(solution)/shard_map/pallas_call | solution.py:359
  20.0 0.6 %collective-permute-start = (bf16[256,768]{1,0:T(8,128)(2,1)S(1)}, bf16[256,768]{1,0:T(8,128)(2,1)S(1)}, u32[]{:S(2)}, u32[]{:S(2)}) collective-permute-start(bf16[256,768]{1,0:T(8,128)(2,1)S(1)} %get-tuple-element.32), channel_id=1, source_target_pairs={{0,1},{1,0},{2,3},{3,2},{4,5},{5,4},{6,7},{7,6},{8,9},{9,8},{10,11... | collective-permute-start | bytes 1179656 | tf_op jit(solution)/shard_map/ppermute | solution.py:444
  20.6 0.1 collective-permute-done.1.moved_ref
  20.6 1.6 %collective-permute-start.2 = (bf16[256,256]{1,0:T(8,128)(2,1)S(1)}, bf16[256,256]{1,0:T(8,128)(2,1)S(1)}, u32[]{:S(2)}, u32[]{:S(2)}) collective-permute-start(bf16[256,256]{1,0:T(8,128)(2,1)S(1)} %shard_map.68.after_ref), channel_id=1, source_target_pairs={{3,1},{2,0},{1,3},{0,2},{7,5},{6,4},{5,7},{4,6},{11,9},{10,8},{9,1... | collective-permute-start | bytes 393224 | tf_op jit(solution)/shard_map/ppermute | solution.py:448
  22.2 0.0 collective-permute-done.moved_ref
  22.2 0.0 copy-done
  22.2 0.6 %shard_map.69.refs_0_ = bf16[256,768]{1,0:T(8,128)(2,1)S(1)} custom-call(bf16[256,1024]{1,0:T(8,128)(2,1)S(1)} %get-tuple-element.28.gated_ref, bf16[1024,768]{1,0:T(8,128)(2,1)S(1)} %copy-done, bf16[256,768]{1,0:T(8,128)(2,1)S(1)} %collective-permute-done.moved_ref, bf16[256,256]{1,0:T(8,128)(2,1)S(1)} %shard_map.68.after_ref), custom_call_target="tpu_custom_call" | custom-call | tf_op jit(solution)/shard_map/pallas_call | solution.py:359
  22.8 1.4 %collective-permute-start.5 = (bf16[256,768]{1,0:T(8,128)(2,1)S(1)}, bf16[256,768]{1,0:T(8,128)(2,1)S(1)}, u32[]{:S(2)}, u32[]{:S(2)}) collective-permute-start(bf16[256,768]{1,0:T(8,128)(2,1)S(1)} %shard_map.69.refs_0_), channel_id=1, source_target_pairs={{3,1},{2,0},{1,3},{0,2},{7,5},{6,4},{5,7},{4,6},{11,9},{10,8},{9,1... | collective-permute-start | bytes 1179656 | tf_op jit(solution)/shard_map/ppermute | solution.py:448
  24.2 2.8 %collective-permute-done.2.refs_1_.refs_0_ = bf16[256,256]{1,0:T(8,128)(2,1)S(1)} collective-permute-done((bf16[256,256]{1,0:T(8,128)(2,1)S(1)}, bf16[256,256]{1,0:T(8,128)(2,1)S(1)}, u32[]{:S(2)}, u32[]{:S(2)}) %collective-permute-start.2) | collective-permute-done | bytes 131104 | tf_op jit(solution)/shard_map/ppermute | solution.py:448
  27.0 2.3 %shard_map.70 = (bf16[256,512]{1,0:T(8,128)(2,1)S(1)}, bf16[256,512]{1,0:T(8,128)(2,1)S(1)}) custom-call(bf16[256,1024]{1,0:T(8,128)(2,1)S(1)} %get-tuple-element.28.gated_ref, bf16[1024,4096]{1,0:T(8,128)(2,1)} %weight_hbm.5, bf16[256,768]{1,0:T(8,128)(2,1)S(1)} %shard_map.69.refs_0_, bf16[256,256]{1,0:T(8,128)(2,1)S(1)} %collective-permute-done.2.refs_1_.refs_0_), custom_call_target="tpu_custom_call" | custom-call | flops 8589934592 | tf_op jit(solution)/shard_map/pallas_call | solution.py:359
  29.2 0.1 collective-permute-start.3
  29.3 0.5 %collective-permute-start.4 = (bf16[256,512]{1,0:T(8,128)(2,1)S(1)}, bf16[256,512]{1,0:T(8,128)(2,1)S(1)}, u32[]{:S(2)}, u32[]{:S(2)}) collective-permute-start(bf16[256,512]{1,0:T(8,128)(2,1)S(1)} %get-tuple-element.36), channel_id=1, source_target_pairs={{0,1},{1,0},{2,3},{3,2},{4,5},{5,4},{6,7},{7,6},{8,9},{9,8},{10,11... | collective-permute-start | bytes 786440 | tf_op jit(solution)/shard_map/ppermute | solution.py:464
  29.8 1.0 %collective-permute-done.3.low_ref = bf16[256,512]{1,0:T(8,128)(2,1)S(1)} collective-permute-done((bf16[256,512]{1,0:T(8,128)(2,1)S(1)}, bf16[256,512]{1,0:T(8,128)(2,1)S(1)}, u32[]{:S(2)}, u32[]{:S(2)}) %collective-permute-start.3) | collective-permute-done | bytes 262176 | tf_op jit(solution)/shard_map/ppermute | solution.py:464
  30.8 0.4 %collective-permute-done.4.high_ref = bf16[256,512]{1,0:T(8,128)(2,1)S(1)} collective-permute-done((bf16[256,512]{1,0:T(8,128)(2,1)S(1)}, bf16[256,512]{1,0:T(8,128)(2,1)S(1)}, u32[]{:S(2)}, u32[]{:S(2)}) %collective-permute-start.4) | collective-permute-done | bytes 262176 | tf_op jit(solution)/shard_map/ppermute | solution.py:464
  31.2 2.3 %shard_map.71 = (bf16[256,256]{1,0:T(8,128)(2,1)S(1)}, f32[256,768]{1,0:T(8,128)S(1)}) custom-call(bf16[256,1024]{1,0:T(8,128)(2,1)S(1)} %get-tuple-element.28.gated_ref, bf16[1024,4096]{1,0:T(8,128)(2,1)} %weight_hbm.5, bf16[256,512]{1,0:T(8,128)(2,1)S(1)} %collective-permute-done.3.low_ref, bf16[256,512]{1,0:T(8,128)(2,1)S(1)} %collective-permute-done.4.high_ref, ...), custom_call_target="tpu_custom_call" | custom-call | tf_op jit(solution)/shard_map/pallas_call | solution.py:359
  33.5 1.2 %collective-permute-done.5.refs_0_ = bf16[256,768]{1,0:T(8,128)(2,1)S(1)} collective-permute-done((bf16[256,768]{1,0:T(8,128)(2,1)S(1)}, bf16[256,768]{1,0:T(8,128)(2,1)S(1)}, u32[]{:S(2)}, u32[]{:S(2)}) %collective-permute-start.5) | collective-permute-done | bytes 393248 | tf_op jit(solution)/shard_map/ppermute | solution.py:448
  34.7 0.8 %shard_map.72 = bf16[256,1024]{1,0:T(8,128)(2,1)} custom-call(bf16[256,256]{1,0:T(8,128)(2,1)S(1)} %get-tuple-element.37.first_ref, f32[256,768]{1,0:T(8,128)S(1)} %get-tuple-element.38.own_ref, bf16[256,768]{1,0:T(8,128)(2,1)S(1)} %collective-permute-done.5.refs_0_), custom_call_target="tpu_custom_call" | custom-call | tf_op jit(solution)/shard_map/pallas_call | solution.py:359
  (3 shorter events, 0.0 us)
Async XLA Ops:
  3.1 14.4 %all-to-all-start = ((bf16[8,16,1024]{2,1,0:T(8,128)(2,1)}), bf16[8,16,1024]{2,1,0:T(8,128)(2,1)S(1)}, u32[]{:S(2)}, u32[]{:S(2)}) async-start(bf16[8,16,1024]{2,1,0:T(8,128)(2,1)} %shard_map.64), calls=%async_computation | async-start | bytes 524288 | tf_op jit(solution)/shard_map/all_to_all | solution.py:391
  17.5 1.8 %copy-start.1 = (bf16[1024,768]{1,0:T(8,128)(2,1)S(1)}, bf16[1024,768]{1,0:T(8,128)(2,1)}, u32[]{:S(2)}) copy-start(bf16[1024,768]{1,0:T(8,128)(2,1)} %get-tuple-element.31.sent_weight) | copy-start | bytes 4718596
  19.2 1.4 %collective-permute-start.1 = (bf16[256,256]{1,0:T(8,128)(2,1)S(1)}, bf16[256,256]{1,0:T(8,128)(2,1)S(1)}, u32[]{:S(2)}, u32[]{:S(2)}) collective-permute-start(bf16[256,256]{1,0:T(8,128)(2,1)S(1)} %get-tuple-element.34), channel_id=1, source_target_pairs={{0,1},{1,0},{2,3},{3,2},{4,5},{5,4},{6,7},{7,6},{8,9},{9,8},{10,11... | collective-permute-start | bytes 393224 | tf_op jit(solution)/shard_map/ppermute | solution.py:438
  20.0 2.2 %collective-permute-start = (bf16[256,768]{1,0:T(8,128)(2,1)S(1)}, bf16[256,768]{1,0:T(8,128)(2,1)S(1)}, u32[]{:S(2)}, u32[]{:S(2)}) collective-permute-start(bf16[256,768]{1,0:T(8,128)(2,1)S(1)} %get-tuple-element.32), channel_id=1, source_target_pairs={{0,1},{1,0},{2,3},{3,2},{4,5},{5,4},{6,7},{7,6},{8,9},{9,8},{10,11... | collective-permute-start | bytes 1179656 | tf_op jit(solution)/shard_map/ppermute | solution.py:444
  20.6 1.6 %copy-start = (bf16[1024,768]{1,0:T(8,128)(2,1)S(1)}, bf16[1024,768]{1,0:T(8,128)(2,1)}, u32[]{:S(2)}) copy-start(bf16[1024,768]{1,0:T(8,128)(2,1)} %get-tuple-element.29.weight_ref) | copy-start | bytes 4718596
  20.6 6.3 %collective-permute-start.2 = (bf16[256,256]{1,0:T(8,128)(2,1)S(1)}, bf16[256,256]{1,0:T(8,128)(2,1)S(1)}, u32[]{:S(2)}, u32[]{:S(2)}) collective-permute-start(bf16[256,256]{1,0:T(8,128)(2,1)S(1)} %shard_map.68.after_ref), channel_id=1, source_target_pairs={{3,1},{2,0},{1,3},{0,2},{7,5},{6,4},{5,7},{4,6},{11,9},{10,8},{9,1... | collective-permute-start | bytes 393224 | tf_op jit(solution)/shard_map/ppermute | solution.py:448
  22.8 11.9 %collective-permute-start.5 = (bf16[256,768]{1,0:T(8,128)(2,1)S(1)}, bf16[256,768]{1,0:T(8,128)(2,1)S(1)}, u32[]{:S(2)}, u32[]{:S(2)}) collective-permute-start(bf16[256,768]{1,0:T(8,128)(2,1)S(1)} %shard_map.69.refs_0_), channel_id=1, source_target_pairs={{3,1},{2,0},{1,3},{0,2},{7,5},{6,4},{5,7},{4,6},{11,9},{10,8},{9,1... | collective-permute-start | bytes 1179656 | tf_op jit(solution)/shard_map/ppermute | solution.py:448
  29.2 1.6 %collective-permute-start.3 = (bf16[256,512]{1,0:T(8,128)(2,1)S(1)}, bf16[256,512]{1,0:T(8,128)(2,1)S(1)}, u32[]{:S(2)}, u32[]{:S(2)}) collective-permute-start(bf16[256,512]{1,0:T(8,128)(2,1)S(1)} %get-tuple-element.35), channel_id=1, source_target_pairs={{0,1},{1,0},{2,3},{3,2},{4,5},{5,4},{6,7},{7,6},{8,9},{9,8},{10,11... | collective-permute-start | bytes 786440 | tf_op jit(solution)/shard_map/ppermute | solution.py:464
  29.3 1.9 %collective-permute-start.4 = (bf16[256,512]{1,0:T(8,128)(2,1)S(1)}, bf16[256,512]{1,0:T(8,128)(2,1)S(1)}, u32[]{:S(2)}, u32[]{:S(2)}) collective-permute-start(bf16[256,512]{1,0:T(8,128)(2,1)S(1)} %get-tuple-element.36), channel_id=1, source_target_pairs={{0,1},{1,0},{2,3},{3,2},{4,5},{5,4},{6,7},{7,6},{8,9},{9,8},{10,11... | collective-permute-start | bytes 786440 | tf_op jit(solution)/shard_map/ppermute | solution.py:464

commit v7 on v6

--- a/solution.py
+++ b/solution.py
@@ -232,7 +232,7 @@
 
 def gate_kernel(
     states_ref, near_ref, reach_ref, decay_ref, far_ref, gate_ref, weight_ref,
-    gated_ref, sent_ref, state_ref,
+    gated_ref, sent_ref, state_ref, total_ref,
 ):
     tok, chan = gate_ref.shape
     shards, modes = states_ref.shape[:2]
@@ -245,7 +245,9 @@
         before = jnp.where(shard < place, passed, before)
     state_ref[...] = before
 
-    def step(index, carry):
+    batch = 2 * LANE
+
+    def carry_pass(index):
         lanes = lanes_at(index)
         decays, terms = [], []
         for mode in range(modes):
@@ -264,10 +266,25 @@
             rows = slice(at, at + 2 * SUB)
             gate = gate_ref[rows, lanes].astype(F32)
             gated_ref[rows, lanes] = (gate * jnp.concatenate(totals, axis=0)).astype(BF16)
+
+    def partial_product(index):
+        channels = pl.ds(pl.multiple_of(index * batch, batch), batch)
+        return jnp.dot(
+            gated_ref[:, channels], weight_ref[channels, :], preferred_element_type=F32
+        )
+
+    def step(index, carry):
+        total_ref[...] += partial_product(index - 1)
+        for half in range(2):
+            carry_pass(2 * index + half)
         return carry
 
-    lax.fori_loop(0, chan // LANE, step, 0)
-    project(gated_ref, weight_ref, sent_ref)
+    for half in range(2):
+        carry_pass(half)
+    total_ref[...] = jnp.zeros_like(total_ref)
+    steps = chan // batch
+    lax.fori_loop(1, steps, step, 0)
+    sent_ref[...] = (total_ref[...] + partial_product(steps - 1)).astype(BF16)
 
 
 def project(left_ref, right_ref, out_ref):
@@ -433,7 +450,7 @@
         gate_kernel,
         [here((tok, chan), BF16), here((tok, away * narrow), BF16)],
         states, *tables, first_weight,
-        scratch=[here((modes, chan), F32)], macs=hint,
+        scratch=[here((modes, chan), F32), here((tok, away * narrow), F32)], macs=hint,
     )
     moved_first = lax.ppermute(sent, "tp", cores)
     kept, sent = call(

time: 35.8 us -> 36 us (level)
  no operation moved by 1% of the time
where the time goes in v7:
time: 36 us; the launch traced here: 35.8 us
  Pallas kernels  17.8 us (49%)
  starting transfers between devices  12 us (33%)
  waiting for transfers between devices  5.93 us (16%)
    pallas_call x9, Pallas kernels, call(): pl.pallas_call(kernel, out_shape=outs, in_specs=specs, out_specs=[out_spe...  17.8 us
    all_to_all x1, starting transfers between devices, body(): lax.all_to_all(wire, 'seq', split_axis=0, concat_axis=0, tiled=True, axis...  7.83 us
    ppermute x2, waiting for transfers between devices, to_chips(): lax.ppermute(each, 'tp', [(rank, (rank + 2 * hop) % tp) for rank in rever...  3.97 us
    ppermute x2, starting transfers between devices, to_chips(): lax.ppermute(each, 'tp', [(rank, (rank + 2 * hop) % tp) for rank in rever...  2.96 us
    ppermute x2, waiting for transfers between devices, body(): halves = [lax.ppermute(each, 'tp', cores) for each in halves]  1.4 us
  transfers between devices with their start and end apart: 7, of which 6 were waited for; matrix products, arithmetic and copies ran while one was open for 0% of the time, Pallas kernels for 33%

profile of v7, /device:TPU:0, one launch (start us, length us, event | category | flops | bytes accessed | tf_op | source)
XLA Modules:
  0.0 35.8 jit_solution(13565035560976214286)
XLA Ops:
  0.0 3.1 %shard_map.64 = bf16[8,16,1024]{2,1,0:T(8,128)(2,1)} custom-call(bf16[256,1024]{1,0:T(8,128)(2,1)} %values_hbm.3, f32[16,1024]{1,0:T(8,128)} %rates_hbm.3), custom_call_target="tpu_custom_call" | custom-call | tf_op jit(solution)/shard_map/pallas_call | solution.py:376
  3.1 7.8 %all-to-all-start = ((bf16[8,16,1024]{2,1,0:T(8,128)(2,1)}), bf16[8,16,1024]{2,1,0:T(8,128)(2,1)S(1)}, u32[]{:S(2)}, u32[]{:S(2)}) async-start(bf16[8,16,1024]{2,1,0:T(8,128)(2,1)} %shard_map.64), calls=%async_computation | async-start | bytes 524288 | tf_op jit(solution)/shard_map/all_to_all | solution.py:408
  10.9 6.0 %shard_map.65 = (f32[256,1024]{1,0:T(8,128)S(1)}, f32[128,1024]{1,0:T(8,128)S(1)}, f32[16,1024]{1,0:T(8,128)S(1)}, f32[16,1024]{1,0:T(8,128)S(1)}, bf16[256,1024...) custom-call(bf16[256,1024]{1,0:T(8,128)(2,1)} %values_hbm.3, ...), custom_call_target="tpu_custom_call" | custom-call | tf_op jit(solution)/shard_map/pallas_call | solution.py:376
  17.0 0.5 %all-to-all-done.states_ref = bf16[8,16,1024]{2,1,0:T(8,128)(2,1)S(1)} async-done(((bf16[8,16,1024]{2,1,0:T(8,128)(2,1)}), bf16[8,16,1024]{2,1,0:T(8,128)(2,1)S(1)}, u32[]{:S(2)}, u32[]{:S(2)}) %all-to-all-start) | async-done | bytes 262176 | tf_op jit(solution)/shard_map/all_to_all | solution.py:408
  17.5 2.0 %shard_map.66 = (bf16[256,1024]{1,0:T(8,128)(2,1)S(1)}, bf16[256,256]{1,0:T(8,128)(2,1)S(1)}) custom-call(bf16[8,16,1024]{2,1,0:T(8,128)(2,1)S(1)} %all-to-all-done.states_ref, f32[256,1024]{1,0:T(8,128)S(1)} %get-tuple-element.22.near_ref, f32[128,1024]{1,0:T(8,128)S(1)} %get-tuple-element.23.reach_ref, f32[16,1024]{1,0:T(8,128)S(1)} %get-tuple-element.24.decay_ref, ...), custom_call_target="tpu_custom_call" | custom-call | flops 8589934592 | tf_op jit(solution)/shard_map/pallas_call | solution.py:376
  19.5 0.1 collective-permute-start.1
  19.5 0.0 copy-done.1
  19.5 0.7 %shard_map.67 = (f32[256,256]{1,0:T(8,128)S(1)}, bf16[256,768]{1,0:T(8,128)(2,1)S(1)}) custom-call(bf16[256,1024]{1,0:T(8,128)(2,1)S(1)} %get-tuple-element.28.gated_ref, bf16[1024,256]{1,0:T(8,128)(2,1)S(1)} %get-tuple-element.30.kept_weight, bf16[1024,768]{1,0:T(8,128)(2,1)S(1)} %copy-done.1), custom_call_target="tpu_custom_call" | custom-call | tf_op jit(solution)/shard_map/pallas_call | solution.py:376
  20.3 0.6 %collective-permute-start = (bf16[256,768]{1,0:T(8,128)(2,1)S(1)}, bf16[256,768]{1,0:T(8,128)(2,1)S(1)}, u32[]{:S(2)}, u32[]{:S(2)}) collective-permute-start(bf16[256,768]{1,0:T(8,128)(2,1)S(1)} %get-tuple-element.32), channel_id=1, source_target_pairs={{0,1},{1,0},{2,3},{3,2},{4,5},{5,4},{6,7},{7,6},{8,9},{9,8},{10,11... | collective-permute-start | bytes 1179656 | tf_op jit(solution)/shard_map/ppermute | solution.py:461
  20.8 0.1 collective-permute-done.1.moved_ref
  20.9 1.6 %collective-permute-start.2 = (bf16[256,256]{1,0:T(8,128)(2,1)S(1)}, bf16[256,256]{1,0:T(8,128)(2,1)S(1)}, u32[]{:S(2)}, u32[]{:S(2)}) collective-permute-start(bf16[256,256]{1,0:T(8,128)(2,1)S(1)} %shard_map.68.after_ref), channel_id=1, source_target_pairs={{3,1},{2,0},{1,3},{0,2},{7,5},{6,4},{5,7},{4,6},{11,9},{10,8},{9,1... | collective-permute-start | bytes 393224 | tf_op jit(solution)/shard_map/ppermute | solution.py:465
  22.5 0.0 collective-permute-done.moved_ref
  22.5 0.0 copy-done
  22.5 0.6 %shard_map.69.refs_0_ = bf16[256,768]{1,0:T(8,128)(2,1)S(1)} custom-call(bf16[256,1024]{1,0:T(8,128)(2,1)S(1)} %get-tuple-element.28.gated_ref, bf16[1024,768]{1,0:T(8,128)(2,1)S(1)} %copy-done, bf16[256,768]{1,0:T(8,128)(2,1)S(1)} %collective-permute-done.moved_ref, bf16[256,256]{1,0:T(8,128)(2,1)S(1)} %shard_map.68.after_ref), custom_call_target="tpu_custom_call" | custom-call | tf_op jit(solution)/shard_map/pallas_call | solution.py:376
  23.1 1.4 %collective-permute-start.5 = (bf16[256,768]{1,0:T(8,128)(2,1)S(1)}, bf16[256,768]{1,0:T(8,128)(2,1)S(1)}, u32[]{:S(2)}, u32[]{:S(2)}) collective-permute-start(bf16[256,768]{1,0:T(8,128)(2,1)S(1)} %shard_map.69.refs_0_), channel_id=1, source_target_pairs={{3,1},{2,0},{1,3},{0,2},{7,5},{6,4},{5,7},{4,6},{11,9},{10,8},{9,1... | collective-permute-start | bytes 1179656 | tf_op jit(solution)/shard_map/ppermute | solution.py:465
  24.4 2.8 %collective-permute-done.2.refs_1_.refs_0_ = bf16[256,256]{1,0:T(8,128)(2,1)S(1)} collective-permute-done((bf16[256,256]{1,0:T(8,128)(2,1)S(1)}, bf16[256,256]{1,0:T(8,128)(2,1)S(1)}, u32[]{:S(2)}, u32[]{:S(2)}) %collective-permute-start.2) | collective-permute-done | bytes 131104 | tf_op jit(solution)/shard_map/ppermute | solution.py:465
  27.2 2.3 %shard_map.70 = (bf16[256,512]{1,0:T(8,128)(2,1)S(1)}, bf16[256,512]{1,0:T(8,128)(2,1)S(1)}) custom-call(bf16[256,1024]{1,0:T(8,128)(2,1)S(1)} %get-tuple-element.28.gated_ref, bf16[1024,4096]{1,0:T(8,128)(2,1)} %weight_hbm.5, bf16[256,768]{1,0:T(8,128)(2,1)S(1)} %shard_map.69.refs_0_, bf16[256,256]{1,0:T(8,128)(2,1)S(1)} %collective-permute-done.2.refs_1_.refs_0_), custom_call_target="tpu_custom_call" | custom-call | flops 8589934592 | tf_op jit(solution)/shard_map/pallas_call | solution.py:376
  29.5 0.1 collective-permute-start.3
  29.6 0.5 %collective-permute-start.4 = (bf16[256,512]{1,0:T(8,128)(2,1)S(1)}, bf16[256,512]{1,0:T(8,128)(2,1)S(1)}, u32[]{:S(2)}, u32[]{:S(2)}) collective-permute-start(bf16[256,512]{1,0:T(8,128)(2,1)S(1)} %get-tuple-element.36), channel_id=1, source_target_pairs={{0,1},{1,0},{2,3},{3,2},{4,5},{5,4},{6,7},{7,6},{8,9},{9,8},{10,11... | collective-permute-start | bytes 786440 | tf_op jit(solution)/shard_map/ppermute | solution.py:481
  30.1 1.0 %collective-permute-done.3.low_ref = bf16[256,512]{1,0:T(8,128)(2,1)S(1)} collective-permute-done((bf16[256,512]{1,0:T(8,128)(2,1)S(1)}, bf16[256,512]{1,0:T(8,128)(2,1)S(1)}, u32[]{:S(2)}, u32[]{:S(2)}) %collective-permute-start.3) | collective-permute-done | bytes 262176 | tf_op jit(solution)/shard_map/ppermute | solution.py:481
  31.1 0.4 %collective-permute-done.4.high_ref = bf16[256,512]{1,0:T(8,128)(2,1)S(1)} collective-permute-done((bf16[256,512]{1,0:T(8,128)(2,1)S(1)}, bf16[256,512]{1,0:T(8,128)(2,1)S(1)}, u32[]{:S(2)}, u32[]{:S(2)}) %collective-permute-start.4) | collective-permute-done | bytes 262176 | tf_op jit(solution)/shard_map/ppermute | solution.py:481
  31.5 2.3 %shard_map.71 = (bf16[256,256]{1,0:T(8,128)(2,1)S(1)}, f32[256,768]{1,0:T(8,128)S(1)}) custom-call(bf16[256,1024]{1,0:T(8,128)(2,1)S(1)} %get-tuple-element.28.gated_ref, bf16[1024,4096]{1,0:T(8,128)(2,1)} %weight_hbm.5, bf16[256,512]{1,0:T(8,128)(2,1)S(1)} %collective-permute-done.3.low_ref, bf16[256,512]{1,0:T(8,128)(2,1)S(1)} %collective-permute-done.4.high_ref, ...), custom_call_target="tpu_custom_call" | custom-call | tf_op jit(solution)/shard_map/pallas_call | solution.py:376
  33.7 1.2 %collective-permute-done.5.refs_0_ = bf16[256,768]{1,0:T(8,128)(2,1)S(1)} collective-permute-done((bf16[256,768]{1,0:T(8,128)(2,1)S(1)}, bf16[256,768]{1,0:T(8,128)(2,1)S(1)}, u32[]{:S(2)}, u32[]{:S(2)}) %collective-permute-start.5) | collective-permute-done | bytes 393248 | tf_op jit(solution)/shard_map/ppermute | solution.py:465
  34.9 0.8 %shard_map.72 = bf16[256,1024]{1,0:T(8,128)(2,1)} custom-call(bf16[256,256]{1,0:T(8,128)(2,1)S(1)} %get-tuple-element.37.first_ref, f32[256,768]{1,0:T(8,128)S(1)} %get-tuple-element.38.own_ref, bf16[256,768]{1,0:T(8,128)(2,1)S(1)} %collective-permute-done.5.refs_0_), custom_call_target="tpu_custom_call" | custom-call | tf_op jit(solution)/shard_map/pallas_call | solution.py:376
  (3 shorter events, 0.0 us)
Async XLA Ops:
  3.1 14.4 %all-to-all-start = ((bf16[8,16,1024]{2,1,0:T(8,128)(2,1)}), bf16[8,16,1024]{2,1,0:T(8,128)(2,1)S(1)}, u32[]{:S(2)}, u32[]{:S(2)}) async-start(bf16[8,16,1024]{2,1,0:T(8,128)(2,1)} %shard_map.64), calls=%async_computation | async-start | bytes 524288 | tf_op jit(solution)/shard_map/all_to_all | solution.py:408
  17.5 2.0 %copy-start.1 = (bf16[1024,768]{1,0:T(8,128)(2,1)S(1)}, bf16[1024,768]{1,0:T(8,128)(2,1)}, u32[]{:S(2)}) copy-start(bf16[1024,768]{1,0:T(8,128)(2,1)} %get-tuple-element.31.sent_weight) | copy-start | bytes 4718596
  19.5 1.4 %collective-permute-start.1 = (bf16[256,256]{1,0:T(8,128)(2,1)S(1)}, bf16[256,256]{1,0:T(8,128)(2,1)S(1)}, u32[]{:S(2)}, u32[]{:S(2)}) collective-permute-start(bf16[256,256]{1,0:T(8,128)(2,1)S(1)} %get-tuple-element.34), channel_id=1, source_target_pairs={{0,1},{1,0},{2,3},{3,2},{4,5},{5,4},{6,7},{7,6},{8,9},{9,8},{10,11... | collective-permute-start | bytes 393224 | tf_op jit(solution)/shard_map/ppermute | solution.py:455
  20.3 2.2 %collective-permute-start = (bf16[256,768]{1,0:T(8,128)(2,1)S(1)}, bf16[256,768]{1,0:T(8,128)(2,1)S(1)}, u32[]{:S(2)}, u32[]{:S(2)}) collective-permute-start(bf16[256,768]{1,0:T(8,128)(2,1)S(1)} %get-tuple-element.32), channel_id=1, source_target_pairs={{0,1},{1,0},{2,3},{3,2},{4,5},{5,4},{6,7},{7,6},{8,9},{9,8},{10,11... | collective-permute-start | bytes 1179656 | tf_op jit(solution)/shard_map/ppermute | solution.py:461
  20.9 1.6 %copy-start = (bf16[1024,768]{1,0:T(8,128)(2,1)S(1)}, bf16[1024,768]{1,0:T(8,128)(2,1)}, u32[]{:S(2)}) copy-start(bf16[1024,768]{1,0:T(8,128)(2,1)} %get-tuple-element.29.weight_ref) | copy-start | bytes 4718596
  20.9 6.3 %collective-permute-start.2 = (bf16[256,256]{1,0:T(8,128)(2,1)S(1)}, bf16[256,256]{1,0:T(8,128)(2,1)S(1)}, u32[]{:S(2)}, u32[]{:S(2)}) collective-permute-start(bf16[256,256]{1,0:T(8,128)(2,1)S(1)} %shard_map.68.after_ref), channel_id=1, source_target_pairs={{3,1},{2,0},{1,3},{0,2},{7,5},{6,4},{5,7},{4,6},{11,9},{10,8},{9,1... | collective-permute-start | bytes 393224 | tf_op jit(solution)/shard_map/ppermute | solution.py:465
  23.1 11.9 %collective-permute-start.5 = (bf16[256,768]{1,0:T(8,128)(2,1)S(1)}, bf16[256,768]{1,0:T(8,128)(2,1)S(1)}, u32[]{:S(2)}, u32[]{:S(2)}) collective-permute-start(bf16[256,768]{1,0:T(8,128)(2,1)S(1)} %shard_map.69.refs_0_), channel_id=1, source_target_pairs={{3,1},{2,0},{1,3},{0,2},{7,5},{6,4},{5,7},{4,6},{11,9},{10,8},{9,1... | collective-permute-start | bytes 1179656 | tf_op jit(solution)/shard_map/ppermute | solution.py:465
  29.5 1.6 %collective-permute-start.3 = (bf16[256,512]{1,0:T(8,128)(2,1)S(1)}, bf16[256,512]{1,0:T(8,128)(2,1)S(1)}, u32[]{:S(2)}, u32[]{:S(2)}) collective-permute-start(bf16[256,512]{1,0:T(8,128)(2,1)S(1)} %get-tuple-element.35), channel_id=1, source_target_pairs={{0,1},{1,0},{2,3},{3,2},{4,5},{5,4},{6,7},{7,6},{8,9},{9,8},{10,11... | collective-permute-start | bytes 786440 | tf_op jit(solution)/shard_map/ppermute | solution.py:481
  29.6 1.9 %collective-permute-start.4 = (bf16[256,512]{1,0:T(8,128)(2,1)S(1)}, bf16[256,512]{1,0:T(8,128)(2,1)S(1)}, u32[]{:S(2)}, u32[]{:S(2)}) collective-permute-start(bf16[256,512]{1,0:T(8,128)(2,1)S(1)} %get-tuple-element.36), channel_id=1, source_target_pairs={{0,1},{1,0},{2,3},{3,2},{4,5},{5,4},{6,7},{7,6},{8,9},{9,8},{10,11... | collective-permute-start | bytes 786440 | tf_op jit(solution)/shard_map/ppermute | solution.py:481

commit v8 on v6

--- a/solution.py
+++ b/solution.py
@@ -48,6 +48,7 @@
 
 
 ROW_CUTS = 4
+STEP_ROWS = 64
 
 
 def column_copies(other, begin, slots, weight_hbm, out_ref, sems):
@@ -253,17 +254,23 @@
             decays.append(jnp.broadcast_to(decay_ref[row, lanes], (SUB, LANE)))
             state = jnp.broadcast_to(state_ref[row, lanes], (SUB, LANE))
             terms.append(state * reach_ref[rows, lanes])
-        for at in range(0, tok, 2 * SUB):
-            totals = []
-            for first in (at, at + SUB):
-                total = near_ref[first : first + SUB, lanes]
-                for mode in range(modes):
-                    total = total + terms[mode]
-                terms = [terms[mode] * decays[mode] for mode in range(modes)]
-                totals.append(total)
-            rows = slice(at, at + 2 * SUB)
-            gate = gate_ref[rows, lanes].astype(F32)
-            gated_ref[rows, lanes] = (gate * jnp.concatenate(totals, axis=0)).astype(BF16)
+        def rows_step(group, terms):
+            terms = list(terms)
+            for at in range(0, STEP_ROWS, 2 * SUB):
+                totals = []
+                for first in (at, at + SUB):
+                    rows = pl.ds(pl.multiple_of(group * STEP_ROWS + first, SUB), SUB)
+                    total = near_ref[rows, lanes]
+                    for mode in range(modes):
+                        total = total + terms[mode]
+                    terms = [terms[mode] * decays[mode] for mode in range(modes)]
+                    totals.append(total)
+                rows = pl.ds(pl.multiple_of(group * STEP_ROWS + at, 2 * SUB), 2 * SUB)
+                gate = gate_ref[rows, lanes].astype(F32)
+                gated_ref[rows, lanes] = (gate * jnp.concatenate(totals, axis=0)).astype(BF16)
+            return tuple(terms)
+
+        lax.fori_loop(0, tok // STEP_ROWS, rows_step, tuple(terms))
         return carry
 
     lax.fori_loop(0, chan // LANE, step, 0)

time: 35.8 us -> 36.2 us (1.011)
  Pallas kernels: 17.5 us -> 18 us
    pallas_call x9, Pallas kernels: 17.5 us -> 18 us  [call(): pl.pallas_call(kernel, out_shape=outs, in_specs=specs, out_specs=[out_spe...]
where the time goes in v8:
time: 36.2 us; the launch traced here: 36 us
  Pallas kernels  18 us (50%)
  starting transfers between devices  12 us (33%)
  waiting for transfers between devices  5.94 us (16%)
    pallas_call x9, Pallas kernels, call(): pl.pallas_call(kernel, out_shape=outs, in_specs=specs, out_specs=[out_spe...  18 us
    all_to_all x1, starting transfers between devices, body(): lax.all_to_all(wire, 'seq', split_axis=0, concat_axis=0, tiled=True, axis...  7.83 us
    ppermute x2, waiting for transfers between devices, to_chips(): lax.ppermute(each, 'tp', [(rank, (rank + 2 * hop) % tp) for rank in rever...  3.97 us
    ppermute x2, starting transfers between devices, to_chips(): lax.ppermute(each, 'tp', [(rank, (rank + 2 * hop) % tp) for rank in rever...  2.95 us
    ppermute x2, waiting for transfers between devices, body(): halves = [lax.ppermute(each, 'tp', cores) for each in halves]  1.4 us
  transfers between devices with their start and end apart: 7, of which 6 were waited for; matrix products, arithmetic and copies ran while one was open for 0% of the time, Pallas kernels for 33%

profile of v8, /device:TPU:0, one launch (start us, length us, event | category | flops | bytes accessed | tf_op | source)
XLA Modules:
  0.0 36.0 jit_solution(6337659468244299368)
XLA Ops:
  0.0 3.1 %shard_map.64 = bf16[8,16,1024]{2,1,0:T(8,128)(2,1)} custom-call(bf16[256,1024]{1,0:T(8,128)(2,1)} %values_hbm.3, f32[16,1024]{1,0:T(8,128)} %rates_hbm.3), custom_call_target="tpu_custom_call" | custom-call | tf_op jit(solution)/shard_map/pallas_call | solution.py:366
  3.1 7.8 %all-to-all-start = ((bf16[8,16,1024]{2,1,0:T(8,128)(2,1)}), bf16[8,16,1024]{2,1,0:T(8,128)(2,1)S(1)}, u32[]{:S(2)}, u32[]{:S(2)}) async-start(bf16[8,16,1024]{2,1,0:T(8,128)(2,1)} %shard_map.64), calls=%async_computation | async-start | bytes 524288 | tf_op jit(solution)/shard_map/all_to_all | solution.py:398
  10.9 6.0 %shard_map.65 = (f32[256,1024]{1,0:T(8,128)S(1)}, f32[128,1024]{1,0:T(8,128)S(1)}, f32[16,1024]{1,0:T(8,128)S(1)}, f32[16,1024]{1,0:T(8,128)S(1)}, bf16[256,1024...) custom-call(bf16[256,1024]{1,0:T(8,128)(2,1)} %values_hbm.3, ...), custom_call_target="tpu_custom_call" | custom-call | tf_op jit(solution)/shard_map/pallas_call | solution.py:366
  17.0 0.5 %all-to-all-done.states_ref = bf16[8,16,1024]{2,1,0:T(8,128)(2,1)S(1)} async-done(((bf16[8,16,1024]{2,1,0:T(8,128)(2,1)}), bf16[8,16,1024]{2,1,0:T(8,128)(2,1)S(1)}, u32[]{:S(2)}, u32[]{:S(2)}) %all-to-all-start) | async-done | bytes 262176 | tf_op jit(solution)/shard_map/all_to_all | solution.py:398
  17.5 2.2 %shard_map.66 = (bf16[256,1024]{1,0:T(8,128)(2,1)S(1)}, bf16[256,256]{1,0:T(8,128)(2,1)S(1)}) custom-call(bf16[8,16,1024]{2,1,0:T(8,128)(2,1)S(1)} %all-to-all-done.states_ref, f32[256,1024]{1,0:T(8,128)S(1)} %get-tuple-element.22.near_ref, f32[128,1024]{1,0:T(8,128)S(1)} %get-tuple-element.23.reach_ref, f32[16,1024]{1,0:T(8,128)S(1)} %get-tuple-element.24.decay_ref, ...), custom_call_target="tpu_custom_call" | custom-call | flops 8589934592 | tf_op jit(solution)/shard_map/pallas_call | solution.py:366
  19.7 0.1 collective-permute-start.1
  19.7 0.0 copy-done.1
  19.7 0.7 %shard_map.67 = (f32[256,256]{1,0:T(8,128)S(1)}, bf16[256,768]{1,0:T(8,128)(2,1)S(1)}) custom-call(bf16[256,1024]{1,0:T(8,128)(2,1)S(1)} %get-tuple-element.28.gated_ref, bf16[1024,256]{1,0:T(8,128)(2,1)S(1)} %get-tuple-element.30.kept_weight, bf16[1024,768]{1,0:T(8,128)(2,1)S(1)} %copy-done.1), custom_call_target="tpu_custom_call" | custom-call | tf_op jit(solution)/shard_map/pallas_call | solution.py:366
  20.5 0.6 %collective-permute-start = (bf16[256,768]{1,0:T(8,128)(2,1)S(1)}, bf16[256,768]{1,0:T(8,128)(2,1)S(1)}, u32[]{:S(2)}, u32[]{:S(2)}) collective-permute-start(bf16[256,768]{1,0:T(8,128)(2,1)S(1)} %get-tuple-element.32), channel_id=1, source_target_pairs={{0,1},{1,0},{2,3},{3,2},{4,5},{5,4},{6,7},{7,6},{8,9},{9,8},{10,11... | collective-permute-start | bytes 1179656 | tf_op jit(solution)/shard_map/ppermute | solution.py:451
  21.0 0.1 collective-permute-done.1.moved_ref
  21.1 1.6 %collective-permute-start.2 = (bf16[256,256]{1,0:T(8,128)(2,1)S(1)}, bf16[256,256]{1,0:T(8,128)(2,1)S(1)}, u32[]{:S(2)}, u32[]{:S(2)}) collective-permute-start(bf16[256,256]{1,0:T(8,128)(2,1)S(1)} %shard_map.68.after_ref), channel_id=1, source_target_pairs={{3,1},{2,0},{1,3},{0,2},{7,5},{6,4},{5,7},{4,6},{11,9},{10,8},{9,1... | collective-permute-start | bytes 393224 | tf_op jit(solution)/shard_map/ppermute | solution.py:455
  22.7 0.0 collective-permute-done.moved_ref
  22.7 0.0 copy-done
  22.7 0.6 %shard_map.69.refs_0_ = bf16[256,768]{1,0:T(8,128)(2,1)S(1)} custom-call(bf16[256,1024]{1,0:T(8,128)(2,1)S(1)} %get-tuple-element.28.gated_ref, bf16[1024,768]{1,0:T(8,128)(2,1)S(1)} %copy-done, bf16[256,768]{1,0:T(8,128)(2,1)S(1)} %collective-permute-done.moved_ref, bf16[256,256]{1,0:T(8,128)(2,1)S(1)} %shard_map.68.after_ref), custom_call_target="tpu_custom_call" | custom-call | tf_op jit(solution)/shard_map/pallas_call | solution.py:366
  23.3 1.4 %collective-permute-start.5 = (bf16[256,768]{1,0:T(8,128)(2,1)S(1)}, bf16[256,768]{1,0:T(8,128)(2,1)S(1)}, u32[]{:S(2)}, u32[]{:S(2)}) collective-permute-start(bf16[256,768]{1,0:T(8,128)(2,1)S(1)} %shard_map.69.refs_0_), channel_id=1, source_target_pairs={{3,1},{2,0},{1,3},{0,2},{7,5},{6,4},{5,7},{4,6},{11,9},{10,8},{9,1... | collective-permute-start | bytes 1179656 | tf_op jit(solution)/shard_map/ppermute | solution.py:455
  24.6 2.8 %collective-permute-done.2.refs_1_.refs_0_ = bf16[256,256]{1,0:T(8,128)(2,1)S(1)} collective-permute-done((bf16[256,256]{1,0:T(8,128)(2,1)S(1)}, bf16[256,256]{1,0:T(8,128)(2,1)S(1)}, u32[]{:S(2)}, u32[]{:S(2)}) %collective-permute-start.2) | collective-permute-done | bytes 131104 | tf_op jit(solution)/shard_map/ppermute | solution.py:455
  27.4 2.3 %shard_map.70 = (bf16[256,512]{1,0:T(8,128)(2,1)S(1)}, bf16[256,512]{1,0:T(8,128)(2,1)S(1)}) custom-call(bf16[256,1024]{1,0:T(8,128)(2,1)S(1)} %get-tuple-element.28.gated_ref, bf16[1024,4096]{1,0:T(8,128)(2,1)} %weight_hbm.5, bf16[256,768]{1,0:T(8,128)(2,1)S(1)} %shard_map.69.refs_0_, bf16[256,256]{1,0:T(8,128)(2,1)S(1)} %collective-permute-done.2.refs_1_.refs_0_), custom_call_target="tpu_custom_call" | custom-call | flops 8589934592 | tf_op jit(solution)/shard_map/pallas_call | solution.py:366
  29.7 0.1 collective-permute-start.3
  29.8 0.5 %collective-permute-start.4 = (bf16[256,512]{1,0:T(8,128)(2,1)S(1)}, bf16[256,512]{1,0:T(8,128)(2,1)S(1)}, u32[]{:S(2)}, u32[]{:S(2)}) collective-permute-start(bf16[256,512]{1,0:T(8,128)(2,1)S(1)} %get-tuple-element.36), channel_id=1, source_target_pairs={{0,1},{1,0},{2,3},{3,2},{4,5},{5,4},{6,7},{7,6},{8,9},{9,8},{10,11... | collective-permute-start | bytes 786440 | tf_op jit(solution)/shard_map/ppermute | solution.py:471
  30.3 1.0 %collective-permute-done.3.low_ref = bf16[256,512]{1,0:T(8,128)(2,1)S(1)} collective-permute-done((bf16[256,512]{1,0:T(8,128)(2,1)S(1)}, bf16[256,512]{1,0:T(8,128)(2,1)S(1)}, u32[]{:S(2)}, u32[]{:S(2)}) %collective-permute-start.3) | collective-permute-done | bytes 262176 | tf_op jit(solution)/shard_map/ppermute | solution.py:471
  31.3 0.4 %collective-permute-done.4.high_ref = bf16[256,512]{1,0:T(8,128)(2,1)S(1)} collective-permute-done((bf16[256,512]{1,0:T(8,128)(2,1)S(1)}, bf16[256,512]{1,0:T(8,128)(2,1)S(1)}, u32[]{:S(2)}, u32[]{:S(2)}) %collective-permute-start.4) | collective-permute-done | bytes 262176 | tf_op jit(solution)/shard_map/ppermute | solution.py:471
  31.7 2.3 %shard_map.71 = (bf16[256,256]{1,0:T(8,128)(2,1)S(1)}, f32[256,768]{1,0:T(8,128)S(1)}) custom-call(bf16[256,1024]{1,0:T(8,128)(2,1)S(1)} %get-tuple-element.28.gated_ref, bf16[1024,4096]{1,0:T(8,128)(2,1)} %weight_hbm.5, bf16[256,512]{1,0:T(8,128)(2,1)S(1)} %collective-permute-done.3.low_ref, bf16[256,512]{1,0:T(8,128)(2,1)S(1)} %collective-permute-done.4.high_ref, ...), custom_call_target="tpu_custom_call" | custom-call | tf_op jit(solution)/shard_map/pallas_call | solution.py:366
  33.9 1.2 %collective-permute-done.5.refs_0_ = bf16[256,768]{1,0:T(8,128)(2,1)S(1)} collective-permute-done((bf16[256,768]{1,0:T(8,128)(2,1)S(1)}, bf16[256,768]{1,0:T(8,128)(2,1)S(1)}, u32[]{:S(2)}, u32[]{:S(2)}) %collective-permute-start.5) | collective-permute-done | bytes 393248 | tf_op jit(solution)/shard_map/ppermute | solution.py:455
  35.1 0.8 %shard_map.72 = bf16[256,1024]{1,0:T(8,128)(2,1)} custom-call(bf16[256,256]{1,0:T(8,128)(2,1)S(1)} %get-tuple-element.37.first_ref, f32[256,768]{1,0:T(8,128)S(1)} %get-tuple-element.38.own_ref, bf16[256,768]{1,0:T(8,128)(2,1)S(1)} %collective-permute-done.5.refs_0_), custom_call_target="tpu_custom_call" | custom-call | tf_op jit(solution)/shard_map/pallas_call | solution.py:366
  (3 shorter events, 0.0 us)
Async XLA Ops:
  3.1 14.4 %all-to-all-start = ((bf16[8,16,1024]{2,1,0:T(8,128)(2,1)}), bf16[8,16,1024]{2,1,0:T(8,128)(2,1)S(1)}, u32[]{:S(2)}, u32[]{:S(2)}) async-start(bf16[8,16,1024]{2,1,0:T(8,128)(2,1)} %shard_map.64), calls=%async_computation | async-start | bytes 524288 | tf_op jit(solution)/shard_map/all_to_all | solution.py:398
  17.5 2.3 %copy-start.1 = (bf16[1024,768]{1,0:T(8,128)(2,1)S(1)}, bf16[1024,768]{1,0:T(8,128)(2,1)}, u32[]{:S(2)}) copy-start(bf16[1024,768]{1,0:T(8,128)(2,1)} %get-tuple-element.31.sent_weight) | copy-start | bytes 4718596
  19.7 1.4 %collective-permute-start.1 = (bf16[256,256]{1,0:T(8,128)(2,1)S(1)}, bf16[256,256]{1,0:T(8,128)(2,1)S(1)}, u32[]{:S(2)}, u32[]{:S(2)}) collective-permute-start(bf16[256,256]{1,0:T(8,128)(2,1)S(1)} %get-tuple-element.34), channel_id=1, source_target_pairs={{0,1},{1,0},{2,3},{3,2},{4,5},{5,4},{6,7},{7,6},{8,9},{9,8},{10,11... | collective-permute-start | bytes 393224 | tf_op jit(solution)/shard_map/ppermute | solution.py:445
  20.5 2.2 %collective-permute-start = (bf16[256,768]{1,0:T(8,128)(2,1)S(1)}, bf16[256,768]{1,0:T(8,128)(2,1)S(1)}, u32[]{:S(2)}, u32[]{:S(2)}) collective-permute-start(bf16[256,768]{1,0:T(8,128)(2,1)S(1)} %get-tuple-element.32), channel_id=1, source_target_pairs={{0,1},{1,0},{2,3},{3,2},{4,5},{5,4},{6,7},{7,6},{8,9},{9,8},{10,11... | collective-permute-start | bytes 1179656 | tf_op jit(solution)/shard_map/ppermute | solution.py:451
  21.1 1.6 %copy-start = (bf16[1024,768]{1,0:T(8,128)(2,1)S(1)}, bf16[1024,768]{1,0:T(8,128)(2,1)}, u32[]{:S(2)}) copy-start(bf16[1024,768]{1,0:T(8,128)(2,1)} %get-tuple-element.29.weight_ref) | copy-start | bytes 4718596
  21.1 6.3 %collective-permute-start.2 = (bf16[256,256]{1,0:T(8,128)(2,1)S(1)}, bf16[256,256]{1,0:T(8,128)(2,1)S(1)}, u32[]{:S(2)}, u32[]{:S(2)}) collective-permute-start(bf16[256,256]{1,0:T(8,128)(2,1)S(1)} %shard_map.68.after_ref), channel_id=1, source_target_pairs={{3,1},{2,0},{1,3},{0,2},{7,5},{6,4},{5,7},{4,6},{11,9},{10,8},{9,1... | collective-permute-start | bytes 393224 | tf_op jit(solution)/shard_map/ppermute | solution.py:455
  23.3 11.9 %collective-permute-start.5 = (bf16[256,768]{1,0:T(8,128)(2,1)S(1)}, bf16[256,768]{1,0:T(8,128)(2,1)S(1)}, u32[]{:S(2)}, u32[]{:S(2)}) collective-permute-start(bf16[256,768]{1,0:T(8,128)(2,1)S(1)} %shard_map.69.refs_0_), channel_id=1, source_target_pairs={{3,1},{2,0},{1,3},{0,2},{7,5},{6,4},{5,7},{4,6},{11,9},{10,8},{9,1... | collective-permute-start | bytes 1179656 | tf_op jit(solution)/shard_map/ppermute | solution.py:455
  29.7 1.6 %collective-permute-start.3 = (bf16[256,512]{1,0:T(8,128)(2,1)S(1)}, bf16[256,512]{1,0:T(8,128)(2,1)S(1)}, u32[]{:S(2)}, u32[]{:S(2)}) collective-permute-start(bf16[256,512]{1,0:T(8,128)(2,1)S(1)} %get-tuple-element.35), channel_id=1, source_target_pairs={{0,1},{1,0},{2,3},{3,2},{4,5},{5,4},{6,7},{7,6},{8,9},{9,8},{10,11... | collective-permute-start | bytes 786440 | tf_op jit(solution)/shard_map/ppermute | solution.py:471
  29.8 1.9 %collective-permute-start.4 = (bf16[256,512]{1,0:T(8,128)(2,1)S(1)}, bf16[256,512]{1,0:T(8,128)(2,1)S(1)}, u32[]{:S(2)}, u32[]{:S(2)}) collective-permute-start(bf16[256,512]{1,0:T(8,128)(2,1)S(1)} %get-tuple-element.36), channel_id=1, source_target_pairs={{0,1},{1,0},{2,3},{3,2},{4,5},{5,4},{6,7},{7,6},{8,9},{9,8},{10,11... | collective-permute-start | bytes 786440 | tf_op jit(solution)/shard_map/ppermute | solution.py:471

commit v9 on v6

--- a/solution.py
+++ b/solution.py
@@ -75,7 +75,7 @@
 
 
 def group_order(count):
-    return [(count // 2 + at) % count for at in range(count)]
+    return [(count // 2 + 1 + at) % count for at in range(count)]
 
 
 def wait_all(copies):

time: 35.8 us -> 36.5 us (1.020)
  starting transfers between devices: 12 us -> 12.4 us
    all_to_all x1, starting transfers between devices: 7.83 us -> 8.3 us  [body(): lax.all_to_all(wire, 'seq', split_axis=0, concat_axis=0, tiled=True, axis...]
where the time goes in v9:
time: 36.5 us; the launch traced here: 36.2 us
  Pallas kernels  17.5 us (48%)
  starting transfers between devices  12.4 us (34%)
  waiting for transfers between devices  6.2 us (17%)
    pallas_call x9, Pallas kernels, call(): pl.pallas_call(kernel, out_shape=outs, in_specs=specs, out_specs=[out_spe...  17.5 us
    all_to_all x1, starting transfers between devices, body(): lax.all_to_all(wire, 'seq', split_axis=0, concat_axis=0, tiled=True, axis...  8.3 us
    ppermute x2, waiting for transfers between devices, to_chips(): lax.ppermute(each, 'tp', [(rank, (rank + 2 * hop) % tp) for rank in rever...  3.97 us
    ppermute x2, starting transfers between devices, to_chips(): lax.ppermute(each, 'tp', [(rank, (rank + 2 * hop) % tp) for rank in rever...  2.95 us
    ppermute x2, waiting for transfers between devices, body(): halves = [lax.ppermute(each, 'tp', cores) for each in halves]  1.4 us
    all_to_all x1, waiting for transfers between devices, body(): lax.all_to_all(wire, 'seq', split_axis=0, concat_axis=0, tiled=True, axis...  0.77 us
  transfers between devices with their start and end apart: 7, of which 6 were waited for; matrix products, arithmetic and copies ran while one was open for 0% of the time, Pallas kernels for 33%

profile of v9, /device:TPU:0, one launch (start us, length us, event | category | flops | bytes accessed | tf_op | source)
XLA Modules:
  0.0 36.2 jit_solution(9433098545425125459)
XLA Ops:
  0.0 3.1 %shard_map.64 = bf16[8,16,1024]{2,1,0:T(8,128)(2,1)} custom-call(bf16[256,1024]{1,0:T(8,128)(2,1)} %values_hbm.3, f32[16,1024]{1,0:T(8,128)} %rates_hbm.3), custom_call_target="tpu_custom_call" | custom-call | tf_op jit(solution)/shard_map/pallas_call | solution.py:359
  3.1 8.3 %all-to-all-start = ((bf16[8,16,1024]{2,1,0:T(8,128)(2,1)}), bf16[8,16,1024]{2,1,0:T(8,128)(2,1)S(1)}, u32[]{:S(2)}, u32[]{:S(2)}) async-start(bf16[8,16,1024]{2,1,0:T(8,128)(2,1)} %shard_map.64), calls=%async_computation | async-start | bytes 524288 | tf_op jit(solution)/shard_map/all_to_all | solution.py:391
  11.4 6.0 %shard_map.65 = (f32[256,1024]{1,0:T(8,128)S(1)}, f32[128,1024]{1,0:T(8,128)S(1)}, f32[16,1024]{1,0:T(8,128)S(1)}, f32[16,1024]{1,0:T(8,128)S(1)}, bf16[256,1024...) custom-call(bf16[256,1024]{1,0:T(8,128)(2,1)} %values_hbm.3, ...), custom_call_target="tpu_custom_call" | custom-call | tf_op jit(solution)/shard_map/pallas_call | solution.py:359
  17.5 0.8 %all-to-all-done.states_ref = bf16[8,16,1024]{2,1,0:T(8,128)(2,1)S(1)} async-done(((bf16[8,16,1024]{2,1,0:T(8,128)(2,1)}), bf16[8,16,1024]{2,1,0:T(8,128)(2,1)S(1)}, u32[]{:S(2)}, u32[]{:S(2)}) %all-to-all-start) | async-done | bytes 262176 | tf_op jit(solution)/shard_map/all_to_all | solution.py:391
  18.2 1.7 %shard_map.66 = (bf16[256,1024]{1,0:T(8,128)(2,1)S(1)}, bf16[256,256]{1,0:T(8,128)(2,1)S(1)}) custom-call(bf16[8,16,1024]{2,1,0:T(8,128)(2,1)S(1)} %all-to-all-done.states_ref, f32[256,1024]{1,0:T(8,128)S(1)} %get-tuple-element.22.near_ref, f32[128,1024]{1,0:T(8,128)S(1)} %get-tuple-element.23.reach_ref, f32[16,1024]{1,0:T(8,128)S(1)} %get-tuple-element.24.decay_ref, ...), custom_call_target="tpu_custom_call" | custom-call | flops 8589934592 | tf_op jit(solution)/shard_map/pallas_call | solution.py:359
  19.9 0.1 collective-permute-start.1
  20.0 0.0 copy-done.1
  20.0 0.7 %shard_map.67 = (f32[256,256]{1,0:T(8,128)S(1)}, bf16[256,768]{1,0:T(8,128)(2,1)S(1)}) custom-call(bf16[256,1024]{1,0:T(8,128)(2,1)S(1)} %get-tuple-element.28.gated_ref, bf16[1024,256]{1,0:T(8,128)(2,1)S(1)} %get-tuple-element.30.kept_weight, bf16[1024,768]{1,0:T(8,128)(2,1)S(1)} %copy-done.1), custom_call_target="tpu_custom_call" | custom-call | tf_op jit(solution)/shard_map/pallas_call | solution.py:359
  20.7 0.6 %collective-permute-start = (bf16[256,768]{1,0:T(8,128)(2,1)S(1)}, bf16[256,768]{1,0:T(8,128)(2,1)S(1)}, u32[]{:S(2)}, u32[]{:S(2)}) collective-permute-start(bf16[256,768]{1,0:T(8,128)(2,1)S(1)} %get-tuple-element.32), channel_id=1, source_target_pairs={{0,1},{1,0},{2,3},{3,2},{4,5},{5,4},{6,7},{7,6},{8,9},{9,8},{10,11... | collective-permute-start | bytes 1179656 | tf_op jit(solution)/shard_map/ppermute | solution.py:444
  21.3 0.1 collective-permute-done.1.moved_ref
  21.4 1.6 %collective-permute-start.2 = (bf16[256,256]{1,0:T(8,128)(2,1)S(1)}, bf16[256,256]{1,0:T(8,128)(2,1)S(1)}, u32[]{:S(2)}, u32[]{:S(2)}) collective-permute-start(bf16[256,256]{1,0:T(8,128)(2,1)S(1)} %shard_map.68.after_ref), channel_id=1, source_target_pairs={{3,1},{2,0},{1,3},{0,2},{7,5},{6,4},{5,7},{4,6},{11,9},{10,8},{9,1... | collective-permute-start | bytes 393224 | tf_op jit(solution)/shard_map/ppermute | solution.py:448
  23.0 0.0 collective-permute-done.moved_ref
  23.0 0.0 copy-done
  23.0 0.6 %shard_map.69.refs_0_ = bf16[256,768]{1,0:T(8,128)(2,1)S(1)} custom-call(bf16[256,1024]{1,0:T(8,128)(2,1)S(1)} %get-tuple-element.28.gated_ref, bf16[1024,768]{1,0:T(8,128)(2,1)S(1)} %copy-done, bf16[256,768]{1,0:T(8,128)(2,1)S(1)} %collective-permute-done.moved_ref, bf16[256,256]{1,0:T(8,128)(2,1)S(1)} %shard_map.68.after_ref), custom_call_target="tpu_custom_call" | custom-call | tf_op jit(solution)/shard_map/pallas_call | solution.py:359
  23.6 1.4 %collective-permute-start.5 = (bf16[256,768]{1,0:T(8,128)(2,1)S(1)}, bf16[256,768]{1,0:T(8,128)(2,1)S(1)}, u32[]{:S(2)}, u32[]{:S(2)}) collective-permute-start(bf16[256,768]{1,0:T(8,128)(2,1)S(1)} %shard_map.69.refs_0_), channel_id=1, source_target_pairs={{3,1},{2,0},{1,3},{0,2},{7,5},{6,4},{5,7},{4,6},{11,9},{10,8},{9,1... | collective-permute-start | bytes 1179656 | tf_op jit(solution)/shard_map/ppermute | solution.py:448
  24.9 2.8 %collective-permute-done.2.refs_1_.refs_0_ = bf16[256,256]{1,0:T(8,128)(2,1)S(1)} collective-permute-done((bf16[256,256]{1,0:T(8,128)(2,1)S(1)}, bf16[256,256]{1,0:T(8,128)(2,1)S(1)}, u32[]{:S(2)}, u32[]{:S(2)}) %collective-permute-start.2) | collective-permute-done | bytes 131104 | tf_op jit(solution)/shard_map/ppermute | solution.py:448
  27.7 2.3 %shard_map.70 = (bf16[256,512]{1,0:T(8,128)(2,1)S(1)}, bf16[256,512]{1,0:T(8,128)(2,1)S(1)}) custom-call(bf16[256,1024]{1,0:T(8,128)(2,1)S(1)} %get-tuple-element.28.gated_ref, bf16[1024,4096]{1,0:T(8,128)(2,1)} %weight_hbm.5, bf16[256,768]{1,0:T(8,128)(2,1)S(1)} %shard_map.69.refs_0_, bf16[256,256]{1,0:T(8,128)(2,1)S(1)} %collective-permute-done.2.refs_1_.refs_0_), custom_call_target="tpu_custom_call" | custom-call | flops 8589934592 | tf_op jit(solution)/shard_map/pallas_call | solution.py:359
  30.0 0.1 collective-permute-start.3
  30.0 0.5 %collective-permute-start.4 = (bf16[256,512]{1,0:T(8,128)(2,1)S(1)}, bf16[256,512]{1,0:T(8,128)(2,1)S(1)}, u32[]{:S(2)}, u32[]{:S(2)}) collective-permute-start(bf16[256,512]{1,0:T(8,128)(2,1)S(1)} %get-tuple-element.36), channel_id=1, source_target_pairs={{0,1},{1,0},{2,3},{3,2},{4,5},{5,4},{6,7},{7,6},{8,9},{9,8},{10,11... | collective-permute-start | bytes 786440 | tf_op jit(solution)/shard_map/ppermute | solution.py:464
  30.5 1.0 %collective-permute-done.3.low_ref = bf16[256,512]{1,0:T(8,128)(2,1)S(1)} collective-permute-done((bf16[256,512]{1,0:T(8,128)(2,1)S(1)}, bf16[256,512]{1,0:T(8,128)(2,1)S(1)}, u32[]{:S(2)}, u32[]{:S(2)}) %collective-permute-start.3) | collective-permute-done | bytes 262176 | tf_op jit(solution)/shard_map/ppermute | solution.py:464
  31.6 0.4 %collective-permute-done.4.high_ref = bf16[256,512]{1,0:T(8,128)(2,1)S(1)} collective-permute-done((bf16[256,512]{1,0:T(8,128)(2,1)S(1)}, bf16[256,512]{1,0:T(8,128)(2,1)S(1)}, u32[]{:S(2)}, u32[]{:S(2)}) %collective-permute-start.4) | collective-permute-done | bytes 262176 | tf_op jit(solution)/shard_map/ppermute | solution.py:464
  31.9 2.3 %shard_map.71 = (bf16[256,256]{1,0:T(8,128)(2,1)S(1)}, f32[256,768]{1,0:T(8,128)S(1)}) custom-call(bf16[256,1024]{1,0:T(8,128)(2,1)S(1)} %get-tuple-element.28.gated_ref, bf16[1024,4096]{1,0:T(8,128)(2,1)} %weight_hbm.5, bf16[256,512]{1,0:T(8,128)(2,1)S(1)} %collective-permute-done.3.low_ref, bf16[256,512]{1,0:T(8,128)(2,1)S(1)} %collective-permute-done.4.high_ref, ...), custom_call_target="tpu_custom_call" | custom-call | tf_op jit(solution)/shard_map/pallas_call | solution.py:359
  34.2 1.2 %collective-permute-done.5.refs_0_ = bf16[256,768]{1,0:T(8,128)(2,1)S(1)} collective-permute-done((bf16[256,768]{1,0:T(8,128)(2,1)S(1)}, bf16[256,768]{1,0:T(8,128)(2,1)S(1)}, u32[]{:S(2)}, u32[]{:S(2)}) %collective-permute-start.5) | collective-permute-done | bytes 393248 | tf_op jit(solution)/shard_map/ppermute | solution.py:448
  35.4 0.8 %shard_map.72 = bf16[256,1024]{1,0:T(8,128)(2,1)} custom-call(bf16[256,256]{1,0:T(8,128)(2,1)S(1)} %get-tuple-element.37.first_ref, f32[256,768]{1,0:T(8,128)S(1)} %get-tuple-element.38.own_ref, bf16[256,768]{1,0:T(8,128)(2,1)S(1)} %collective-permute-done.5.refs_0_), custom_call_target="tpu_custom_call" | custom-call | tf_op jit(solution)/shard_map/pallas_call | solution.py:359
  (3 shorter events, 0.0 us)
Async XLA Ops:
  3.1 15.1 %all-to-all-start = ((bf16[8,16,1024]{2,1,0:T(8,128)(2,1)}), bf16[8,16,1024]{2,1,0:T(8,128)(2,1)S(1)}, u32[]{:S(2)}, u32[]{:S(2)}) async-start(bf16[8,16,1024]{2,1,0:T(8,128)(2,1)} %shard_map.64), calls=%async_computation | async-start | bytes 524288 | tf_op jit(solution)/shard_map/all_to_all | solution.py:391
  18.2 1.8 %copy-start.1 = (bf16[1024,768]{1,0:T(8,128)(2,1)S(1)}, bf16[1024,768]{1,0:T(8,128)(2,1)}, u32[]{:S(2)}) copy-start(bf16[1024,768]{1,0:T(8,128)(2,1)} %get-tuple-element.31.sent_weight) | copy-start | bytes 4718596
  19.9 1.4 %collective-permute-start.1 = (bf16[256,256]{1,0:T(8,128)(2,1)S(1)}, bf16[256,256]{1,0:T(8,128)(2,1)S(1)}, u32[]{:S(2)}, u32[]{:S(2)}) collective-permute-start(bf16[256,256]{1,0:T(8,128)(2,1)S(1)} %get-tuple-element.34), channel_id=1, source_target_pairs={{0,1},{1,0},{2,3},{3,2},{4,5},{5,4},{6,7},{7,6},{8,9},{9,8},{10,11... | collective-permute-start | bytes 393224 | tf_op jit(solution)/shard_map/ppermute | solution.py:438
  20.7 2.2 %collective-permute-start = (bf16[256,768]{1,0:T(8,128)(2,1)S(1)}, bf16[256,768]{1,0:T(8,128)(2,1)S(1)}, u32[]{:S(2)}, u32[]{:S(2)}) collective-permute-start(bf16[256,768]{1,0:T(8,128)(2,1)S(1)} %get-tuple-element.32), channel_id=1, source_target_pairs={{0,1},{1,0},{2,3},{3,2},{4,5},{5,4},{6,7},{7,6},{8,9},{9,8},{10,11... | collective-permute-start | bytes 1179656 | tf_op jit(solution)/shard_map/ppermute | solution.py:444
  21.3 1.6 %copy-start = (bf16[1024,768]{1,0:T(8,128)(2,1)S(1)}, bf16[1024,768]{1,0:T(8,128)(2,1)}, u32[]{:S(2)}) copy-start(bf16[1024,768]{1,0:T(8,128)(2,1)} %get-tuple-element.29.weight_ref) | copy-start | bytes 4718596
  21.4 6.3 %collective-permute-start.2 = (bf16[256,256]{1,0:T(8,128)(2,1)S(1)}, bf16[256,256]{1,0:T(8,128)(2,1)S(1)}, u32[]{:S(2)}, u32[]{:S(2)}) collective-permute-start(bf16[256,256]{1,0:T(8,128)(2,1)S(1)} %shard_map.68.after_ref), channel_id=1, source_target_pairs={{3,1},{2,0},{1,3},{0,2},{7,5},{6,4},{5,7},{4,6},{11,9},{10,8},{9,1... | collective-permute-start | bytes 393224 | tf_op jit(solution)/shard_map/ppermute | solution.py:448
  23.6 11.9 %collective-permute-start.5 = (bf16[256,768]{1,0:T(8,128)(2,1)S(1)}, bf16[256,768]{1,0:T(8,128)(2,1)S(1)}, u32[]{:S(2)}, u32[]{:S(2)}) collective-permute-start(bf16[256,768]{1,0:T(8,128)(2,1)S(1)} %shard_map.69.refs_0_), channel_id=1, source_target_pairs={{3,1},{2,0},{1,3},{0,2},{7,5},{6,4},{5,7},{4,6},{11,9},{10,8},{9,1... | collective-permute-start | bytes 1179656 | tf_op jit(solution)/shard_map/ppermute | solution.py:448
  30.0 1.6 %collective-permute-start.3 = (bf16[256,512]{1,0:T(8,128)(2,1)S(1)}, bf16[256,512]{1,0:T(8,128)(2,1)S(1)}, u32[]{:S(2)}, u32[]{:S(2)}) collective-permute-start(bf16[256,512]{1,0:T(8,128)(2,1)S(1)} %get-tuple-element.35), channel_id=1, source_target_pairs={{0,1},{1,0},{2,3},{3,2},{4,5},{5,4},{6,7},{7,6},{8,9},{9,8},{10,11... | collective-permute-start | bytes 786440 | tf_op jit(solution)/shard_map/ppermute | solution.py:464
  30.0 1.9 %collective-permute-start.4 = (bf16[256,512]{1,0:T(8,128)(2,1)S(1)}, bf16[256,512]{1,0:T(8,128)(2,1)S(1)}, u32[]{:S(2)}, u32[]{:S(2)}) collective-permute-start(bf16[256,512]{1,0:T(8,128)(2,1)S(1)} %get-tuple-element.36), channel_id=1, source_target_pairs={{0,1},{1,0},{2,3},{3,2},{4,5},{5,4},{6,7},{7,6},{8,9},{9,8},{10,11... | collective-permute-start | bytes 786440 | tf_op jit(solution)/shard_map/ppermute | solution.py:464

commit v10 on v6

--- a/solution.py
+++ b/solution.py
@@ -215,7 +215,7 @@
                     total = total + terms[mode]
                 terms = [terms[mode] * decays[mode] for mode in range(modes)]
                 order_ref[pl.ds(block * SUB + at, SUB, stride=run), :] = total
-        near_ref[:, lanes] = order_ref[...]
+        near_ref[:, lanes] = order_ref[:tok, :]
         decay_ref[:, lanes] = jnp.exp(-float(SUB) * rates)
         far_ref[:, lanes] = jnp.exp(-float(tok) * rates)
         return carry
@@ -419,7 +419,7 @@
             here((SUB, LANE), F32),
             here((modes * SUB, LANE), F32),
             here((tok // SUB // SUB, modes * SUB, LANE), F32),
-            here((tok, LANE), F32),
+            here((tok + tok // SUB, LANE), F32),
             here((chan, away * wide), BF16),
             here((chan, away * wide), BF16),
             pltpu.SemaphoreType.DMA((len(sources),)),

time: 35.8 us -> 35.8 us (level)
  no operation moved by 1% of the time
where the time goes in v10:
time: 35.8 us; the launch traced here: 35.5 us
  Pallas kernels  17.5 us (49%)
  starting transfers between devices  12 us (34%)
  waiting for transfers between devices  5.94 us (17%)
    pallas_call x9, Pallas kernels, call(): pl.pallas_call(kernel, out_shape=outs, in_specs=specs, out_specs=[out_spe...  17.5 us
    all_to_all x1, starting transfers between devices, body(): lax.all_to_all(wire, 'seq', split_axis=0, concat_axis=0, tiled=True, axis...  7.83 us
    ppermute x2, waiting for transfers between devices, to_chips(): lax.ppermute(each, 'tp', [(rank, (rank + 2 * hop) % tp) for rank in rever...  3.97 us
    ppermute x2, starting transfers between devices, to_chips(): lax.ppermute(each, 'tp', [(rank, (rank + 2 * hop) % tp) for rank in rever...  2.96 us
    ppermute x2, waiting for transfers between devices, body(): halves = [lax.ppermute(each, 'tp', cores) for each in halves]  1.4 us
  transfers between devices with their start and end apart: 7, of which 6 were waited for; matrix products, arithmetic and copies ran while one was open for 0% of the time, Pallas kernels for 33%

profile of v10, /device:TPU:0, one launch (start us, length us, event | category | flops | bytes accessed | tf_op | source)
XLA Modules:
  0.0 35.5 jit_solution(3950252501606261409)
XLA Ops:
  0.0 3.1 %shard_map.64 = bf16[8,16,1024]{2,1,0:T(8,128)(2,1)} custom-call(bf16[256,1024]{1,0:T(8,128)(2,1)} %values_hbm.3, f32[16,1024]{1,0:T(8,128)} %rates_hbm.3), custom_call_target="tpu_custom_call" | custom-call | tf_op jit(solution)/shard_map/pallas_call | solution.py:359
  3.1 7.8 %all-to-all-start = ((bf16[8,16,1024]{2,1,0:T(8,128)(2,1)}), bf16[8,16,1024]{2,1,0:T(8,128)(2,1)S(1)}, u32[]{:S(2)}, u32[]{:S(2)}) async-start(bf16[8,16,1024]{2,1,0:T(8,128)(2,1)} %shard_map.64), calls=%async_computation | async-start | bytes 524288 | tf_op jit(solution)/shard_map/all_to_all | solution.py:391
  10.9 6.0 %shard_map.65 = (f32[256,1024]{1,0:T(8,128)S(1)}, f32[128,1024]{1,0:T(8,128)S(1)}, f32[16,1024]{1,0:T(8,128)S(1)}, f32[16,1024]{1,0:T(8,128)S(1)}, bf16[256,1024...) custom-call(bf16[256,1024]{1,0:T(8,128)(2,1)} %values_hbm.3, ...), custom_call_target="tpu_custom_call" | custom-call | tf_op jit(solution)/shard_map/pallas_call | solution.py:359
  17.0 0.5 %all-to-all-done.states_ref = bf16[8,16,1024]{2,1,0:T(8,128)(2,1)S(1)} async-done(((bf16[8,16,1024]{2,1,0:T(8,128)(2,1)}), bf16[8,16,1024]{2,1,0:T(8,128)(2,1)S(1)}, u32[]{:S(2)}, u32[]{:S(2)}) %all-to-all-start) | async-done | bytes 262176 | tf_op jit(solution)/shard_map/all_to_all | solution.py:391
  17.5 1.7 %shard_map.66 = (bf16[256,1024]{1,0:T(8,128)(2,1)S(1)}, bf16[256,256]{1,0:T(8,128)(2,1)S(1)}) custom-call(bf16[8,16,1024]{2,1,0:T(8,128)(2,1)S(1)} %all-to-all-done.states_ref, f32[256,1024]{1,0:T(8,128)S(1)} %get-tuple-element.22.near_ref, f32[128,1024]{1,0:T(8,128)S(1)} %get-tuple-element.23.reach_ref, f32[16,1024]{1,0:T(8,128)S(1)} %get-tuple-element.24.decay_ref, ...), custom_call_target="tpu_custom_call" | custom-call | flops 8589934592 | tf_op jit(solution)/shard_map/pallas_call | solution.py:359
  19.2 0.1 collective-permute-start.1
  19.3 0.0 copy-done.1
  19.3 0.7 %shard_map.67 = (f32[256,256]{1,0:T(8,128)S(1)}, bf16[256,768]{1,0:T(8,128)(2,1)S(1)}) custom-call(bf16[256,1024]{1,0:T(8,128)(2,1)S(1)} %get-tuple-element.28.gated_ref, bf16[1024,256]{1,0:T(8,128)(2,1)S(1)} %get-tuple-element.30.kept_weight, bf16[1024,768]{1,0:T(8,128)(2,1)S(1)} %copy-done.1), custom_call_target="tpu_custom_call" | custom-call | tf_op jit(solution)/shard_map/pallas_call | solution.py:359
  20.0 0.6 %collective-permute-start = (bf16[256,768]{1,0:T(8,128)(2,1)S(1)}, bf16[256,768]{1,0:T(8,128)(2,1)S(1)}, u32[]{:S(2)}, u32[]{:S(2)}) collective-permute-start(bf16[256,768]{1,0:T(8,128)(2,1)S(1)} %get-tuple-element.32), channel_id=1, source_target_pairs={{0,1},{1,0},{2,3},{3,2},{4,5},{5,4},{6,7},{7,6},{8,9},{9,8},{10,11... | collective-permute-start | bytes 1179656 | tf_op jit(solution)/shard_map/ppermute | solution.py:444
  20.6 0.1 collective-permute-done.1.moved_ref
  20.6 1.6 %collective-permute-start.2 = (bf16[256,256]{1,0:T(8,128)(2,1)S(1)}, bf16[256,256]{1,0:T(8,128)(2,1)S(1)}, u32[]{:S(2)}, u32[]{:S(2)}) collective-permute-start(bf16[256,256]{1,0:T(8,128)(2,1)S(1)} %shard_map.68.after_ref), channel_id=1, source_target_pairs={{3,1},{2,0},{1,3},{0,2},{7,5},{6,4},{5,7},{4,6},{11,9},{10,8},{9,1... | collective-permute-start | bytes 393224 | tf_op jit(solution)/shard_map/ppermute | solution.py:448
  22.2 0.0 collective-permute-done.moved_ref
  22.2 0.0 copy-done
  22.2 0.6 %shard_map.69.refs_0_ = bf16[256,768]{1,0:T(8,128)(2,1)S(1)} custom-call(bf16[256,1024]{1,0:T(8,128)(2,1)S(1)} %get-tuple-element.28.gated_ref, bf16[1024,768]{1,0:T(8,128)(2,1)S(1)} %copy-done, bf16[256,768]{1,0:T(8,128)(2,1)S(1)} %collective-permute-done.moved_ref, bf16[256,256]{1,0:T(8,128)(2,1)S(1)} %shard_map.68.after_ref), custom_call_target="tpu_custom_call" | custom-call | tf_op jit(solution)/shard_map/pallas_call | solution.py:359
  22.8 1.4 %collective-permute-start.5 = (bf16[256,768]{1,0:T(8,128)(2,1)S(1)}, bf16[256,768]{1,0:T(8,128)(2,1)S(1)}, u32[]{:S(2)}, u32[]{:S(2)}) collective-permute-start(bf16[256,768]{1,0:T(8,128)(2,1)S(1)} %shard_map.69.refs_0_), channel_id=1, source_target_pairs={{3,1},{2,0},{1,3},{0,2},{7,5},{6,4},{5,7},{4,6},{11,9},{10,8},{9,1... | collective-permute-start | bytes 1179656 | tf_op jit(solution)/shard_map/ppermute | solution.py:448
  24.2 2.8 %collective-permute-done.2.refs_1_.refs_0_ = bf16[256,256]{1,0:T(8,128)(2,1)S(1)} collective-permute-done((bf16[256,256]{1,0:T(8,128)(2,1)S(1)}, bf16[256,256]{1,0:T(8,128)(2,1)S(1)}, u32[]{:S(2)}, u32[]{:S(2)}) %collective-permute-start.2) | collective-permute-done | bytes 131104 | tf_op jit(solution)/shard_map/ppermute | solution.py:448
  27.0 2.3 %shard_map.70 = (bf16[256,512]{1,0:T(8,128)(2,1)S(1)}, bf16[256,512]{1,0:T(8,128)(2,1)S(1)}) custom-call(bf16[256,1024]{1,0:T(8,128)(2,1)S(1)} %get-tuple-element.28.gated_ref, bf16[1024,4096]{1,0:T(8,128)(2,1)} %weight_hbm.5, bf16[256,768]{1,0:T(8,128)(2,1)S(1)} %shard_map.69.refs_0_, bf16[256,256]{1,0:T(8,128)(2,1)S(1)} %collective-permute-done.2.refs_1_.refs_0_), custom_call_target="tpu_custom_call" | custom-call | flops 8589934592 | tf_op jit(solution)/shard_map/pallas_call | solution.py:359
  29.2 0.1 collective-permute-start.3
  29.3 0.5 %collective-permute-start.4 = (bf16[256,512]{1,0:T(8,128)(2,1)S(1)}, bf16[256,512]{1,0:T(8,128)(2,1)S(1)}, u32[]{:S(2)}, u32[]{:S(2)}) collective-permute-start(bf16[256,512]{1,0:T(8,128)(2,1)S(1)} %get-tuple-element.36), channel_id=1, source_target_pairs={{0,1},{1,0},{2,3},{3,2},{4,5},{5,4},{6,7},{7,6},{8,9},{9,8},{10,11... | collective-permute-start | bytes 786440 | tf_op jit(solution)/shard_map/ppermute | solution.py:464
  29.8 1.0 %collective-permute-done.3.low_ref = bf16[256,512]{1,0:T(8,128)(2,1)S(1)} collective-permute-done((bf16[256,512]{1,0:T(8,128)(2,1)S(1)}, bf16[256,512]{1,0:T(8,128)(2,1)S(1)}, u32[]{:S(2)}, u32[]{:S(2)}) %collective-permute-start.3) | collective-permute-done | bytes 262176 | tf_op jit(solution)/shard_map/ppermute | solution.py:464
  30.8 0.4 %collective-permute-done.4.high_ref = bf16[256,512]{1,0:T(8,128)(2,1)S(1)} collective-permute-done((bf16[256,512]{1,0:T(8,128)(2,1)S(1)}, bf16[256,512]{1,0:T(8,128)(2,1)S(1)}, u32[]{:S(2)}, u32[]{:S(2)}) %collective-permute-start.4) | collective-permute-done | bytes 262176 | tf_op jit(solution)/shard_map/ppermute | solution.py:464
  31.2 2.3 %shard_map.71 = (bf16[256,256]{1,0:T(8,128)(2,1)S(1)}, f32[256,768]{1,0:T(8,128)S(1)}) custom-call(bf16[256,1024]{1,0:T(8,128)(2,1)S(1)} %get-tuple-element.28.gated_ref, bf16[1024,4096]{1,0:T(8,128)(2,1)} %weight_hbm.5, bf16[256,512]{1,0:T(8,128)(2,1)S(1)} %collective-permute-done.3.low_ref, bf16[256,512]{1,0:T(8,128)(2,1)S(1)} %collective-permute-done.4.high_ref, ...), custom_call_target="tpu_custom_call" | custom-call | tf_op jit(solution)/shard_map/pallas_call | solution.py:359
  33.5 1.2 %collective-permute-done.5.refs_0_ = bf16[256,768]{1,0:T(8,128)(2,1)S(1)} collective-permute-done((bf16[256,768]{1,0:T(8,128)(2,1)S(1)}, bf16[256,768]{1,0:T(8,128)(2,1)S(1)}, u32[]{:S(2)}, u32[]{:S(2)}) %collective-permute-start.5) | collective-permute-done | bytes 393248 | tf_op jit(solution)/shard_map/ppermute | solution.py:448
  34.7 0.8 %shard_map.72 = bf16[256,1024]{1,0:T(8,128)(2,1)} custom-call(bf16[256,256]{1,0:T(8,128)(2,1)S(1)} %get-tuple-element.37.first_ref, f32[256,768]{1,0:T(8,128)S(1)} %get-tuple-element.38.own_ref, bf16[256,768]{1,0:T(8,128)(2,1)S(1)} %collective-permute-done.5.refs_0_), custom_call_target="tpu_custom_call" | custom-call | tf_op jit(solution)/shard_map/pallas_call | solution.py:359
  (3 shorter events, 0.0 us)
Async XLA Ops:
  3.1 14.4 %all-to-all-start = ((bf16[8,16,1024]{2,1,0:T(8,128)(2,1)}), bf16[8,16,1024]{2,1,0:T(8,128)(2,1)S(1)}, u32[]{:S(2)}, u32[]{:S(2)}) async-start(bf16[8,16,1024]{2,1,0:T(8,128)(2,1)} %shard_map.64), calls=%async_computation | async-start | bytes 524288 | tf_op jit(solution)/shard_map/all_to_all | solution.py:391
  17.5 1.8 %copy-start.1 = (bf16[1024,768]{1,0:T(8,128)(2,1)S(1)}, bf16[1024,768]{1,0:T(8,128)(2,1)}, u32[]{:S(2)}) copy-start(bf16[1024,768]{1,0:T(8,128)(2,1)} %get-tuple-element.31.sent_weight) | copy-start | bytes 4718596
  19.2 1.4 %collective-permute-start.1 = (bf16[256,256]{1,0:T(8,128)(2,1)S(1)}, bf16[256,256]{1,0:T(8,128)(2,1)S(1)}, u32[]{:S(2)}, u32[]{:S(2)}) collective-permute-start(bf16[256,256]{1,0:T(8,128)(2,1)S(1)} %get-tuple-element.34), channel_id=1, source_target_pairs={{0,1},{1,0},{2,3},{3,2},{4,5},{5,4},{6,7},{7,6},{8,9},{9,8},{10,11... | collective-permute-start | bytes 393224 | tf_op jit(solution)/shard_map/ppermute | solution.py:438
  20.0 2.2 %collective-permute-start = (bf16[256,768]{1,0:T(8,128)(2,1)S(1)}, bf16[256,768]{1,0:T(8,128)(2,1)S(1)}, u32[]{:S(2)}, u32[]{:S(2)}) collective-permute-start(bf16[256,768]{1,0:T(8,128)(2,1)S(1)} %get-tuple-element.32), channel_id=1, source_target_pairs={{0,1},{1,0},{2,3},{3,2},{4,5},{5,4},{6,7},{7,6},{8,9},{9,8},{10,11... | collective-permute-start | bytes 1179656 | tf_op jit(solution)/shard_map/ppermute | solution.py:444
  20.6 1.6 %copy-start = (bf16[1024,768]{1,0:T(8,128)(2,1)S(1)}, bf16[1024,768]{1,0:T(8,128)(2,1)}, u32[]{:S(2)}) copy-start(bf16[1024,768]{1,0:T(8,128)(2,1)} %get-tuple-element.29.weight_ref) | copy-start | bytes 4718596
  20.6 6.3 %collective-permute-start.2 = (bf16[256,256]{1,0:T(8,128)(2,1)S(1)}, bf16[256,256]{1,0:T(8,128)(2,1)S(1)}, u32[]{:S(2)}, u32[]{:S(2)}) collective-permute-start(bf16[256,256]{1,0:T(8,128)(2,1)S(1)} %shard_map.68.after_ref), channel_id=1, source_target_pairs={{3,1},{2,0},{1,3},{0,2},{7,5},{6,4},{5,7},{4,6},{11,9},{10,8},{9,1... | collective-permute-start | bytes 393224 | tf_op jit(solution)/shard_map/ppermute | solution.py:448
  22.8 11.9 %collective-permute-start.5 = (bf16[256,768]{1,0:T(8,128)(2,1)S(1)}, bf16[256,768]{1,0:T(8,128)(2,1)S(1)}, u32[]{:S(2)}, u32[]{:S(2)}) collective-permute-start(bf16[256,768]{1,0:T(8,128)(2,1)S(1)} %shard_map.69.refs_0_), channel_id=1, source_target_pairs={{3,1},{2,0},{1,3},{0,2},{7,5},{6,4},{5,7},{4,6},{11,9},{10,8},{9,1... | collective-permute-start | bytes 1179656 | tf_op jit(solution)/shard_map/ppermute | solution.py:448
  29.2 1.6 %collective-permute-start.3 = (bf16[256,512]{1,0:T(8,128)(2,1)S(1)}, bf16[256,512]{1,0:T(8,128)(2,1)S(1)}, u32[]{:S(2)}, u32[]{:S(2)}) collective-permute-start(bf16[256,512]{1,0:T(8,128)(2,1)S(1)} %get-tuple-element.35), channel_id=1, source_target_pairs={{0,1},{1,0},{2,3},{3,2},{4,5},{5,4},{6,7},{7,6},{8,9},{9,8},{10,11... | collective-permute-start | bytes 786440 | tf_op jit(solution)/shard_map/ppermute | solution.py:464
  29.3 1.9 %collective-permute-start.4 = (bf16[256,512]{1,0:T(8,128)(2,1)S(1)}, bf16[256,512]{1,0:T(8,128)(2,1)S(1)}, u32[]{:S(2)}, u32[]{:S(2)}) collective-permute-start(bf16[256,512]{1,0:T(8,128)(2,1)S(1)} %get-tuple-element.36), channel_id=1, source_target_pairs={{0,1},{1,0},{2,3},{3,2},{4,5},{5,4},{6,7},{7,6},{8,9},{9,8},{10,11... | collective-permute-start | bytes 786440 | tf_op jit(solution)/shard_map/ppermute | solution.py:464

commit v11 on v10

--- a/solution.py
+++ b/solution.py
@@ -75,7 +75,7 @@
 
 
 def group_order(count):
-    return [(count // 2 + at) % count for at in range(count)]
+    return [(count // 4 + at) % count for at in range(count)]
 
 
 def wait_all(copies):

time: 35.8 us -> 36.7 us (1.025)
  waiting for transfers between devices: 5.94 us -> 6.83 us
    all_to_all x1, waiting for transfers between devices: 0.51 us -> 1.41 us  [body(): lax.all_to_all(wire, 'seq', split_axis=0, concat_axis=0, tiled=True, axis...]
where the time goes in v11:
time: 36.7 us; the launch traced here: 36.4 us
  Pallas kernels  17.5 us (48%)
  starting transfers between devices  12 us (33%)
  waiting for transfers between devices  6.83 us (19%)
    pallas_call x9, Pallas kernels, call(): pl.pallas_call(kernel, out_shape=outs, in_specs=specs, out_specs=[out_spe...  17.5 us
    all_to_all x1, starting transfers between devices, body(): lax.all_to_all(wire, 'seq', split_axis=0, concat_axis=0, tiled=True, axis...  7.83 us
    ppermute x2, waiting for transfers between devices, to_chips(): lax.ppermute(each, 'tp', [(rank, (rank + 2 * hop) % tp) for rank in rever...  3.97 us
    ppermute x2, starting transfers between devices, to_chips(): lax.ppermute(each, 'tp', [(rank, (rank + 2 * hop) % tp) for rank in rever...  2.96 us
    all_to_all x1, waiting for transfers between devices, body(): lax.all_to_all(wire, 'seq', split_axis=0, concat_axis=0, tiled=True, axis...  1.41 us
    ppermute x2, waiting for transfers between devices, body(): halves = [lax.ppermute(each, 'tp', cores) for each in halves]  1.4 us
  transfers between devices with their start and end apart: 7, of which 6 were waited for; matrix products, arithmetic and copies ran while one was open for 0% of the time, Pallas kernels for 33%

profile of v11, /device:TPU:0, one launch (start us, length us, event | category | flops | bytes accessed | tf_op | source)
XLA Modules:
  0.0 36.4 jit_solution(18106309766854719831)
XLA Ops:
  0.0 3.1 %shard_map.64 = bf16[8,16,1024]{2,1,0:T(8,128)(2,1)} custom-call(bf16[256,1024]{1,0:T(8,128)(2,1)} %values_hbm.3, f32[16,1024]{1,0:T(8,128)} %rates_hbm.3), custom_call_target="tpu_custom_call" | custom-call | tf_op jit(solution)/shard_map/pallas_call | solution.py:359
  3.1 7.8 %all-to-all-start = ((bf16[8,16,1024]{2,1,0:T(8,128)(2,1)}), bf16[8,16,1024]{2,1,0:T(8,128)(2,1)S(1)}, u32[]{:S(2)}, u32[]{:S(2)}) async-start(bf16[8,16,1024]{2,1,0:T(8,128)(2,1)} %shard_map.64), calls=%async_computation | async-start | bytes 524288 | tf_op jit(solution)/shard_map/all_to_all | solution.py:391
  10.9 6.0 %shard_map.65 = (f32[256,1024]{1,0:T(8,128)S(1)}, f32[128,1024]{1,0:T(8,128)S(1)}, f32[16,1024]{1,0:T(8,128)S(1)}, f32[16,1024]{1,0:T(8,128)S(1)}, bf16[256,1024...) custom-call(bf16[256,1024]{1,0:T(8,128)(2,1)} %values_hbm.3, ...), custom_call_target="tpu_custom_call" | custom-call | tf_op jit(solution)/shard_map/pallas_call | solution.py:359
  17.0 1.4 %all-to-all-done.states_ref = bf16[8,16,1024]{2,1,0:T(8,128)(2,1)S(1)} async-done(((bf16[8,16,1024]{2,1,0:T(8,128)(2,1)}), bf16[8,16,1024]{2,1,0:T(8,128)(2,1)S(1)}, u32[]{:S(2)}, u32[]{:S(2)}) %all-to-all-start) | async-done | bytes 262176 | tf_op jit(solution)/shard_map/all_to_all | solution.py:391
  18.4 1.7 %shard_map.66 = (bf16[256,1024]{1,0:T(8,128)(2,1)S(1)}, bf16[256,256]{1,0:T(8,128)(2,1)S(1)}) custom-call(bf16[8,16,1024]{2,1,0:T(8,128)(2,1)S(1)} %all-to-all-done.states_ref, f32[256,1024]{1,0:T(8,128)S(1)} %get-tuple-element.22.near_ref, f32[128,1024]{1,0:T(8,128)S(1)} %get-tuple-element.23.reach_ref, f32[16,1024]{1,0:T(8,128)S(1)} %get-tuple-element.24.decay_ref, ...), custom_call_target="tpu_custom_call" | custom-call | flops 8589934592 | tf_op jit(solution)/shard_map/pallas_call | solution.py:359
  20.1 0.1 collective-permute-start.1
  20.2 0.0 copy-done.1
  20.2 0.7 %shard_map.67 = (f32[256,256]{1,0:T(8,128)S(1)}, bf16[256,768]{1,0:T(8,128)(2,1)S(1)}) custom-call(bf16[256,1024]{1,0:T(8,128)(2,1)S(1)} %get-tuple-element.28.gated_ref, bf16[1024,256]{1,0:T(8,128)(2,1)S(1)} %get-tuple-element.30.kept_weight, bf16[1024,768]{1,0:T(8,128)(2,1)S(1)} %copy-done.1), custom_call_target="tpu_custom_call" | custom-call | tf_op jit(solution)/shard_map/pallas_call | solution.py:359
  20.9 0.6 %collective-permute-start = (bf16[256,768]{1,0:T(8,128)(2,1)S(1)}, bf16[256,768]{1,0:T(8,128)(2,1)S(1)}, u32[]{:S(2)}, u32[]{:S(2)}) collective-permute-start(bf16[256,768]{1,0:T(8,128)(2,1)S(1)} %get-tuple-element.32), channel_id=1, source_target_pairs={{0,1},{1,0},{2,3},{3,2},{4,5},{5,4},{6,7},{7,6},{8,9},{9,8},{10,11... | collective-permute-start | bytes 1179656 | tf_op jit(solution)/shard_map/ppermute | solution.py:444
  21.5 0.1 collective-permute-done.1.moved_ref
  21.5 1.6 %collective-permute-start.2 = (bf16[256,256]{1,0:T(8,128)(2,1)S(1)}, bf16[256,256]{1,0:T(8,128)(2,1)S(1)}, u32[]{:S(2)}, u32[]{:S(2)}) collective-permute-start(bf16[256,256]{1,0:T(8,128)(2,1)S(1)} %shard_map.68.after_ref), channel_id=1, source_target_pairs={{3,1},{2,0},{1,3},{0,2},{7,5},{6,4},{5,7},{4,6},{11,9},{10,8},{9,1... | collective-permute-start | bytes 393224 | tf_op jit(solution)/shard_map/ppermute | solution.py:448
  23.1 0.0 collective-permute-done.moved_ref
  23.1 0.0 copy-done
  23.1 0.6 %shard_map.69.refs_0_ = bf16[256,768]{1,0:T(8,128)(2,1)S(1)} custom-call(bf16[256,1024]{1,0:T(8,128)(2,1)S(1)} %get-tuple-element.28.gated_ref, bf16[1024,768]{1,0:T(8,128)(2,1)S(1)} %copy-done, bf16[256,768]{1,0:T(8,128)(2,1)S(1)} %collective-permute-done.moved_ref, bf16[256,256]{1,0:T(8,128)(2,1)S(1)} %shard_map.68.after_ref), custom_call_target="tpu_custom_call" | custom-call | tf_op jit(solution)/shard_map/pallas_call | solution.py:359
  23.7 1.4 %collective-permute-start.5 = (bf16[256,768]{1,0:T(8,128)(2,1)S(1)}, bf16[256,768]{1,0:T(8,128)(2,1)S(1)}, u32[]{:S(2)}, u32[]{:S(2)}) collective-permute-start(bf16[256,768]{1,0:T(8,128)(2,1)S(1)} %shard_map.69.refs_0_), channel_id=1, source_target_pairs={{3,1},{2,0},{1,3},{0,2},{7,5},{6,4},{5,7},{4,6},{11,9},{10,8},{9,1... | collective-permute-start | bytes 1179656 | tf_op jit(solution)/shard_map/ppermute | solution.py:448
  25.1 2.8 %collective-permute-done.2.refs_1_.refs_0_ = bf16[256,256]{1,0:T(8,128)(2,1)S(1)} collective-permute-done((bf16[256,256]{1,0:T(8,128)(2,1)S(1)}, bf16[256,256]{1,0:T(8,128)(2,1)S(1)}, u32[]{:S(2)}, u32[]{:S(2)}) %collective-permute-start.2) | collective-permute-done | bytes 131104 | tf_op jit(solution)/shard_map/ppermute | solution.py:448
  27.9 2.3 %shard_map.70 = (bf16[256,512]{1,0:T(8,128)(2,1)S(1)}, bf16[256,512]{1,0:T(8,128)(2,1)S(1)}) custom-call(bf16[256,1024]{1,0:T(8,128)(2,1)S(1)} %get-tuple-element.28.gated_ref, bf16[1024,4096]{1,0:T(8,128)(2,1)} %weight_hbm.5, bf16[256,768]{1,0:T(8,128)(2,1)S(1)} %shard_map.69.refs_0_, bf16[256,256]{1,0:T(8,128)(2,1)S(1)} %collective-permute-done.2.refs_1_.refs_0_), custom_call_target="tpu_custom_call" | custom-call | flops 8589934592 | tf_op jit(solution)/shard_map/pallas_call | solution.py:359
  30.1 0.1 collective-permute-start.3
  30.2 0.5 %collective-permute-start.4 = (bf16[256,512]{1,0:T(8,128)(2,1)S(1)}, bf16[256,512]{1,0:T(8,128)(2,1)S(1)}, u32[]{:S(2)}, u32[]{:S(2)}) collective-permute-start(bf16[256,512]{1,0:T(8,128)(2,1)S(1)} %get-tuple-element.36), channel_id=1, source_target_pairs={{0,1},{1,0},{2,3},{3,2},{4,5},{5,4},{6,7},{7,6},{8,9},{9,8},{10,11... | collective-permute-start | bytes 786440 | tf_op jit(solution)/shard_map/ppermute | solution.py:464
  30.7 1.0 %collective-permute-done.3.low_ref = bf16[256,512]{1,0:T(8,128)(2,1)S(1)} collective-permute-done((bf16[256,512]{1,0:T(8,128)(2,1)S(1)}, bf16[256,512]{1,0:T(8,128)(2,1)S(1)}, u32[]{:S(2)}, u32[]{:S(2)}) %collective-permute-start.3) | collective-permute-done | bytes 262176 | tf_op jit(solution)/shard_map/ppermute | solution.py:464
  31.7 0.4 %collective-permute-done.4.high_ref = bf16[256,512]{1,0:T(8,128)(2,1)S(1)} collective-permute-done((bf16[256,512]{1,0:T(8,128)(2,1)S(1)}, bf16[256,512]{1,0:T(8,128)(2,1)S(1)}, u32[]{:S(2)}, u32[]{:S(2)}) %collective-permute-start.4) | collective-permute-done | bytes 262176 | tf_op jit(solution)/shard_map/ppermute | solution.py:464
  32.1 2.3 %shard_map.71 = (bf16[256,256]{1,0:T(8,128)(2,1)S(1)}, f32[256,768]{1,0:T(8,128)S(1)}) custom-call(bf16[256,1024]{1,0:T(8,128)(2,1)S(1)} %get-tuple-element.28.gated_ref, bf16[1024,4096]{1,0:T(8,128)(2,1)} %weight_hbm.5, bf16[256,512]{1,0:T(8,128)(2,1)S(1)} %collective-permute-done.3.low_ref, bf16[256,512]{1,0:T(8,128)(2,1)S(1)} %collective-permute-done.4.high_ref, ...), custom_call_target="tpu_custom_call" | custom-call | tf_op jit(solution)/shard_map/pallas_call | solution.py:359
  34.4 1.2 %collective-permute-done.5.refs_0_ = bf16[256,768]{1,0:T(8,128)(2,1)S(1)} collective-permute-done((bf16[256,768]{1,0:T(8,128)(2,1)S(1)}, bf16[256,768]{1,0:T(8,128)(2,1)S(1)}, u32[]{:S(2)}, u32[]{:S(2)}) %collective-permute-start.5) | collective-permute-done | bytes 393248 | tf_op jit(solution)/shard_map/ppermute | solution.py:448
  35.6 0.8 %shard_map.72 = bf16[256,1024]{1,0:T(8,128)(2,1)} custom-call(bf16[256,256]{1,0:T(8,128)(2,1)S(1)} %get-tuple-element.37.first_ref, f32[256,768]{1,0:T(8,128)S(1)} %get-tuple-element.38.own_ref, bf16[256,768]{1,0:T(8,128)(2,1)S(1)} %collective-permute-done.5.refs_0_), custom_call_target="tpu_custom_call" | custom-call | tf_op jit(solution)/shard_map/pallas_call | solution.py:359
  (3 shorter events, 0.0 us)
Async XLA Ops:
  3.1 15.3 %all-to-all-start = ((bf16[8,16,1024]{2,1,0:T(8,128)(2,1)}), bf16[8,16,1024]{2,1,0:T(8,128)(2,1)S(1)}, u32[]{:S(2)}, u32[]{:S(2)}) async-start(bf16[8,16,1024]{2,1,0:T(8,128)(2,1)} %shard_map.64), calls=%async_computation | async-start | bytes 524288 | tf_op jit(solution)/shard_map/all_to_all | solution.py:391
  18.4 1.8 %copy-start.1 = (bf16[1024,768]{1,0:T(8,128)(2,1)S(1)}, bf16[1024,768]{1,0:T(8,128)(2,1)}, u32[]{:S(2)}) copy-start(bf16[1024,768]{1,0:T(8,128)(2,1)} %get-tuple-element.31.sent_weight) | copy-start | bytes 4718596
  20.1 1.4 %collective-permute-start.1 = (bf16[256,256]{1,0:T(8,128)(2,1)S(1)}, bf16[256,256]{1,0:T(8,128)(2,1)S(1)}, u32[]{:S(2)}, u32[]{:S(2)}) collective-permute-start(bf16[256,256]{1,0:T(8,128)(2,1)S(1)} %get-tuple-element.34), channel_id=1, source_target_pairs={{0,1},{1,0},{2,3},{3,2},{4,5},{5,4},{6,7},{7,6},{8,9},{9,8},{10,11... | collective-permute-start | bytes 393224 | tf_op jit(solution)/shard_map/ppermute | solution.py:438
  20.9 2.2 %collective-permute-start = (bf16[256,768]{1,0:T(8,128)(2,1)S(1)}, bf16[256,768]{1,0:T(8,128)(2,1)S(1)}, u32[]{:S(2)}, u32[]{:S(2)}) collective-permute-start(bf16[256,768]{1,0:T(8,128)(2,1)S(1)} %get-tuple-element.32), channel_id=1, source_target_pairs={{0,1},{1,0},{2,3},{3,2},{4,5},{5,4},{6,7},{7,6},{8,9},{9,8},{10,11... | collective-permute-start | bytes 1179656 | tf_op jit(solution)/shard_map/ppermute | solution.py:444
  21.5 1.6 %copy-start = (bf16[1024,768]{1,0:T(8,128)(2,1)S(1)}, bf16[1024,768]{1,0:T(8,128)(2,1)}, u32[]{:S(2)}) copy-start(bf16[1024,768]{1,0:T(8,128)(2,1)} %get-tuple-element.29.weight_ref) | copy-start | bytes 4718596
  21.5 6.3 %collective-permute-start.2 = (bf16[256,256]{1,0:T(8,128)(2,1)S(1)}, bf16[256,256]{1,0:T(8,128)(2,1)S(1)}, u32[]{:S(2)}, u32[]{:S(2)}) collective-permute-start(bf16[256,256]{1,0:T(8,128)(2,1)S(1)} %shard_map.68.after_ref), channel_id=1, source_target_pairs={{3,1},{2,0},{1,3},{0,2},{7,5},{6,4},{5,7},{4,6},{11,9},{10,8},{9,1... | collective-permute-start | bytes 393224 | tf_op jit(solution)/shard_map/ppermute | solution.py:448
  23.7 11.9 %collective-permute-start.5 = (bf16[256,768]{1,0:T(8,128)(2,1)S(1)}, bf16[256,768]{1,0:T(8,128)(2,1)S(1)}, u32[]{:S(2)}, u32[]{:S(2)}) collective-permute-start(bf16[256,768]{1,0:T(8,128)(2,1)S(1)} %shard_map.69.refs_0_), channel_id=1, source_target_pairs={{3,1},{2,0},{1,3},{0,2},{7,5},{6,4},{5,7},{4,6},{11,9},{10,8},{9,1... | collective-permute-start | bytes 1179656 | tf_op jit(solution)/shard_map/ppermute | solution.py:448
  30.1 1.6 %collective-permute-start.3 = (bf16[256,512]{1,0:T(8,128)(2,1)S(1)}, bf16[256,512]{1,0:T(8,128)(2,1)S(1)}, u32[]{:S(2)}, u32[]{:S(2)}) collective-permute-start(bf16[256,512]{1,0:T(8,128)(2,1)S(1)} %get-tuple-element.35), channel_id=1, source_target_pairs={{0,1},{1,0},{2,3},{3,2},{4,5},{5,4},{6,7},{7,6},{8,9},{9,8},{10,11... | collective-permute-start | bytes 786440 | tf_op jit(solution)/shard_map/ppermute | solution.py:464
  30.2 1.9 %collective-permute-start.4 = (bf16[256,512]{1,0:T(8,128)(2,1)S(1)}, bf16[256,512]{1,0:T(8,128)(2,1)S(1)}, u32[]{:S(2)}, u32[]{:S(2)}) collective-permute-start(bf16[256,512]{1,0:T(8,128)(2,1)S(1)} %get-tuple-element.36), channel_id=1, source_target_pairs={{0,1},{1,0},{2,3},{3,2},{4,5},{5,4},{6,7},{7,6},{8,9},{9,8},{10,11... | collective-permute-start | bytes 786440 | tf_op jit(solution)/shard_map/ppermute | solution.py:464
